TPU v7x, 32 devices: a whole 2x2x4 slice. The times are simulated.
32 devices in a mesh: dp: 8 (over y, x, core), mp: 4 (over z).
Axes of the slice: x: 2, y: 2, z: 4, core: 2. Of those that a mesh axis runs over, the one named last changes fastest.
Arguments:
- tokens: bfloat16 [16384, 2048], P(('dp', 'mp')), may hold values from -6 to 6
- cotangent: bfloat16 [16384, 2048], P(('dp', 'mp'))
- lengths: int32 [8, 2], P('dp'), may hold values from 1 to 2047, as said below
- w_qkv: float32 [2048, 6144], P('dp', 'mp')
- w_out: float32 [2048, 2048], P('mp', 'dp')
- w_up: float32 [2048, 8192], P('dp', 'mp'), may hold values from -0.125 to 0.125
- w_down: float32 [8192, 2048], P('mp', 'dp')
- norm_vec: float32 [6, 2048], replicated
- b_qkv: float32 [6144], P('mp'), may hold values from -1.2 to 1.2
- b_up: float32 [8192], P('mp'), may hold values from -3 to 3
- m_qkv: float32 [2048, 6144], P('dp', 'mp')
- m_out: float32 [2048, 2048], P('mp', 'dp')
- m_up: float32 [2048, 8192], P('dp', 'mp')
- m_down: float32 [8192, 2048], P('mp', 'dp')
- m_norm: float32 [6, 2048], replicated
- m_bqkv: float32 [6144], P('mp')
- m_bup: float32 [8192], P('mp')
- v_qkv: float32 [2048, 6144], P('dp', 'mp'), as said below
- v_out: float32 [2048, 2048], P('mp', 'dp'), as said below
- v_up: float32 [2048, 8192], P('dp', 'mp'), as said below
- v_down: float32 [8192, 2048], P('mp', 'dp'), as said below
- v_norm: float32 [6, 2048], replicated, as said below
- v_bqkv: float32 [6144], P('mp'), as said below
- v_bup: float32 [8192], P('mp'), as said below
Outputs:
- layer_out: bfloat16 [16384, 2048], P(('dp', 'mp'))
- grad_in: bfloat16 [16384, 2048], P(('dp', 'mp'))
- grad_norm: float32 [], replicated
- upd_qkv: float32 [2048, 6144], P('dp', 'mp')
- upd_out: float32 [2048, 2048], P('mp', 'dp')
- upd_up: float32 [2048, 8192], P('dp', 'mp')
- upd_down: float32 [8192, 2048], P('mp', 'dp')
- upd_norm: float32 [6, 2048], replicated
- upd_bqkv: float32 [6144], P('mp')
- upd_bup: float32 [8192], P('mp')
- mom_qkv: float32 [2048, 6144], P('dp', 'mp')
- mom_out: float32 [2048, 2048], P('mp', 'dp')
- mom_up: float32 [2048, 8192], P('dp', 'mp')
- mom_down: float32 [8192, 2048], P('mp', 'dp')
- mom_norm: float32 [6, 2048], replicated
- mom_bqkv: float32 [6144], P('mp')
- mom_bup: float32 [8192], P('mp')
- sec_qkv: float32 [2048, 6144], P('dp', 'mp')
- sec_out: float32 [2048, 2048], P('mp', 'dp')
- sec_up: float32 [2048, 8192], P('dp', 'mp')
- sec_down: float32 [8192, 2048], P('mp', 'dp')
- sec_norm: float32 [6, 2048], replicated
- sec_bqkv: float32 [6144], P('mp')
- sec_bup: float32 [8192], P('mp')
Inputs may be any that keep to these rules, and one draw needn't show every extreme that they name: lengths[g, 0] is at least 1537, lengths[g, 1] is at least 1, and their sum is at most 2048. `v_qkv`: every entry is positive. `v_out`: every entry is positive. `v_up`: every entry is positive. `v_down`: every entry is positive. `v_norm`: every entry is positive. `v_bqkv`: every entry is positive. `v_bup`: every entry is positive.
All inputs are finite; a program needn't handle non-finite values.
Results may differ from a plain program's by a relative error of at most 0.015.
The roundings to bfloat16 on the way count: a program that leaves them out, or rounds other values in their place, can miss the bound.
Values may be sent and summed in bfloat16 or wider, within the bound.
No kernel may reach another device: no remote copies, remote signals or barrier semaphores. Data moves between devices by JAX's collectives and lax.ppermute only.
A program may use at most 320 MiB of HBM per device.

v0:
```python
import jax
import jax.numpy as jnp
from jax import lax
from jax.sharding import PartitionSpec as P

D = 2048
HD = 128
ROT = 32
GROUP_TOK = 2048
STEP = 10


LN_EPS = 1e-05
ROPE_BASE = 10000.0
CLIP_NORM = 1.0
BETA_ONE = 0.9
BETA_TWO = 0.95
ADAM_EPS = 1e-08
DECAY = 0.01
RATE_SMALL = 1.0


def layer_norm(values, gain, shift):
    centre = values - jnp.mean(values, axis=-1, keepdims=True)
    spread = jnp.mean(centre * centre, axis=-1, keepdims=True)
    return centre * lax.rsqrt(spread + LN_EPS) * gain + shift


def row_layout(lengths_row, count):
    first_len = lengths_row[0]
    used = lengths_row[0] + lengths_row[1]
    row_ids = jnp.arange(count, dtype=jnp.int32)
    segment = (row_ids >= first_len).astype(jnp.int32) + (row_ids >= used).astype(jnp.int32)
    begin = jnp.where(segment == 0, 0, jnp.where(segment == 1, first_len, used))
    position = (row_ids - begin).astype(jnp.float32)
    return (segment, position, row_ids < used)


def rotary(values, position):
    half = ROT // 2
    inverse = ROPE_BASE ** (-jnp.arange(half, dtype=jnp.float32) * 2.0 / ROT)
    angle = position[:, None] * inverse[None, :]
    angle = jnp.concatenate([angle, angle], axis=-1)
    cosine = jnp.cos(angle)[:, None, :]
    sine = jnp.sin(angle)[:, None, :]
    turned = values[..., :ROT]
    rolled = jnp.concatenate([-turned[..., half:], turned[..., :half]], axis=-1)
    return jnp.concatenate([turned * cosine + rolled * sine, values[..., ROT:]], axis=-1)


def gelu_exact(values):
    return jax.nn.gelu(values, approximate=False)


def adam_step(weight, grad, first, second, rate, decay):
    first_new = BETA_ONE * first + (1.0 - BETA_ONE) * grad
    second_new = BETA_TWO * second + (1.0 - BETA_TWO) * grad * grad
    first_hat = first_new / (1.0 - BETA_ONE**STEP)
    second_hat = second_new / (1.0 - BETA_TWO**STEP)
    weight_new = weight - rate * (first_hat / (jnp.sqrt(second_hat) + ADAM_EPS) + decay * weight)
    return (weight_new, first_new, second_new)


def local(
    tokens,
    cotangent,
    lengths,
    w_qkv,
    w_out,
    w_up,
    w_down,
    norm_vec,
    b_qkv,
    b_up,
    m_qkv,
    m_out,
    m_up,
    m_down,
    m_norm,
    m_bqkv,
    m_bup,
    v_qkv,
    v_out,
    v_up,
    v_down,
    v_norm,
    v_bqkv,
    v_bup,
):
    own_rows = tokens.shape[0]
    dim_model = tokens.shape[1]
    group_rows = own_rows * lax.axis_size("mp")
    mp_place = lax.axis_index("mp")
    dp_place = lax.axis_index("dp")
    segment, position, live = row_layout(lengths[0], group_rows)
    row_ids = jnp.arange(group_rows, dtype=jnp.int32)
    live_own = lax.dynamic_slice_in_dim(live, mp_place * own_rows, own_rows, 0)
    full_qkv, full_up, full_out, full_down = (
        lax.all_gather(w_qkv.astype(jnp.bfloat16), "dp", axis=0, tiled=True),
        lax.all_gather(w_up.astype(jnp.bfloat16), "dp", axis=0, tiled=True),
        lax.all_gather(w_out.astype(jnp.bfloat16), "dp", axis=1, tiled=True),
        lax.all_gather(w_down.astype(jnp.bfloat16), "dp", axis=1, tiled=True),
    )
    token_vals = tokens.astype(jnp.float32)
    first_norm = layer_norm(token_vals, norm_vec[0], norm_vec[1]).astype(jnp.bfloat16)
    second_norm = layer_norm(token_vals, norm_vec[2], norm_vec[3]).astype(jnp.bfloat16)
    first_rows, second_rows = (
        lax.all_gather(first_norm, "mp", axis=0, tiled=True),
        lax.all_gather(second_norm, "mp", axis=0, tiled=True),
    )
    head_count = full_qkv.shape[1] // (3 * HD)
    mixed = jnp.dot(first_rows, full_qkv, preferred_element_type=jnp.float32) + b_qkv
    mixed = mixed.reshape(group_rows, head_count, 3, HD)
    query_b = rotary(mixed[:, :, 0], position).astype(jnp.bfloat16)
    key_b = rotary(mixed[:, :, 1], position).astype(jnp.bfloat16)
    value_b = mixed[:, :, 2].astype(jnp.bfloat16)
    width = min(512, group_rows)
    blocks = group_rows // width
    scale = HD ** (-0.5)

    def masked_scores(query_block, rows_block, seg_block):
        raw = (
            jnp.einsum("qhd,khd->hqk", query_block, key_b, preferred_element_type=jnp.float32)
            * scale
        )
        allowed = (seg_block[:, None] == segment[None, :]) & (
            row_ids[None, :] <= rows_block[:, None]
        )
        return jnp.where(allowed[None], raw, -jnp.inf)

    def forward_block(packed):
        query_block, rows_block, seg_block = packed
        scores = masked_scores(query_block, rows_block, seg_block)
        top = jnp.max(scores, axis=-1, keepdims=True)
        expo = jnp.exp(scores - top)
        total = jnp.sum(expo, axis=-1, keepdims=True)
        weights_b = (expo / total).astype(jnp.bfloat16)
        context = jnp.einsum("hqk,khd->qhd", weights_b, value_b, preferred_element_type=jnp.float32)
        return (context, (top + jnp.log(total))[..., 0])

    query_blocks = query_b.reshape(blocks, width, head_count, HD)
    row_blocks = row_ids.reshape(blocks, width)
    seg_blocks = segment.reshape(blocks, width)
    context, log_total = lax.map(forward_block, (query_blocks, row_blocks, seg_blocks))
    attended = context.reshape(group_rows, head_count * HD).astype(jnp.bfloat16)
    hidden = jnp.dot(second_rows, full_up, preferred_element_type=jnp.float32) + b_up
    active = gelu_exact(hidden).astype(jnp.bfloat16)
    attn_part = jnp.dot(attended, full_out, preferred_element_type=jnp.float32)
    ffn_part = jnp.dot(active, full_down, preferred_element_type=jnp.float32)
    branch = lax.psum_scatter(
        (attn_part + ffn_part).astype(jnp.bfloat16), "mp", scatter_dimension=0, tiled=True
    ).astype(jnp.float32)
    layer_out = (token_vals + branch + norm_vec[4] + norm_vec[5]).astype(jnp.bfloat16)
    back_own = cotangent * live_own[:, None].astype(jnp.bfloat16)
    back_rows = lax.all_gather(back_own, "mp", axis=0, tiled=True)
    grad_context = jnp.dot(back_rows, full_out.T, preferred_element_type=jnp.float32).astype(
        jnp.bfloat16
    )
    grad_out = jnp.einsum("rc,rd->cd", attended, back_rows, preferred_element_type=jnp.float32)
    grad_down = jnp.einsum("rf,rd->fd", active, back_rows, preferred_element_type=jnp.float32)
    grad_active = jnp.dot(back_rows, full_down.T, preferred_element_type=jnp.float32)
    gelu_back = jax.vjp(gelu_exact, hidden)[1]
    grad_hidden = gelu_back(grad_active)[0].astype(jnp.bfloat16)
    context_grads = grad_context.reshape(blocks, width, head_count, HD)

    def back_block(carry, packed):
        key_grad, value_grad = carry
        query_block, rows_block, seg_block, dctx_block, lse_block = packed
        scores = masked_scores(query_block, rows_block, seg_block)
        weights_f = jnp.exp(scores - lse_block[:, :, None])
        dweights = jnp.einsum(
            "qhd,khd->hqk", dctx_block, value_b, preferred_element_type=jnp.float32
        )
        inner = jnp.sum(weights_f * dweights, axis=-1, keepdims=True)
        dscores = (weights_f * (dweights - inner)).astype(jnp.bfloat16)
        query_grad = (
            jnp.einsum("hqk,khd->qhd", dscores, key_b, preferred_element_type=jnp.float32) * scale
        )
        key_grad = (
            key_grad
            + jnp.einsum("hqk,qhd->khd", dscores, query_block, preferred_element_type=jnp.float32)
            * scale
        )
        value_grad = value_grad + jnp.einsum(
            "hqk,qhd->khd",
            weights_f.astype(jnp.bfloat16),
            dctx_block,
            preferred_element_type=jnp.float32,
        )
        return ((key_grad, value_grad), query_grad)

    zero_rows = jnp.zeros((group_rows, head_count, HD), jnp.float32)
    (key_grad, value_grad), query_grad = lax.scan(
        back_block,
        (zero_rows, zero_rows),
        (query_blocks, row_blocks, seg_blocks, context_grads, log_total),
    )
    query_grad = query_grad.reshape(group_rows, head_count, HD)
    rotate_back = jax.vjp(lambda values: rotary(values, position), query_grad)[1]
    query_pre = rotate_back(query_grad)[0]
    key_pre = rotate_back(key_grad)[0]
    mixed_grad = jnp.stack([query_pre, key_pre, value_grad], axis=2)
    mixed_grad = mixed_grad.reshape(group_rows, head_count * 3 * HD).astype(jnp.bfloat16)
    grad_qkv = jnp.einsum("rd,rc->dc", first_rows, mixed_grad, preferred_element_type=jnp.float32)
    grad_up = jnp.einsum("rd,rf->df", second_rows, grad_hidden, preferred_element_type=jnp.float32)
    grad_bqkv = jnp.sum(mixed_grad, axis=0, dtype=jnp.float32)
    grad_bup = jnp.sum(grad_hidden, axis=0, dtype=jnp.float32)
    back_vals = back_own.astype(jnp.float32)
    out_bias = jnp.sum(back_vals, axis=0)
    left = jnp.dot(mixed_grad, full_qkv.T, preferred_element_type=jnp.float32)
    right = jnp.dot(grad_hidden, full_up.T, preferred_element_type=jnp.float32)
    both_inputs = lax.psum_scatter(
        jnp.concatenate([left, right], axis=1).astype(jnp.bfloat16),
        "mp",
        scatter_dimension=0,
        tiled=True,
    ).astype(jnp.float32)
    first_back = jax.vjp(layer_norm, token_vals, norm_vec[0], norm_vec[1])[1]
    second_back = jax.vjp(layer_norm, token_vals, norm_vec[2], norm_vec[3])[1]
    input_one, gain_one, shift_one = first_back(both_inputs[:, :dim_model])
    input_two, gain_two, shift_two = second_back(both_inputs[:, dim_model:])
    grad_in = (back_vals + input_one + input_two).astype(jnp.bfloat16)
    small_part = jnp.stack([gain_one, shift_one, gain_two, shift_two, out_bias, out_bias])
    grad_small = lax.psum(small_part, ("dp", "mp"))
    sum_qkv, sum_out, sum_up, sum_down, sum_bqkv, sum_bup = (
        lax.psum(grad_qkv.astype(jnp.bfloat16), "dp").astype(jnp.float32),
        lax.psum(grad_out.astype(jnp.bfloat16), "dp").astype(jnp.float32),
        lax.psum(grad_up.astype(jnp.bfloat16), "dp").astype(jnp.float32),
        lax.psum(grad_down.astype(jnp.bfloat16), "dp").astype(jnp.float32),
        lax.psum(grad_bqkv.astype(jnp.bfloat16), "dp").astype(jnp.float32),
        lax.psum(grad_bup.astype(jnp.bfloat16), "dp").astype(jnp.float32),
    )
    part_qkv = lax.dynamic_slice_in_dim(sum_qkv, dp_place * w_qkv.shape[0], w_qkv.shape[0], 0)
    part_out = lax.dynamic_slice_in_dim(sum_out, dp_place * w_out.shape[1], w_out.shape[1], 1)
    part_up = lax.dynamic_slice_in_dim(sum_up, dp_place * w_up.shape[0], w_up.shape[0], 0)
    part_down = lax.dynamic_slice_in_dim(sum_down, dp_place * w_down.shape[1], w_down.shape[1], 1)
    local_squares = (
        jnp.sum(part_qkv * part_qkv)
        + jnp.sum(part_out * part_out)
        + jnp.sum(part_up * part_up)
        + jnp.sum(part_down * part_down)
        + (jnp.sum(sum_bqkv * sum_bqkv) + jnp.sum(sum_bup * sum_bup)) / lax.axis_size("dp")
    )
    total_squares = lax.psum(local_squares, ("dp", "mp")) + jnp.sum(grad_small * grad_small)
    grad_norm = jnp.sqrt(total_squares)
    factor = jnp.minimum(1.0, CLIP_NORM / (grad_norm + 1e-06))
    rate_big = 2.5 * D ** (-0.5)
    rate_out = 2.5 * max(16 * D // GROUP_TOK, 1) ** (-0.5)
    upd_qkv, mom_qkv, sec_qkv = adam_step(w_qkv, factor * part_qkv, m_qkv, v_qkv, rate_big, DECAY)
    upd_out, mom_out, sec_out = adam_step(w_out, factor * part_out, m_out, v_out, rate_out, DECAY)
    upd_up, mom_up, sec_up = adam_step(w_up, factor * part_up, m_up, v_up, rate_big, DECAY)
    upd_down, mom_down, sec_down = adam_step(
        w_down, factor * part_down, m_down, v_down, rate_big, DECAY
    )
    upd_norm, mom_norm, sec_norm = adam_step(
        norm_vec, factor * grad_small, m_norm, v_norm, RATE_SMALL, 0.0
    )
    upd_bqkv, mom_bqkv, sec_bqkv = adam_step(
        b_qkv, factor * sum_bqkv, m_bqkv, v_bqkv, RATE_SMALL, 0.0
    )
    upd_bup, mom_bup, sec_bup = adam_step(b_up, factor * sum_bup, m_bup, v_bup, RATE_SMALL, 0.0)
    return (
        layer_out,
        grad_in,
        grad_norm,
        upd_qkv,
        upd_out,
        upd_up,
        upd_down,
        upd_norm,
        upd_bqkv,
        upd_bup,
        mom_qkv,
        mom_out,
        mom_up,
        mom_down,
        mom_norm,
        mom_bqkv,
        mom_bup,
        sec_qkv,
        sec_out,
        sec_up,
        sec_down,
        sec_norm,
        sec_bqkv,
        sec_bup,
    )


def solution(mesh):
    return jax.shard_map(
        local,
        mesh=mesh,
        in_specs=(
            P(("dp", "mp"), None),
            P(("dp", "mp"), None),
            P("dp", None),
            P("dp", "mp"),
            P("mp", "dp"),
            P("dp", "mp"),
            P("mp", "dp"),
            P(),
            P("mp"),
            P("mp"),
            P("dp", "mp"),
            P("mp", "dp"),
            P("dp", "mp"),
            P("mp", "dp"),
            P(),
            P("mp"),
            P("mp"),
            P("dp", "mp"),
            P("mp", "dp"),
            P("dp", "mp"),
            P("mp", "dp"),
            P(),
            P("mp"),
            P("mp"),
        ),
        out_specs=(
            P(("dp", "mp"), None),
            P(("dp", "mp"), None),
            P(),
            P("dp", "mp"),
            P("mp", "dp"),
            P("dp", "mp"),
            P("mp", "dp"),
            P(),
            P("mp"),
            P("mp"),
            P("dp", "mp"),
            P("mp", "dp"),
            P("dp", "mp"),
            P("mp", "dp"),
            P(),
            P("mp"),
            P("mp"),
            P("dp", "mp"),
            P("mp", "dp"),
            P("dp", "mp"),
            P("mp", "dp"),
            P(),
            P("mp"),
            P("mp"),
        ),
        check_vma=False,
    )
```

profile of v0, /device:TPU:0, one launch (start us, length us, event | category | flops | bytes accessed | tf_op | source)
XLA Modules:
  0.0 1650.8 jit_solution(16023649016257041067)
XLA Ops:
  30.1 28.7 %all-gather.10.cloned.1.call-done = bf16[2048,1536]{1,0:T(8,128)(2,1)} async-done(((bf16[256,1536]{1,0:T(8,128)(2,1)}), bf16[2048,1536]{1,0:T(8,128)(2,1)}) %all-gather.10.cloned.1.call-update) | async-done | bytes 6291472 | tf_op jit(solution)/shard_map/all_gather | solution.py:99
  58.8 151.8 %all-gather.8.cloned.1.call-done = bf16[2048,2048]{1,0:T(8,128)(2,1)} async-done(((bf16[512,2048]{1,0:T(8,128)(2,1)}), bf16[2048,2048]{1,0:T(8,128)(2,1)}) %all-gather.8.cloned.1.call-update) | async-done | bytes 8388624 | tf_op jit(solution)/shard_map/all_gather | solution.py:108
  210.6 18.0 %convolution_add_fusion = f32[2048,1536]{0,1:T(8,128)S(1)} fusion(bf16[2048,2048]{1,0:T(8,128)(2,1)} %all-gather.8.cloned.1.call-done, bf16[2048,1536]{1,0:T(8,128)(2,1)} %all-gather.10.cloned.1.call-done, f32[1536]{0:T(1024)S(1)} %copy-done.58), kind=kOutput, calls=%fused_computation.77 | convolution fusion | flops 12888047616 | bytes 27269120 | tf_op jit(solution)/shard_map/dot_general | solution.py:112
  236.2 5.4 copy.154
  241.6 5.4 copy.155
  247.0 4.8 slice.139
  251.9 7.2 slice_negate_fusion.2
  265.0 5.6 fusion.70
  281.9 66.6 %while.28 = (s32[]{:T(128)}, bf16[4,512,4,128]{3,1,2,0:T(8,128)(2,1)}, f32[4,4,512]{2,1,0:T(4,128)S(1)}, s32[4,512]{1,0:T(4,128)S(1)}, s32[4,512]{1,0:T(4,128)S(...) while((s32[]{:T(128)}, ...), condition=%wide.region_5.6_spmd.clone, body=%wide.region_2.0_spmd.clone.sunk | while | flops 2200969216 | bytes 68777104 | solution.py:144
  292.4 6.2 fusion.184
  309.0 6.2 fusion.184
  325.7 6.2 fusion.184
  342.3 6.2 fusion.184
  348.5 42.6 %all-gather.20.cloned.1.call-done = bf16[2048,2048]{1,0:T(8,128)(2,1)} async-done(((bf16[512,2048]{1,0:T(8,128)(2,1)}), bf16[2048,2048]{1,0:T(8,128)(2,1)}) %all-gather.20.cloned.1.call-update) | async-done | bytes 8388624 | tf_op jit(solution)/shard_map/all_gather | solution.py:155
  391.2 9.9 convolution_convert_fusion.6
  405.1 258.7 %while.29 = (s32[]{:T(128)}, f32[2048,4,128]{0,2,1:T(8,128)}, f32[2048,4,128]{0,2,1:T(8,128)}, f32[4,512,4,128]{3,1,0,2:T(8,128)}, bf16[4,512,4,128]{3,1,2,0:T(8...) while((s32[]{:T(128)}, f32[2048,4,128]{0,2,1:T(8,128)}, ...), condition=%wide.region_9.10_spmd.clone, body=%wide.region_7.9_spmd.clone.sunk | while | flops 5440282624 | bytes 203511600 | solution.py:193
  407.1 9.4 fusion.193
  417.8 12.6 multiply_reduce_fusion.3
  430.4 15.3 multiply_convert_fusion.3
  445.8 7.5 bitcast_add_fusion.4
  456.6 11.0 bitcast_add_fusion.5
  469.5 9.4 fusion.193
  480.2 12.5 multiply_reduce_fusion.3
  492.7 15.0 multiply_convert_fusion.3
  507.7 8.7 bitcast_add_fusion.4
  519.8 12.2 bitcast_add_fusion.5
  533.9 9.4 fusion.193
  544.5 12.9 multiply_reduce_fusion.3
  557.4 14.9 multiply_convert_fusion.3
  572.3 8.7 bitcast_add_fusion.4
  584.5 12.2 bitcast_add_fusion.5
  598.6 10.1 fusion.193
  609.9 12.5 multiply_reduce_fusion.3
  622.4 16.0 multiply_convert_fusion.3
  638.4 8.9 bitcast_add_fusion.4
  650.7 12.7 bitcast_add_fusion.5
  663.8 5.4 copy.113
  669.2 5.5 split.32
  677.9 4.7 copy.115
  686.7 4.6 fusion.128
  691.3 5.3 fusion.129
  697.4 7.5 pad_add_fusion.1
  708.6 4.4 fusion.126
  713.1 8.8 copy.116
  725.3 10.0 convolution_convert_fusion.5
  735.3 15.8 convolution_convert_fusion.4
  751.1 24.2 %fusion.132 = f32[2048,2048]{1,0:T(8,128)} fusion(bf16[2048,2048]{1,0:T(8,128)(2,1)} %all-gather.14.cloned.1.call-done, bf16[2048,2048]{1,0:T(8,128)(2,1)} %all-gather.16.cloned.1.call-done), kind=kOutput, calls=%fused_computation.232 | convolution fusion | flops 17179869184 | bytes 33554432 | tf_op jit(solution)/shard_map/dot_general | solution.py:146
  775.3 63.8 %fusion.124 = (bf16[2048]{0:T(1024)(128)(2,1)}, bf16[2048,2048]{1,0:T(8,128)(2,1)}, f32[2048,2048]{1,0:T(8,128)}) fusion(f32[2048,2048]{1,0:T(8,128)} %fusion.132, f32[2048]{0:T(1024)S(1)} %copy-done.51, bf16[2048,2048]{1,0:T(8,128)(2,1)} %all-gather.20.cloned.1.call-done, bf16[2048,2048]{1,0:T(8,128)(2,1)} %all-gather.18.cloned.1.call-done), kind=kOutput, calls=%fused_computation.225 | convolution fusion | flops 17490245632 | bytes 58732544 | tf_op jit(solution)/shard_map/dot_general | solution.py:161
  839.1 8.6 multiply_convert_fusion.1
  847.7 25.7 %convolution_convert_fusion = bf16[2048,2048]{1,0:T(8,128)(2,1)} fusion(bf16[2048,2048]{1,0:T(8,128)(2,1)S(1)} %multiply_convert_fusion.1, bf16[2048,2048]{1,0:T(8,128)(2,1)} %all-gather.20.cloned.1.call-done), kind=kOutput, calls=%fused_computation.78 | convolution fusion | flops 17184063488 | bytes 25165824 | tf_op jit(solution)/shard_map/rf,rd->fd/dot_general | solution.py:160
  873.5 20.7 %convolution_convert_fusion.1 = bf16[2048,2048]{1,0:T(8,128)(2,1)} fusion(bf16[2048,2048]{1,0:T(8,128)(2,1)S(1)} %bitcast.196, bf16[2048,2048]{1,0:T(8,128)(2,1)S(1)} %copy-done.63), kind=kOutput, calls=%fused_computation.79 | convolution fusion | flops 17184063488 | bytes 25165824 | tf_op jit(solution)/shard_map/rd,rf->df/dot_general | solution.py:205
  894.2 17.5 %convolution_convert_fusion.3 = bf16[2048,2048]{1,0:T(8,128)(2,1)S(1)} fusion(bf16[2048,1536]{0,1:T(8,128)(2,1)} %bitcast.165, bf16[2048,1536]{1,0:T(8,128)(2,1)} %all-gather.10.cloned.1.call-done), kind=kOutput, calls=%fused_computation.81 | convolution fusion | flops 12889096192 | bytes 20971520 | tf_op jit(solution)/shard_map/dot_general | solution.py:210
  911.7 22.5 %convolution_convert_fusion.2 = bf16[2048,2048]{1,0:T(8,128)(2,1)S(1)} fusion(bf16[2048,2048]{1,0:T(8,128)(2,1)} %get-tuple-element.374, bf16[2048,2048]{1,0:T(8,128)(2,1)} %all-gather.16.cloned.1.call-done), kind=kOutput, calls=%fused_computation.80 | convolution fusion | flops 17184063488 | bytes 25165824 | tf_op jit(solution)/shard_map/dot_general | solution.py:211
  934.2 6.8 pad_maximum_fusion
  942.6 10.9 fusion.82
  953.5 25.9 %add_convert_fusion.1 = bf16[2048,2048]{1,0:T(8,128)(2,1)} fusion(f32[2048,2048]{1,0:T(8,128)} %fusion.82, bf16[2048,2048]{1,0:T(8,128)(2,1)} %copy-done.24, bf16[2048,2048]{1,0:T(8,128)(2,1)} %all-gather.18.cloned.1.call-done), kind=kOutput, calls=%fused_computation.61 | convolution fusion | flops 17188257792 | bytes 41943040 | tf_op jit(solution)/shard_map/dot_general | solution.py:149
  980.2 14.5 all-reduce.9
  997.2 206.2 %all-reduce.13.cloned.1.call-done = (bf16[2048,1536]{1,0:T(8,128)(2,1)}, bf16[512,2048]{1,0:T(8,128)(2,1)}, bf16[2048,2048]{1,0:T(8,128)(2,1)}, bf16[2048,2048]{1,0:T(8,128)(2,1)}) async-done(((bf16[2048,1536]{1,0:T(8,128)(2,1)}, bf16[512,2048]{1,0:T(8,128)(2,1)}, bf16[2048,2048]{1,0:T(8,128)(2,1)}, bf16[2048,2048]{1,0:T(8,128)(2,1)}), (bf16[2048,1536]{1,0:T(8,128)(2,1)}, bf16[512,2048]{1,0:T(8,128)(2,1)}, ...) | async-done | bytes 25165840 | tf_op jit(solution)/shard_map/psum | solution.py:226
  1215.0 271.4 %reduce-scatter.5.cloned.1.call-done = bf16[512,4096]{1,0:T(8,128)(2,1)} async-done(((bf16[2048,4096]{1,0:T(8,128)(2,1)}), bf16[512,4096]{1,0:T(8,128)(2,1)}) %reduce-scatter.5.cloned.1.call-update) | async-done | bytes 4194320 | tf_op jit(solution)/shard_map/reduce_scatter | solution.py:212
  1497.3 45.3 %all-reduce.8 = (f32[]{:T(128)}, f32[6,2048]{1,0:T(8,128)S(1)}) all-reduce(f32[]{:T(128)S(6)} %add.335, f32[6,2048]{1,0:T(8,128)S(1)} %stack.28), channel_id=1, replica_groups=mesh['dp'=8,'mp'=4] {'dp','mp'}, use_global_device_ids=true, to_apply=%region_29.30 | all-reduce | flops 12289 | bytes 98312 | tf_op jit(solution)/shard_map/psum | solution.py:244
  1551.4 6.5 multiply_subtract_fusion
  1558.0 5.3 multiply_subtract_fusion.1
  1567.5 67.3 %reduce-scatter.3.cloned.1.call-done = bf16[512,2048]{1,0:T(8,128)(2,1)} async-done(((bf16[2048,2048]{1,0:T(8,128)(2,1)}), bf16[512,2048]{1,0:T(8,128)(2,1)}) %reduce-scatter.3.cloned.1.call-update) | async-done | bytes 2097168 | tf_op jit(solution)/shard_map/reduce_scatter | solution.py:150
  1634.8 7.7 fusion.56
  (304 shorter events, 168.0 us)
Async XLA Ops:
  7.2 51.5 %all-gather.10.cloned.1.call-start = ((), (), s32[]{:S(2)}) async-start(), calls=%async_computation.3 | async-start | bytes 7077888 | tf_op jit(solution)/shard_map/all_gather | solution.py:99
  9.8 200.8 %all-gather.8.cloned.1.call-start = ((), (), s32[]{:S(2)}) async-start(), calls=%async_computation.2 | async-start | bytes 10485760 | tf_op jit(solution)/shard_map/all_gather | solution.py:108
  10.2 5.4 copy-start.43
  15.7 332.9 %all-gather.12.cloned.1.call-start = ((), (), s32[]{:S(2)}) async-start(), calls=%async_computation.4 | async-start | bytes 2359296 | tf_op jit(solution)/shard_map/all_gather | solution.py:101
  16.5 374.7 %all-gather.20.cloned.1.call-start = ((), (), s32[]{:S(2)}) async-start(), calls=%async_computation.9 | async-start | bytes 10485760 | tf_op jit(solution)/shard_map/all_gather | solution.py:155
  20.9 730.2 %all-gather.14.cloned.1.call-start = ((), (), s32[]{:S(2)}) async-start(), calls=%async_computation.5 | async-start | bytes 10485760 | tf_op jit(solution)/shard_map/all_gather | solution.py:109
  21.5 729.6 %all-gather.16.cloned.1.call-start = ((), (), s32[]{:S(2)}) async-start(), calls=%async_computation.6 | async-start | bytes 9437184 | tf_op jit(solution)/shard_map/all_gather | solution.py:100
  24.5 186.1 %copy-start.58 = (f32[1536]{0:T(1024)S(1)}, f32[1536]{0:T(1024)}, u32[]{:S(2)}) copy-start(f32[1536]{0:T(1024)} %param.36) | copy-start | bytes 18436
  24.5 750.8 %all-gather.18.cloned.1.call-start = ((), (), s32[]{:S(2)}) async-start(), calls=%async_computation.7 | async-start | bytes 9437184 | tf_op jit(solution)/shard_map/all_gather | solution.py:102
  25.7 1177.7 %all-reduce.13.cloned.1.call-start = ((), (), s32[]{:S(2)}) async-start(), calls=%async_computation.11 | async-start | bytes 50331648 | tf_op jit(solution)/shard_map/psum | solution.py:226
  28.7 236.3 %copy-start.16 = (f32[2048,32]{1,0:T(8,128)}, f32[2048,32]{1,0:T(8,128)S(1)}, u32[]{:S(2)}) copy-start(f32[2048,32]{1,0:T(8,128)S(1)} %copy.104) | copy-start | bytes 786436
  228.6 7.6 copy-start.18
  259.1 5.9 copy-start.3
  407.1 10.7 copy-start.5
  417.8 12.6 copy-start.10
  445.8 7.5 copy-start
  469.5 10.7 copy-start.5
  480.2 12.6 copy-start.10
  507.7 8.7 copy-start
  533.8 10.7 copy-start.5
  544.5 12.9 copy-start.10
  572.3 8.7 copy-start
  598.6 11.3 copy-start.5
  609.9 12.5 copy-start.10
  638.4 8.9 copy-start
  669.2 5.5 copy-start.8
  691.3 5.3 copy-start.9
  691.3 6.1 copy-start.12
  697.4 7.5 copy-start.15
  721.9 13.4 slice-start
  721.9 13.4 slice-start.2
  725.3 10.0 copy-start.29
  725.3 10.0 slice-start.1
  725.3 10.0 slice-start.3
  751.1 24.2 %copy-start.51 = (f32[2048]{0:T(1024)S(1)}, f32[2048]{0:T(1024)}, u32[]{:S(2)}) copy-start(f32[2048]{0:T(1024)} %param.37) | copy-start | bytes 24580
  775.3 63.8 %copy-start.13 = (f32[2048,2048]{1,0:T(8,128)S(1)}, f32[2048,2048]{1,0:T(8,128)}, u32[]{:S(2)}) copy-start(f32[2048,2048]{1,0:T(8,128)} %fusion.132) | copy-start | bytes 50331652
  839.1 34.3 %slice-start.4 = ((s8[8388608]{0:T(1024)(128)(4,1)}), s8[4194304]{0:T(1024)(128)(4,1)S(1)}, s32[]{:S(2)}) async-start(s8[8388608]{0:T(1024)(128)(4,1)} %bitcast.195), calls=%async_computation.16 | async-start | bytes 8388608
  847.7 25.7 %copy-start.24 = (bf16[2048,2048]{1,0:T(8,128)(2,1)}, bf16[2048,2048]{1,0:T(8,128)(2,1)S(1)}, u32[]{:S(2)}) copy-start(bf16[2048,2048]{1,0:T(8,128)(2,1)S(1)} %multiply_convert_fusion.1) | copy-start | bytes 25165828
  847.7 25.7 %slice-start.5 = ((s8[8388608]{0:T(1024)(128)(4,1)}), s8[4194304]{0:T(1024)(128)(4,1)S(1)}, s32[]{:S(2)}) async-start(s8[8388608]{0:T(1024)(128)(4,1)} %bitcast.195), calls=%async_computation.17 | async-start | bytes 8388608
  847.7 25.7 %copy-start.63 = (bf16[2048,2048]{1,0:T(8,128)(2,1)S(1)}, bf16[2048,2048]{1,0:T(8,128)(2,1)}, u32[]{:S(2)}) copy-start(bf16[2048,2048]{1,0:T(8,128)(2,1)} %get-tuple-element.374) | copy-start | bytes 25165828
  894.2 592.2 %reduce-scatter.5.cloned.1.call-start = ((), (), s32[]{:S(2)}) async-start(), calls=%async_computation.10 | async-start | bytes 20971520 | tf_op jit(solution)/shard_map/reduce_scatter | solution.py:212
  941.0 693.8 %reduce-scatter.3.cloned.1.call-start = ((), (), s32[]{:S(2)}) async-start(), calls=%async_computation.8 | async-start | bytes 10485760 | tf_op jit(solution)/shard_map/reduce_scatter | solution.py:150
  1214.9 274.7 %copy-start.7 = (bf16[512,2048]{1,0:T(8,128)(2,1)S(1)}, bf16[512,2048]{1,0:T(8,128)(2,1)}, u32[]{:S(2)}) copy-start(bf16[512,2048]{1,0:T(8,128)(2,1)} %param.28) | copy-start | bytes 6291460
  1214.9 274.7 %copy-start.37 = (f32[1,2048]{1,0:T(1,128)S(1)}, f32[1,2048]{1,0:T(1,128)}, u32[]{:S(2)}) copy-start(f32[1,2048]{1,0:T(1,128)} %copy-done.36) | copy-start | bytes 24580
  1215.0 274.7 %copy-start.39 = (f32[1,2048]{1,0:T(1,128)S(1)}, f32[1,2048]{1,0:T(1,128)}, u32[]{:S(2)}) copy-start(f32[1,2048]{1,0:T(1,128)} %copy-done.38) | copy-start | bytes 24580
  1215.0 274.7 %copy-start.44 = (f32[512]{0:T(512)S(1)}, f32[512]{0:T(512)}, u32[]{:S(2)}) copy-start(f32[512]{0:T(512)} %copy-done.43) | copy-start | bytes 6148
  1493.0 53.2 %copy-start.52 = (f32[2048]{0:T(1024)S(1)}, f32[2048]{0:T(1024)}, u32[]{:S(2)}) copy-start(f32[2048]{0:T(1024)} %param.37) | copy-start | bytes 24580
  1493.0 53.2 %copy-start.56 = (f32[2048]{0:T(1024)S(1)}, f32[2048]{0:T(1024)}, u32[]{:S(2)}) copy-start(f32[2048]{0:T(1024)} %param.44) | copy-start | bytes 24580
  1493.0 53.2 %copy-start.57 = (f32[2048]{0:T(1024)S(1)}, f32[2048]{0:T(1024)}, u32[]{:S(2)}) copy-start(f32[2048]{0:T(1024)} %param.51) | copy-start | bytes 24580
  1493.0 53.8 %copy-start.59 = (f32[1536]{0:T(1024)S(1)}, f32[1536]{0:T(1024)}, u32[]{:S(2)}) copy-start(f32[1536]{0:T(1024)} %param.36) | copy-start | bytes 18436
  1493.0 53.8 %copy-start.60 = (f32[1536]{0:T(1024)S(1)}, f32[1536]{0:T(1024)}, u32[]{:S(2)}) copy-start(f32[1536]{0:T(1024)} %param.43) | copy-start | bytes 18436
  1493.0 55.1 %copy-start.28 = (f32[512,256]{1,0:T(8,128)S(1)}, f32[512,256]{1,0:T(8,128)}, u32[]{:S(2)}) copy-start(f32[512,256]{1,0:T(8,128)} %param.32) | copy-start | bytes 1572868
  1493.0 55.1 %copy-start.35 = (f32[512,256]{1,0:T(8,128)S(1)}, f32[512,256]{1,0:T(8,128)}, u32[]{:S(2)}) copy-start(f32[512,256]{1,0:T(8,128)} %param.39) | copy-start | bytes 1572868
  1493.0 57.6 %copy-start.41 = (f32[6,2048]{1,0:T(8,128)S(1)}, f32[6,2048]{1,0:T(8,128)}, u32[]{:S(2)}) copy-start(f32[6,2048]{1,0:T(8,128)} %param.35) | copy-start | bytes 147460
  1493.1 57.6 %copy-start.45 = (f32[6,2048]{1,0:T(8,128)S(1)}, f32[6,2048]{1,0:T(8,128)}, u32[]{:S(2)}) copy-start(f32[6,2048]{1,0:T(8,128)} %param.42) | copy-start | bytes 147460
  1493.1 57.6 %copy-start.46 = (f32[6,2048]{1,0:T(8,128)S(1)}, f32[6,2048]{1,0:T(8,128)}, u32[]{:S(2)}) copy-start(f32[6,2048]{1,0:T(8,128)} %param.49) | copy-start | bytes 147460
  1544.6 6.7 copy-start.22
  1551.4 6.5 copy-start.23
  1551.4 6.5 copy-start.31
  1551.4 6.5 copy-start.32
  1557.9 5.3 copy-start.25
  1557.9 5.3 copy-start.33
  1563.3 71.5 %copy-start.47 = (f32[1,2048]{1,0:T(1,128)S(1)}, f32[1,2048]{1,0:T(1,128)}, u32[]{:S(2)}) copy-start(f32[1,2048]{1,0:T(1,128)} %get-tuple-element.408) | copy-start | bytes 24580
  1563.3 71.5 %copy-start.48 = (f32[1,2048]{1,0:T(1,128)S(1)}, f32[1,2048]{1,0:T(1,128)}, u32[]{:S(2)}) copy-start(f32[1,2048]{1,0:T(1,128)} %get-tuple-element.413) | copy-start | bytes 24580
  (31 other events, 103.8 us)
Sparse Core Ops, SparseCore 0:
  10.5 48.2 all-gather.9
  60.9 149.6 all-gather.7
  213.0 26.4 all-gather.11
  241.5 149.6 all-gather.19
  393.1 147.8 all-gather.13
  543.4 52.6 all-gather.15
  598.5 55.9 all-gather.17
  894.3 309.1 all-reduce.12
  1205.9 280.3 reduce-scatter.4
  1488.6 146.1 reduce-scatter.2
where the time goes:
time: 1660 us; the launch traced here: 1650 us
  waiting for transfers between devices  769 us (46%)
  matrix products  491 us (30%)
  other arithmetic  224 us (13%)
  local copies, waits for them, and re-layouts  83.1 us (5%)
  blocking collectives  59.8 us (4%)
  between operations  22.9 us (1%)
    reduce_scatter x1, waiting for transfers between devices, local(): lax.psum_scatter(jnp.concatenate([left, right], axis=1).astype(jnp.bfloat...  271 us
    psum x1, waiting for transfers between devices, local(): lax.psum(grad_qkv.astype(jnp.bfloat16), 'dp').astype(jnp.float32)  206 us
    all_gather x1, waiting for transfers between devices, local(): lax.all_gather(first_norm, 'mp', axis=0, tiled=True)  152 us
    reduce_scatter x1, waiting for transfers between devices, local(): lax.psum_scatter((attn_part + ffn_part).astype(jnp.bfloat16), 'mp', scatt...  67.3 us
    dot_general x1, matrix products, local(): jnp.dot(back_rows, full_down.T, preferred_element_type=jnp.float32)  63.8 us
    convert_element_type x4, other arithmetic, back_block(): dscores = (weights_f * (dweights - inner)).astype(jnp.bfloat16)  61.2 us
    dot_general x8, matrix products, masked_scores(): jnp.einsum('qhd,khd->hqk', query_block, key_b, preferred_element_type=jnp...  55.2 us
    dot_general x4, matrix products, back_block(): jnp.einsum('qhd,khd->hqk', dctx_block, value_b, preferred_element_type=jn...  50.5 us
  transfers between devices with their start and end apart: 10, of which 6 were waited for; matrix products, arithmetic and copies ran while one was open for 40% of the time, Pallas kernels for 0%

commit v1 on v0

v1 whole, which is shorter than its diff:
```python
import functools

import jax
import jax.numpy as jnp
from jax import lax
from jax.experimental import pallas as pl
from jax.experimental.pallas import tpu as pltpu
from jax.sharding import Mesh
from jax.sharding import PartitionSpec as P

D = 2048
HD = 128
ROT = 32
GROUP_TOK = 2048
STEP = 10

LN_EPS = 1e-05
ROPE_BASE = 10000.0
CLIP_NORM = 1.0
BETA_ONE = 0.9
BETA_TWO = 0.95
ADAM_EPS = 1e-08
DECAY = 0.01
RATE_SMALL = 1.0

F32 = jnp.float32
BF16 = jnp.bfloat16
MB = 1 << 20
SQRT_HALF = 0.7071067811865476
DENSITY = 0.3989422804014327
SCALE_TWO = HD**-0.5 * 1.4426950408889634

NN = (((1,), (0,)), ((), ()))
NT = (((1,), (1,)), ((), ()))
TN = (((0,), (0,)), ((), ()))


def mm(a, b, dims=NN):
    return lax.dot_general(a, b, dims, preferred_element_type=F32)


def cost(flops, nbytes, trans=0):
    return pl.CostEstimate(flops=int(flops), bytes_accessed=int(nbytes), transcendentals=int(trans))


def params(mib, *sem):
    return pltpu.CompilerParams(
        vmem_limit_bytes=mib * MB, dimension_semantics=sem if sem else None
    )


def shape(dims, dtype):
    return jax.ShapeDtypeStruct(dims, dtype)


HBM = pl.BlockSpec(memory_space=pl.ANY)


def after(value, *earlier):
    return lax.optimization_barrier((value, earlier))[0]


def fetch(table, sources, buf, sem):
    step, last = pl.program_id(0), pl.num_programs(0) - 1
    size = buf.shape[1]

    def start(at):
        slot = lax.rem(at, 2)
        for i, source in enumerate(sources):

            @pl.when(table[at, 1] == i)
            def _(source=source):
                span = pl.ds(pl.multiple_of(table[at, 2] * size, size), size)
                pltpu.make_async_copy(source.at[span], buf.at[slot], sem.at[slot]).start()

    @pl.when(step == 0)
    def _():
        start(step)

    @pl.when(step < last)
    def _():
        start(step + 1)

    slot = lax.rem(step, 2)
    pltpu.make_async_copy(sources[0].at[pl.ds(0, size)], buf.at[slot], sem.at[slot]).wait()
    return slot


def turn(u, cosine, low, high):
    return u * cosine + pltpu.roll(u, HD - ROT // 2, 1) * low + pltpu.roll(u, ROT // 2, 1) * high


def turn_back(g, cosine, low, high):
    return g * cosine - pltpu.roll(g, HD - ROT // 2, 1) * low - pltpu.roll(g, ROT // 2, 1) * high


def enter_kernel(many, units, table, *refs):
    sources = refs[:many]
    vec_ref, w_ref, bu_ref, bq_ref, cos_ref, low_ref, high_ref = refs[many : many + 7]
    xo_ref, a1_ref, a2_ref, stat_ref, act_ref, gp_ref, qkv_ref, buf, sem = refs[-9:]
    slot = fetch(table, sources, buf, sem)
    x_in = buf[slot]
    xo_ref[...] = x_in
    x = x_in.astype(F32)
    mean = jnp.mean(x, axis=1, keepdims=True)
    centre = x - mean
    rstd = lax.rsqrt(jnp.mean(centre * centre, axis=1, keepdims=True) + LN_EPS)
    xhat = centre * rstd
    a1_ref[...] = (xhat * vec_ref[0:1, :] + vec_ref[1:2, :]).astype(BF16)
    a2_ref[...] = (xhat * vec_ref[2:3, :] + vec_ref[3:4, :]).astype(BF16)
    lane = lax.broadcasted_iota(jnp.int32, stat_ref.shape, 1)
    stat_ref[...] = jnp.where(lane == 0, mean, rstd)
    tile = min(1024, units)
    for at in range(0, units, tile):
        span = slice(at, at + tile)
        hidden = mm(a2_ref[...], w_ref[:, span]) + bu_ref[:, span]
        phi_cum = 0.5 + 0.5 * lax.erf(hidden * SQRT_HALF)
        act_ref[:, span] = (hidden * phi_cum).astype(BF16)
        dens = jnp.exp(-0.5 * hidden * hidden) * DENSITY
        gp_ref[:, span] = (phi_cum + hidden * dens).astype(BF16)
    mixed = mm(a1_ref[...], w_ref[:, units:]) + bq_ref[...]
    rotation = (cos_ref[...], low_ref[...], high_ref[...])
    for part in range(mixed.shape[1] // HD):
        piece = mixed[:, part * HD : (part + 1) * HD]
        if part % 3 < 2:
            piece = turn(piece, *rotation)
        qkv_ref[:, part * HD : (part + 1) * HD] = piece.astype(BF16)


def enter(rows, table, sources, norm_vec, w_in, b_up, b_qkv, rotation, old):
    many, steps = len(sources), table.shape[0]
    units, wide = b_up.shape[1], b_qkv.shape[1]
    group = rotation[0].shape[0]
    row = lambda n: pl.BlockSpec((rows, n), lambda i, p: (p[i, 0], 0))
    fixed = lambda v: pl.BlockSpec(v.shape, lambda i, p: (0, 0), pipeline_mode=pl.Buffered(1))
    in_specs = [HBM] * many + [fixed(v) for v in (norm_vec, w_in, b_up, b_qkv)] + [row(HD)] * 3
    args = [table, *sources, norm_vec, w_in, b_up, b_qkv, *rotation]
    widths = ((D, BF16), (D, BF16), (D, BF16), (128, F32), (units, BF16), (units, BF16), (wide, BF16))
    aliases = {}
    if old is not None:
        aliases = {len(args) + i: i for i in range(7)}
        in_specs += [HBM] * 7
        args += list(old)
    return pl.pallas_call(
        functools.partial(enter_kernel, many, units),
        grid_spec=pltpu.PrefetchScalarGridSpec(
            num_scalar_prefetch=1,
            grid=(steps,),
            in_specs=in_specs,
            out_specs=[row(n) for n, _ in widths],
            scratch_shapes=[pltpu.VMEM((2, rows, D), BF16), pltpu.SemaphoreType.DMA((2,))],
        ),
        out_shape=[shape((group, n), kind) for n, kind in widths],
        input_output_aliases=aliases,
        compiler_params=params(60),
        cost_estimate=cost(2 * steps * rows * D * (units + wide), 2 * D * (units + wide)),
        name="enter",
    )(*args)


def masked(scores, at, cases, width, begin):
    key_at = lax.broadcasted_iota(jnp.int32, (width, width), 0)
    query_at = lax.broadcasted_iota(jnp.int32, (width, width), 1)
    ok = key_at <= query_at
    if at == cases - 1:
        ok = ok & (key_at + at * width >= begin)
    return jnp.where(ok, scores, -jnp.inf)


def fwd_case(at, cases, width, q_ref, k_ref, v_ref, begin_ref, o_ref, lse_ref):
    first = at * width
    query, begin = q_ref[...], begin_ref[...]
    near = masked(mm(k_ref[first : first + width, :], query, NT), at, cases, width, begin)
    top = jnp.max(near, axis=0, keepdims=True)
    if at:
        far = mm(k_ref[0:first, :], query, NT)
        if at == cases - 1:
            far = far + jnp.where(begin > 0, -jnp.inf, 0.0)
        top = jnp.maximum(top, jnp.max(far, axis=0, keepdims=True))
    near = jnp.exp2((near - top) * SCALE_TWO)
    total = jnp.sum(near, axis=0, keepdims=True)
    if at:
        far = jnp.exp2((far - top) * SCALE_TWO)
        total = total + jnp.sum(far, axis=0, keepdims=True)
    part = 1.0 / total
    out = mm(v_ref[first : first + width, :], (near * part).astype(BF16), TN)
    if at:
        out = out + mm(v_ref[0:first, :], (far * part).astype(BF16), TN)
    o_ref[...] = out.T.astype(BF16)
    lse_ref[0] = top * SCALE_TWO + jnp.log2(total)


def attn_fwd_kernel(cases, width, q_ref, k_ref, v_ref, begin_ref, *rest):
    o_ref, lse_ref = rest[-2:]
    for at in range(cases):

        @pl.when(pl.program_id(1) == at)
        def _(at=at):
            fwd_case(at, cases, width, q_ref, k_ref, v_ref, begin_ref, o_ref, lse_ref)


def attn_fwd(first, count, qkv, begin, old):
    group = qkv.shape[0]
    heads = qkv.shape[1] // (3 * HD)
    width = min(1024, group)
    cases = group // width
    flops = 2 * 2 * count * group * group * HD * 5 // 8
    in_specs = [
        pl.BlockSpec((width, HD), lambda h, i: (i, 3 * (first + h))),
        pl.BlockSpec((group, HD), lambda h, i: (0, 3 * (first + h) + 1)),
        pl.BlockSpec((group, HD), lambda h, i: (0, 3 * (first + h) + 2)),
        pl.BlockSpec((1, width), lambda h, i: (0, i)),
    ]
    args, aliases = [qkv, qkv, qkv, begin], {}
    if old is not None:
        aliases = {len(args) + i: i for i in range(2)}
        in_specs += [HBM] * 2
        args += list(old)
    return pl.pallas_call(
        functools.partial(attn_fwd_kernel, cases, width),
        grid=(count, cases),
        in_specs=in_specs,
        out_specs=[
            pl.BlockSpec((width, HD), lambda h, i: (i, first + h)),
            pl.BlockSpec((1, 1, width), lambda h, i: (first + h, 0, i)),
        ],
        out_shape=[shape((group, heads * HD), BF16), shape((heads, 1, group), F32)],
        input_output_aliases=aliases,
        compiler_params=params(56),
        cost_estimate=cost(4 * flops, 8 * group * count * HD, count * group * group * 5 // 8),
        name="attend",
    )(*args)


def bwd_case(at, cases, width, refs):
    (q_ref, k_ref, v_ref, do_ref, begin_ref, lse_ref, dk_acc, dv_acc) = refs
    first = at * width
    query, dctx, begin, lse = q_ref[...], do_ref[...], begin_ref[...], lse_ref[0]
    spans = [slice(first, first + width)] + ([slice(0, first)] if at else [])
    parts = []
    for span in spans:
        scores = mm(k_ref[span, :], query, NT) * SCALE_TWO - lse
        if span.start == first:
            scores = masked(scores, at, cases, width, begin)
        elif at == cases - 1:
            scores = scores + jnp.where(begin > 0, -jnp.inf, 0.0)
        prob = jnp.exp2(scores)
        dprob = mm(v_ref[span, :], dctx, NT)
        parts.append((span, prob, dprob, jnp.sum(prob * dprob, axis=0, keepdims=True)))
    inner = sum(p[3] for p in parts)
    dq = None
    for span, prob, dprob, _ in parts:
        dscores = (prob * (dprob - inner)).astype(BF16)
        dv_acc[span, :] += mm(prob.astype(BF16), dctx)
        dk_acc[span, :] += mm(dscores, query)
        more = mm(k_ref[span, :], dscores, TN)
        dq = more if dq is None else dq + more
    return dq.T


def attn_bwd_kernel(
    cases, width, q_ref, k_ref, v_ref, do_ref, begin_ref, lse_ref, cos_ref, low_ref, high_ref,
    out_ref, sum_ref, dk_acc, dv_acc,
):
    step = pl.program_id(1)

    @pl.when(step == 0)
    def _():
        dk_acc[...] = jnp.zeros_like(dk_acc)
        dv_acc[...] = jnp.zeros_like(dv_acc)

    refs = (q_ref, k_ref, v_ref, do_ref, begin_ref, lse_ref, dk_acc, dv_acc)
    for at in range(cases):

        @pl.when(step == at)
        def _(at=at):
            dq = bwd_case(at, cases, width, refs) * (HD**-0.5)
            span = slice(at * width, (at + 1) * width)
            back = turn_back(dq, cos_ref[span, :], low_ref[span, :], high_ref[span, :])
            out_ref[span, 0:HD] = back.astype(BF16)

    @pl.when(step == cases - 1)
    def _():
        dk = dk_acc[...] * (HD**-0.5)
        back = turn_back(dk, cos_ref[...], low_ref[...], high_ref[...])
        out_ref[:, HD : 2 * HD] = back.astype(BF16)
        out_ref[:, 2 * HD : 3 * HD] = dv_acc[...].astype(BF16)
        total = jnp.sum(out_ref[...].astype(F32), axis=0, keepdims=True)
        sum_ref[...] = jnp.broadcast_to(total, sum_ref.shape)


def attn_bwd(qkv, dctx, begin, lse, tables):
    group = qkv.shape[0]
    heads = qkv.shape[1] // (3 * HD)
    width = min(512, group)
    cases = group // width
    table = pl.BlockSpec((group, HD), lambda h, i: (0, 0))
    flops = 5 * 2 * heads * group * group * HD * 5 // 8
    return pl.pallas_call(
        functools.partial(attn_bwd_kernel, cases, width),
        grid=(heads, cases),
        in_specs=[
            pl.BlockSpec((width, HD), lambda h, i: (i, 3 * h)),
            pl.BlockSpec((group, HD), lambda h, i: (0, 3 * h + 1)),
            pl.BlockSpec((group, HD), lambda h, i: (0, 3 * h + 2)),
            pl.BlockSpec((width, HD), lambda h, i: (i, h)),
            pl.BlockSpec((1, width), lambda h, i: (0, i)),
            pl.BlockSpec((1, 1, width), lambda h, i: (h, 0, i)),
            table,
            table,
            table,
        ],
        out_specs=[
            pl.BlockSpec((group, 3 * HD), lambda h, i: (0, h)),
            pl.BlockSpec((8, 3 * HD), lambda h, i: (0, h)),
        ],
        out_shape=[shape((group, heads * 3 * HD), BF16), shape((8, heads * 3 * HD), F32)],
        scratch_shapes=[pltpu.VMEM((group, HD), F32), pltpu.VMEM((group, HD), F32)],
        compiler_params=params(56),
        cost_estimate=cost(flops / 2, 3 * group * heads * HD),
        name="attend_back",
    )(qkv, qkv, qkv, dctx, begin, lse, *tables)


def branch_kernel(units, o_ref, act_ref, w_ref, out_ref):
    total = mm(act_ref[...], w_ref[0:units, :]) + mm(o_ref[...], w_ref[units:, :])
    out_ref[...] = total.astype(BF16)


def branch_all(o, act, w_back):
    group, heads, units = o.shape[0], o.shape[1], act.shape[1]
    rows, tile = 512, D // 2
    return pl.pallas_call(
        functools.partial(branch_kernel, units),
        grid=(D // tile, group // rows),
        in_specs=[
            pl.BlockSpec((rows, heads), lambda j, i: (i, 0)),
            pl.BlockSpec((rows, units), lambda j, i: (i, 0)),
            pl.BlockSpec((heads + units, tile), lambda j, i: (0, j)),
        ],
        out_specs=pl.BlockSpec((rows, tile), lambda j, i: (i, j)),
        out_shape=shape((group, D), BF16),
        compiler_params=params(56),
        cost_estimate=cost(2 * group * D * (heads + units), 2 * D * (heads + units)),
        name="branch",
    )(o, act, w_back)


def leave_kernel(many, units, table, *refs):
    sources, (w_ref, gp_ref) = refs[:many], refs[many : many + 2]
    eo_ref, dh_ref, do_ref, sum_ref, buf, sem = refs[-6:]
    slot = fetch(table, sources, buf, sem)

    @pl.when(pl.program_id(0) == 0)
    def _():
        sum_ref[...] = jnp.zeros_like(sum_ref)

    back = buf[slot]
    eo_ref[...] = back
    tile = min(1024, units)
    for at in range(0, units, tile):
        span = slice(at, at + tile)
        dact = mm(back, w_ref[span, :], NT)
        dhid = (dact * gp_ref[:, span].astype(F32)).astype(BF16)
        dh_ref[:, span] = dhid
        total = jnp.sum(dhid.astype(F32), axis=0, keepdims=True)
        sum_ref[:, span] += jnp.broadcast_to(total, (8, tile))
    do_ref[...] = mm(back, w_ref[units:, :], NT).astype(BF16)


def leave(rows, table, sources, w_back, gp, old):
    many, steps = len(sources), table.shape[0]
    group, units = gp.shape
    heads = w_back.shape[0] - units
    row = lambda n: pl.BlockSpec((rows, n), lambda i, p: (p[i, 0], 0))
    in_specs = [HBM] * many + [
        pl.BlockSpec(w_back.shape, lambda i, p: (0, 0), pipeline_mode=pl.Buffered(1)),
        row(units),
    ]
    args = [table, *sources, w_back, gp]
    aliases = {}
    if old is not None:
        aliases = {len(args) + i: i for i in range(3)}
        in_specs += [HBM] * 3
        args += list(old)
    return pl.pallas_call(
        functools.partial(leave_kernel, many, units),
        grid_spec=pltpu.PrefetchScalarGridSpec(
            num_scalar_prefetch=1,
            grid=(steps,),
            in_specs=in_specs,
            out_specs=[row(D), row(units), row(heads), pl.BlockSpec((8, units), lambda i, p: (0, 0))],
            scratch_shapes=[pltpu.VMEM((2, rows, D), BF16), pltpu.SemaphoreType.DMA((2,))],
        ),
        out_shape=[
            shape((group, D), BF16),
            shape((group, units), BF16),
            shape((group, heads), BF16),
            shape((8, units), F32),
        ],
        input_output_aliases=aliases,
        compiler_params=params(60),
        cost_estimate=cost(2 * steps * rows * D * (units + heads), 2 * D * (units + heads)),
        name="leave",
    )(*args)


def din_kernel(dm_ref, dh_ref, w_ref, x_ref, stat_ref, vec_ref, g_ref, sum_ref):
    units = dh_ref.shape[1]
    left = mm(dm_ref[...], w_ref[:, units:], NT)
    right = mm(dh_ref[...], w_ref[:, 0:units], NT)
    g_ref[...] = (left * vec_ref[0:1, :] + right * vec_ref[2:3, :]).astype(BF16)
    xhat = (x_ref[...].astype(F32) - stat_ref[:, 0:1]) * stat_ref[:, 1:2]
    rows = [left * xhat, left, right * xhat, right]
    sums = jnp.concatenate(
        [jnp.sum(r, axis=0, keepdims=True) for r in rows] + [jnp.zeros((4, left.shape[1]), F32)], axis=0
    )

    @pl.when(pl.program_id(1) == 0)
    def _():
        sum_ref[...] = sums

    @pl.when(pl.program_id(1) > 0)
    def _():
        sum_ref[...] += sums


def din_all(dmixed, dhid, w_in, x, stat, norm_vec):
    group, heads3, units = dmixed.shape[0], dmixed.shape[1], dhid.shape[1]
    rows, tile = 512, 1024
    return pl.pallas_call(
        din_kernel,
        grid=(D // tile, group // rows),
        in_specs=[
            pl.BlockSpec((rows, heads3), lambda j, i: (i, 0)),
            pl.BlockSpec((rows, units), lambda j, i: (i, 0)),
            pl.BlockSpec((tile, heads3 + units), lambda j, i: (j, 0)),
            pl.BlockSpec((rows, tile), lambda j, i: (i, j)),
            pl.BlockSpec((rows, 128), lambda j, i: (i, 0)),
            pl.BlockSpec((6, tile), lambda j, i: (0, j)),
        ],
        out_specs=[
            pl.BlockSpec((rows, tile), lambda j, i: (i, j)),
            pl.BlockSpec((8, tile), lambda j, i: (0, j)),
        ],
        out_shape=[shape((group, D), BF16), shape((8, D), F32)],
        compiler_params=params(60),
        cost_estimate=cost(group * D * (heads3 + units) / 2, D * (heads3 + units) / 2),
        name="input_back",
    )(dmixed, dhid, w_in, x, stat, norm_vec)


def wgrad_kernel(n_left, n_right, cut_left, many, place, *refs):
    lefts, rights = refs[:n_left], refs[n_left : n_left + n_right]
    rest = refs[n_left + n_right :]
    got, outs = (rest[0], rest[1:]) if len(rest) > many else (None, rest)
    pairs = list(zip(lefts, rights)) if cut_left else [(v, rights[0]) for v in lefts]
    values = [mm(a[...], b[...], TN) for a, b in pairs]
    axis = 1 if cut_left else 0

    def put(ref):
        at = 0
        for value in values:
            span = slice(at, at + value.shape[axis])
            at += value.shape[axis]
            view = (0, slice(None), span) if cut_left else (0, span, slice(None))
            if got is not None:
                value = value + got[view].astype(F32)
            ref[view] = value.astype(BF16)

    if many == 1:
        put(outs[0])
    else:
        for i in range(many):

            @pl.when(pl.program_id(0) == i)
            def _(i=i):
                put(outs[i])


def wgrad(lefts, rights, cut_left, weight, place, quads, got):
    rows = lefts[0].shape[0]
    whole = lambda n: pl.BlockSpec((rows, n), lambda i, p: (0, 0), pipeline_mode=pl.Buffered(1))
    part = lambda n: pl.BlockSpec((rows, n // (2 * quads)), lambda i, p: (0, 2 * (i ^ p[1]) + p[0]))
    widths = [v.shape[1] for v in lefts], [v.shape[1] for v in rights]
    if cut_left:
        in_specs = [part(n) for n in widths[0]] + [whole(n) for n in widths[1]]
        tile = (widths[0][0] // (2 * quads), sum(widths[1]))
    else:
        in_specs = [whole(n) for n in widths[0]] + [part(n) for n in widths[1]]
        tile = (sum(widths[0]), widths[1][0] // (2 * quads))
    args = [place, *lefts, *rights]
    stacked = pl.BlockSpec((1, *tile), lambda i, p: (i, 0, 0))
    if got is None:
        out_specs, out_shape = [stacked], [shape((quads, *tile), BF16)]
    else:
        in_specs.append(stacked)
        args.append(got)
        out_specs = [
            pl.BlockSpec((1, *tile), lambda i, p: (0, 0, 0), pipeline_mode=pl.Buffered(1))
        ] * quads
        out_shape = [shape((1, *tile), BF16)] * quads
    flops = rows * tile[0] * tile[1] * 2 * quads * weight
    return pl.pallas_call(
        functools.partial(wgrad_kernel, len(lefts), len(rights), cut_left, len(out_specs)),
        grid_spec=pltpu.PrefetchScalarGridSpec(
            num_scalar_prefetch=1, grid=(quads,), in_specs=in_specs, out_specs=out_specs
        ),
        out_shape=out_shape,
        compiler_params=params(60),
        cost_estimate=cost(flops, 2 * rows * sum(widths[0] + widths[1])),
        name="weight_grad",
    )(*args)


def part_kernel(n_left, turns, size, place, *refs):
    lefts, rights, rest = refs[:n_left], refs[n_left : n_left + turns], refs[n_left + turns :]
    base_ref = rest[0] if len(rest) == 4 else None
    out_ref, rows_ref, sem = rest[-3:]

    @pl.when(pl.program_id(0) == 0)
    def _():
        copies, at = [], 0
        for i, left in enumerate(lefts):
            span = slice(at, at + left.shape[1])
            at += left.shape[1]
            for k in range(turns):
                source = left.at[pl.ds(pl.multiple_of(place[2 + k] * size, size), size)]
                target = rows_ref.at[k * size : (k + 1) * size, span]
                copies.append(pltpu.make_async_copy(source, target, sem.at[i, k]))
        for copy in copies:
            copy.start()
        for copy in copies:
            copy.wait()

    right = jnp.concatenate([r[...] for r in rights], axis=0) if turns > 1 else rights[0][...]
    value = mm(rows_ref[...], right, TN)
    if base_ref is not None:
        value = value + base_ref[0]
    out_ref[0] = value.astype(out_ref.dtype)


def wgrad_part(lefts, right, size, place, turns, quads, base):
    widths = [v.shape[1] for v in lefts]
    tile = (sum(widths), right.shape[1] // (2 * quads))
    in_specs = [HBM] * len(lefts) + [
        pl.BlockSpec((size, tile[1]), lambda i, p, k=k: (p[2 + k], 2 * (i ^ p[1]) + p[0]))
        for k in range(turns)
    ]
    args = [place, *lefts] + [right] * turns
    stacked = pl.BlockSpec((1, *tile), lambda i, p: (i, 0, 0))
    if base is not None:
        in_specs.append(stacked)
        args.append(base)
    return pl.pallas_call(
        functools.partial(part_kernel, len(lefts), turns, size),
        grid_spec=pltpu.PrefetchScalarGridSpec(
            num_scalar_prefetch=1,
            grid=(quads,),
            in_specs=in_specs,
            out_specs=stacked,
            scratch_shapes=[
                pltpu.VMEM((turns * size, tile[0]), BF16),
                pltpu.SemaphoreType.DMA((len(lefts), turns)),
            ],
        ),
        out_shape=shape((quads, *tile), F32 if base is None else BF16),
        compiler_params=params(60),
        cost_estimate=cost(size * turns * tile[0] * tile[1] * 2 * quads, 0),
        name="weight_grad_part",
    )(*args)


def line_turns(count):
    table = []
    for place in range(count):
        order = []
        for step in range(1, count):
            if place - step >= 0:
                order.append((True, step))
            if place + step < count:
                order.append((False, step))
        table.append(order)
    return table


def lookup(table, place):
    return jnp.asarray(table, jnp.int32)[place]


class Gather:
    def __init__(self, pieces, count, place):
        self.right, self.left = [[v] for v in pieces], [[v] for v in pieces]
        self.count, self.place = count, place

    def step(self, piece, *earlier):
        count, right, left = self.count, self.right[piece], self.left[piece]
        step = len(right)
        here, there = after((right[-1], left[-1]), *earlier)
        right.append(lax.ppermute(here, "mp", [(i, i + 1) for i in range(step - 1, count - 1)]))
        left.append(lax.ppermute(there, "mp", [(i + 1, i) for i in range(0, count - step)]))

    def last(self):
        return [(r[-1], l[-1]) for r, l in zip(self.right, self.left)]

    def turns(self, first, last, size):
        count, many = self.count, len(self.right)
        each = self.right[0][0].shape[0] // size
        turns = line_turns(count)
        sources, tables = [], [[] for _ in range(count)]
        for turn_at in range(first, last + 1):
            for piece in range(many):
                for i in range(count):
                    side, far = turns[i][turn_at - 1] if turn_at else (True, 0)
                    key = (side, far, piece)
                    if key not in sources:
                        sources.append(key)
                    at = (i - far if side else i + far) * many + piece
                    tables[i] += [[at * each + k, sources.index(key), k] for k in range(each)]
        arrays = [(self.right if side else self.left)[piece][far] for side, far, piece in sources]
        return lookup(tables, self.place), arrays


def everywhere(value, axes):
    for axis, size in axes:
        hop = 1
        while hop < size:
            value = value + lax.ppermute(value, axis, [(i, i ^ hop) for i in range(size)])
            hop *= 2
    return value


def adam_step(weight, grad, first, second, rate, decay):
    first_new = BETA_ONE * first + (1.0 - BETA_ONE) * grad
    second_new = BETA_TWO * second + (1.0 - BETA_TWO) * grad * grad
    first_hat = first_new / (1.0 - BETA_ONE**STEP)
    second_hat = second_new / (1.0 - BETA_TWO**STEP)
    weight_new = weight - rate * (first_hat / (jnp.sqrt(second_hat) + ADAM_EPS) + decay * weight)
    return (weight_new, first_new, second_new)


def rotation_tables(position):
    half = ROT // 2
    inverse = ROPE_BASE ** (-jnp.arange(half, dtype=F32) * 2.0 / ROT)
    angle = position[:, None] * inverse[None, :]
    cosine, sine = jnp.cos(angle), jnp.sin(angle)
    rows = position.shape[0]
    rest = jnp.zeros((rows, HD - ROT), F32)
    zero = jnp.zeros((rows, half), F32)
    return (
        jnp.concatenate([cosine, cosine, rest + 1.0], axis=1),
        jnp.concatenate([-sine, zero, rest], axis=1),
        jnp.concatenate([zero, sine, rest], axis=1),
    )


def local(
    tokens, cotangent, lengths, w_qkv, w_out, w_up, w_down, norm_vec, b_qkv, b_up,
    m_qkv, m_out, m_up, m_down, m_norm, m_bqkv, m_bup,
    v_qkv, v_out, v_up, v_down, v_norm, v_bqkv, v_bup,
):
    rows = tokens.shape[0]
    count = lax.axis_size("mp")
    quads = lax.axis_size("quad")
    place = lax.axis_index("mp")
    core = lax.axis_index("pair")
    group = rows * count
    dp = ("quad", "pair")

    first_len = lengths[0, 0]
    used = lengths[0, 0] + lengths[0, 1]
    row_ids = jnp.arange(group, dtype=jnp.int32)
    begin = jnp.where(row_ids >= used, used, jnp.where(row_ids >= first_len, first_len, 0))
    begin = begin.astype(jnp.int32)
    tables = rotation_tables((row_ids - begin).astype(F32))
    begin = begin.reshape(1, group)
    own_ids = jnp.arange(rows, dtype=jnp.int32) + place * rows
    live_own = (own_ids < used).astype(BF16)

    sub = min(256, rows)
    back_own = cotangent * live_own[:, None]
    x_line = Gather([tokens], count, place)
    x_line.step(0)
    full_in = jnp.concatenate([w_up.astype(BF16), w_qkv.astype(BF16)], axis=1)
    full_in = lax.all_gather(full_in, dp, axis=0, tiled=True)
    late_down, late_out = after((w_down, w_out), x_line.last()[0])
    full_back = jnp.concatenate([late_down.astype(BF16), late_out.astype(BF16)], axis=0)
    full_back = lax.all_gather(full_back, dp, axis=1, tiled=True)
    b_up_row, b_qkv_row = b_up.reshape(1, -1), b_qkv.reshape(1, -1)

    for step in range(2, count):
        x_line.step(0)
    enter_rest = (norm_vec, full_in, b_up_row, b_qkv_row, tables)
    table, sources = x_line.turns(0, count - 2, sub)
    state = enter(sub, table, sources, *enter_rest, None)
    e_line = Gather([after(back_own, state[0])], count, place)
    e_line.step(0)
    table, sources = x_line.turns(count - 1, count - 1, sub)
    table = after(table, state, x_line.last())
    state = enter(sub, table, sources, *enter_rest, state)
    x_all, a1, a2, stat, act, gelu_slope, qkv = state

    heads = qkv.shape[1] // (3 * HD)
    attended = attn_fwd(0, heads // 2, qkv, begin, None)
    e_line.step(0, attended[0])
    attended, lse = attn_fwd(heads // 2, heads - heads // 2, qkv, begin, attended)
    parts = branch_all(attended, act, full_back)

    def leave_at(first, last, old, *earlier):
        table, sources = e_line.turns(first, last, sub)
        old = None if old is None else old[:3]
        return leave(sub, after(table, *earlier), sources, full_back, gelu_slope, old)

    for step in range(3, count):
        e_line.step(0, parts)
    one = leave_at(0, 1, None, parts)
    two = leave_at(2, count - 2, one, one)
    quad = lax.axis_index("quad")
    here = jnp.stack([core, quad]).astype(jnp.int32)
    there = jnp.stack([1 - core, quad]).astype(jnp.int32)
    arrival = lookup(
        [[i] + [i - far if side else i + far for side, far in line_turns(count)[i]] for i in range(count)],
        place,
    )
    second = (act, attended)
    early = jnp.concatenate([there, arrival[: count - 1]])
    give_second = wgrad_part(second, two[0], rows, after(early, two[1]), count - 1, quads, None)
    three = leave_at(count - 1, count - 1, two, give_second, e_line.last())
    back_rows, dhid, dctx = three[:3]
    grad_bup = (one[3] + two[3] + three[3])[0]
    parts = after(parts, give_second, e_line.last())
    branch = lax.psum_scatter(parts, "mp", scatter_dimension=0, tiled=True)

    def give(product, *earlier):
        half = wgrad(*product, after(there, *earlier), quads, None)[0]
        return lax.ppermute(half, "pair", [(0, 1), (1, 0)]), half

    def settle(product, got, *earlier):
        blocks = wgrad(*product, after(here, *earlier), quads, got)
        terms = [
            lax.ppermute(blocks[hop], "quad", [(i, i ^ hop) for i in range(quads)])
            for hop in range(1, quads)
        ]
        return [blocks[0]] + terms

    def total(terms):
        return sum(v[0].astype(F32) for v in terms)

    up = ((a2,), (dhid,), True, 0.05)
    late = jnp.concatenate([there, arrival[count - 1 :]])
    mark = wgrad_part(second, back_rows, rows, after(late, dhid), 1, quads, give_second)
    got_second = lax.ppermute(mark, "pair", [(0, 1), (1, 0)])
    got_up, mark = give(up, mark)
    sum_second = settle((second, (back_rows,), False, 0.25), got_second, mark)
    dmixed, col_qkv = attn_bwd(qkv, dctx, after(begin, sum_second[0]), lse, tables)
    grad_bqkv = col_qkv[0]
    inner = ((a1,), (dmixed,), True, 9)
    sum_up = settle(up, got_up, dmixed)
    grad_parts, col = din_all(
        after(dmixed, sum_up[0], *sum_second[1:]), dhid, full_in, x_all, stat, norm_vec
    )
    grad_rows = lax.psum_scatter(grad_parts, "mp", scatter_dimension=0, tiled=True).astype(F32)

    back_vals = back_own.astype(F32)
    out_bias = jnp.sum(back_vals, axis=0)
    small = jnp.concatenate([col[0:4], out_bias[None], out_bias[None]], axis=0)
    packed = jnp.concatenate([small.reshape(-1), grad_bqkv, grad_bup]).reshape(-1, 128)
    got_inner, mark = give(inner, grad_parts, branch, *sum_up[1:])
    packed = everywhere(packed, (("pair", 2),))
    sum_inner = settle(inner, got_inner, mark, packed)
    packed = everywhere(packed, (("quad", quads),))
    part_up, part_qkv, sum_second = total(sum_up), total(sum_inner), total(sum_second)
    units = act.shape[1]
    part_down, part_out = sum_second[:units], sum_second[units:]
    token_vals = tokens.astype(F32)
    layer_out = (token_vals + branch.astype(F32) + norm_vec[4] + norm_vec[5]).astype(BF16)

    n_small = small.size // 128
    n_qkv = grad_bqkv.size // 128
    small_sum = everywhere(packed[:n_small], (("mp", count),))
    grad_small = small_sum.reshape(6, D)
    sum_bqkv = packed[n_small : n_small + n_qkv].reshape(-1)
    sum_bup = packed[n_small + n_qkv :].reshape(-1)

    mean, rstd = (lax.dynamic_slice_in_dim(stat, place * rows, rows, 0)[:, i : i + 1] for i in (0, 1))
    xhat = (token_vals - mean) * rstd
    grad_in = back_vals + rstd * (
        grad_rows
        - jnp.mean(grad_rows, axis=1, keepdims=True)
        - xhat * jnp.mean(grad_rows * xhat, axis=1, keepdims=True)
    )
    grad_in = grad_in.astype(BF16)

    local_squares = (
        jnp.sum(part_qkv * part_qkv)
        + jnp.sum(part_out * part_out)
        + jnp.sum(part_up * part_up)
        + jnp.sum(part_down * part_down)
        + (jnp.sum(sum_bqkv * sum_bqkv) + jnp.sum(sum_bup * sum_bup)) / (2 * quads)
    )
    total = everywhere(
        jnp.broadcast_to(local_squares, (8, 128)), (("pair", 2), ("quad", quads), ("mp", count))
    )[0, 0]
    grad_norm = jnp.sqrt(total + jnp.sum(grad_small * grad_small))
    factor = jnp.minimum(1.0, CLIP_NORM / (grad_norm + 1e-06))
    rate_big = 2.5 * D ** (-0.5)
    rate_out = 2.5 * max(16 * D // GROUP_TOK, 1) ** (-0.5)
    upd_qkv, mom_qkv, sec_qkv = adam_step(w_qkv, factor * part_qkv, m_qkv, v_qkv, rate_big, DECAY)
    upd_out, mom_out, sec_out = adam_step(w_out, factor * part_out, m_out, v_out, rate_out, DECAY)
    upd_up, mom_up, sec_up = adam_step(w_up, factor * part_up, m_up, v_up, rate_big, DECAY)
    upd_down, mom_down, sec_down = adam_step(
        w_down, factor * part_down, m_down, v_down, rate_big, DECAY
    )
    upd_norm, mom_norm, sec_norm = adam_step(
        norm_vec, factor * grad_small, m_norm, v_norm, RATE_SMALL, 0.0
    )
    upd_bqkv, mom_bqkv, sec_bqkv = adam_step(
        b_qkv, factor * sum_bqkv, m_bqkv, v_bqkv, RATE_SMALL, 0.0
    )
    upd_bup, mom_bup, sec_bup = adam_step(b_up, factor * sum_bup, m_bup, v_bup, RATE_SMALL, 0.0)
    return (
        layer_out, grad_in, grad_norm,
        upd_qkv, upd_out, upd_up, upd_down, upd_norm, upd_bqkv, upd_bup,
        mom_qkv, mom_out, mom_up, mom_down, mom_norm, mom_bqkv, mom_bup,
        sec_qkv, sec_out, sec_up, sec_down, sec_norm, sec_bqkv, sec_bup,
    )


def solution(mesh):
    devices = mesh.devices
    split = Mesh(
        devices.reshape(devices.shape[0] // 2, 2, devices.shape[1]), ("quad", "pair", "mp")
    )
    dp = ("quad", "pair")
    tok, row, col = P(("quad", "pair", "mp"), None), P(dp, "mp"), P("mp", dp)
    weights = (row, col, row, col, P(), P("mp"), P("mp"))
    return jax.shard_map(
        local,
        mesh=split,
        in_specs=(tok, tok, P(dp, None)) + weights * 3,
        out_specs=(tok, tok, P()) + weights * 3,
        check_vma=False,
    )
```

time: 1660 us -> 665 us (0.40)
  waiting for transfers between devices: 769 us -> 133 us
  matrix products: 491 us -> 0 us
  Pallas kernels: 0 us -> 352 us
  other arithmetic: 224 us -> 68.8 us
  local copies, waits for them, and re-layouts: 83.1 us -> 15.7 us
  starting transfers between devices: 0.59 us -> 65.9 us
  blocking collectives: 59.8 us -> 0 us
    dot_general x40 -> x0, matrix products: 491 us -> none  [the longest x1 63.8 us: local(): jnp.dot(back_rows, full_down.T, preferred_element_type=jnp.float32)]
    pallas_call x0 -> x17, Pallas kernels: none -> 352 us  [the longest x5 79.3 us: wgrad(): pl.pallas_call(functools.partial(wgrad_kernel, len(lefts), len(rights), c...]
    reduce_scatter x2, waiting for transfers between devices: 339 us -> 5.43 us  [the longest x1 5.42 us: local(): lax.psum_scatter(grad_parts, 'mp', scatter_dimension=0, tiled=True)]
    all_gather x7 -> x2, waiting for transfers between devices: 223 us -> 0.02 us  [the longest x1 0.02 us: local(): full_in = lax.all_gather(full_in, dp, axis=0, tiled=True)]
    psum x1 -> x0, waiting for transfers between devices: 206 us -> none  [local(): lax.psum(grad_qkv.astype(jnp.bfloat16), 'dp').astype(jnp.float32)]
    ppermute x0 -> x34, waiting for transfers between devices: none -> 128 us  [the longest x6 81 us: step(): lax.ppermute(there, 'mp', [(i + 1, i) for i in range(0, count - step)])]
    convert_element_type x14 -> x7, other arithmetic: 92.1 us -> 8.07 us  [the longest x1 5.36 us: local(): grad_in = grad_in.astype(BF16)]
    ppermute x0 -> x34, starting transfers between devices: none -> 65.5 us  [the longest x6 25.3 us: step(): lax.ppermute(here, 'mp', [(i, i + 1) for i in range(step - 1, count - 1)])]
  transfers between devices with their start and end apart: 10 -> 38, of which waited for: 6 -> 12; matrix products, arithmetic and copies ran while one was open for 40% -> 11% of each run, Pallas kernels for 0% -> 53%
where the time goes in v1:
time: 665 us; the launch traced here: 658 us
  Pallas kernels  352 us (53%)
  waiting for transfers between devices  133 us (20%)
  other arithmetic  68.8 us (10%)
  starting transfers between devices  65.9 us (10%)
  between operations  22.5 us (3%)
  local copies, waits for them, and re-layouts  15.7 us (2%)
    ppermute x6, waiting for transfers between devices, step(): lax.ppermute(there, 'mp', [(i + 1, i) for i in range(0, count - step)])  81 us
    pallas_call x5, Pallas kernels, wgrad(): pl.pallas_call(functools.partial(wgrad_kernel, len(lefts), len(rights), c...  79.3 us
    pallas_call x2, Pallas kernels, enter(): pl.pallas_call(functools.partial(enter_kernel, many, units), grid_spec=pl...  64 us
    pallas_call x3, Pallas kernels, leave(): pl.pallas_call(functools.partial(leave_kernel, many, units), grid_spec=pl...  46.5 us
    pallas_call x1, Pallas kernels, attn_bwd(): pl.pallas_call(functools.partial(attn_bwd_kernel, cases, width), grid=(he...  44 us
    ppermute x10, waiting for transfers between devices, everywhere(): lax.ppermute(value, axis, [(i, i ^ hop) for i in range(size)])  41.3 us
    pallas_call x1, Pallas kernels, din_all(): pl.pallas_call(din_kernel, grid=(D // tile, group // rows), in_specs=[pl....  40.2 us
    pallas_call x1, Pallas kernels, branch_all(): pl.pallas_call(functools.partial(branch_kernel, units), grid=(D // tile,...  28.3 us
  transfers between devices with their start and end apart: 38, of which 12 were waited for; matrix products, arithmetic and copies ran while one was open for 11% of the time, Pallas kernels for 53%

profile of v1, /device:TPU:0, one launch (start us, length us, event | category | flops | bytes accessed | tf_op | source)
XLA Modules:
  0.0 657.7 jit_solution(11161134164547530601)
XLA Ops:
  7.2 1.8 convert_element_type.93
  9.3 1.4 pad_maximum_fusion
  10.8 1.4 collective-permute-start
  12.2 6.9 %collective-permute-start.1 = (bf16[512,2048]{1,0:T(8,128)(2,1)}, bf16[512,2048]{1,0:T(8,128)(2,1)}, u32[]{:S(2)}, u32[]{:S(2)}) collective-permute-start(bf16[512,2048]{1,0:T(8,128)(2,1)} %refs_0_.1), channel_id=1, source_target_pairs={{0,1},{1,2},{2,3},{4,5},{5,6},{6,7},{8,9},{9,10},{10,11},{12,13},{... | collective-permute-start | bytes 6291464 | tf_op jit(solution)/shard_map/ppermute | solution.py:600
  19.1 42.6 %collective-permute-done.refs_1_ = bf16[512,2048]{1,0:T(8,128)(2,1)S(1)} collective-permute-done((bf16[512,2048]{1,0:T(8,128)(2,1)}, bf16[512,2048]{1,0:T(8,128)(2,1)S(1)}, u32[]{:S(2)}, u32[]{:S(2)}) %collective-permute-start) | collective-permute-done | bytes 2097184 | tf_op jit(solution)/shard_map/ppermute | solution.py:601
  67.0 2.0 collective-permute-start.3
  75.5 2.7 convert_reduce_fusion.1
  78.3 3.7 multiply_sine_fusion
  82.1 2.5 maximum_maximum_fusion.2
  84.6 30.5 %collective-permute-done.2.refs_3_.refs_1_ = bf16[512,2048]{1,0:T(8,128)(2,1)} collective-permute-done((bf16[512,2048]{1,0:T(8,128)(2,1)}, bf16[512,2048]{1,0:T(8,128)(2,1)}, u32[]{:S(2)}, u32[]{:S(2)}) %collective-permute-start.2) | collective-permute-done | bytes 2097184 | tf_op jit(solution)/shard_map/ppermute | solution.py:601
  115.1 2.0 collective-permute-start.4
  117.1 1.5 collective-permute-start.5
  118.6 43.2 %enter.2 = (bf16[2048,2048]{1,0:T(8,128)(2,1)}, bf16[2048,2048]{1,0:T(8,128)(2,1)}, bf16[2048,2048]{1,0:T(8,128)(2,1)}, f32[2048,128]{1,0:T(8,128)}, bf16[2048,2...) custom-call(s32[6,3]{1,0:T(8,128)} %copy.72.table, bf16[512,2048]{1,0:T(8,128)(2,1)} %refs_0_.1, ...), custom_call_target="tpu_custom_call" | custom-call | flops 22548578304 | bytes 14680064 | tf_op jit(solution)/shard_map/enter/pallas_call | solution.py:144
  163.1 10.0 %collective-permute-start.7 = (bf16[512,2048]{1,0:T(8,128)(2,1)S(1)}, bf16[512,2048]{1,0:T(8,128)(2,1)}, u32[]{:S(2)}, u32[]{:S(2)}) collective-permute-start(bf16[512,2048]{1,0:T(8,128)(2,1)S(1)} %get-tuple-element.122.refs_0_), channel_id=1, source_target_pairs={{0,1},{1,2},{2,3},{4,5},{5,6},{6,7},{8,9},{9,10},{10,11},{12,13},{... | collective-permute-start | bytes 6291464 | tf_op jit(solution)/shard_map/ppermute | solution.py:600
  176.3 20.8 %enter.3 = (bf16[2048,2048]{1,0:T(8,128)(2,1)}, bf16[2048,2048]{1,0:T(8,128)(2,1)}, bf16[2048,2048]{1,0:T(8,128)(2,1)}, f32[2048,128]{1,0:T(8,128)}, bf16[2048,2...) custom-call(s32[2,3]{1,0:T(2,128)} %fusion.24.table, ...), custom_call_target="tpu_custom_call", output_to_operand_aliasing={{0}: (12, {}), {1}: (13, {}), {2}: (14, {}), {3}: (15, {}),... | custom-call | flops 7516192768 | bytes 14680064 | tf_op jit(solution)/shard_map/enter/pallas_call | solution.py:144
  197.1 11.4 %attend.2 = (bf16[2048,512]{1,0:T(8,128)(2,1)}, f32[4,1,2048]{2,1,0:T(1,128)}) custom-call(bf16[2048,1536]{1,0:T(8,128)(2,1)} %get-tuple-element.113.q_ref.k_ref.v_ref, bf16[2048,1536]{1,0:T(8,128)(2,1)} %get-tuple-element.113.q_ref.k_ref.v_ref, bf16[2048,1536]{1,0:T(8,128)(2,1)} %get-tuple-element.113.q_ref.k_ref.v_ref, ...), custom_call_target="tpu_custom_call" | custom-call | flops 10737418240 | bytes 4194304 | tf_op jit(solution)/shard_map/attend/pallas_call | solution.py:219
  208.5 4.3 collective-permute-done.6.refs_1_
  215.2 2.4 collective-permute-start.9
  217.6 11.4 %attend.3 = (bf16[2048,512]{1,0:T(8,128)(2,1)}, f32[4,1,2048]{2,1,0:T(1,128)}) custom-call(bf16[2048,1536]{1,0:T(8,128)(2,1)} %get-tuple-element.113.q_ref.k_ref.v_ref, bf16[2048,1536]{1,0:T(8,128)(2,1)} %get-tuple-element.113.q_ref.k_ref.v_ref, ...), custom_call_target="tpu_custom_call", output_to_operand_aliasing={{0}: (4, {}), {1}: (5, {})} | custom-call | flops 10737418240 | bytes 4194304 | tf_op jit(solution)/shard_map/attend/pallas_call | solution.py:219
  229.0 28.3 %branch.1 = bf16[2048,2048]{1,0:T(8,128)(2,1)} custom-call(bf16[2048,512]{1,0:T(8,128)(2,1)} %get-tuple-element.116.o_ref.refs_1_, bf16[2048,2048]{1,0:T(8,128)(2,1)} %get-tuple-element.117.act_ref.refs_0_, bf16[2560,2048]{1,0:T(8,128)(2,1)} %all-gather.5.cloned.1.call-done.w_ref.refs_3_.refs_4_), custom_call_target="tpu_custom_call" | custom-call | flops 21474836480 | bytes 10485760 | tf_op jit(solution)/shard_map/branch/pallas_call | solution.py:333
  257.3 3.6 collective-permute-done.8.refs_0_.refs_1_
  261.0 2.0 collective-permute-start.10
  263.0 1.5 collective-permute-start.11
  264.4 19.7 %leave.3 = (bf16[2048,2048]{1,0:T(8,128)(2,1)}, bf16[2048,2048]{1,0:T(8,128)(2,1)}, bf16[2048,512]{1,0:T(8,128)(2,1)}, f32[8,2048]{1,0:T(8,128)}) custom-call(s32[4,3]{1,0:T(4,128)} %dynamic-slice_bitcast_fusion.table, bf16[512,2048]{1,0:T(8,128)(2,1)} %copy-done.2, bf16[512,2048]{1,0:T(8,128)(2,1)} %collective-permute-done.6.refs_1_, ...), custom_call_target="tpu_custom_call" | custom-call | flops 10737418240 | bytes 10485760 | tf_op jit(solution)/shard_map/leave/pallas_call | solution.py:386
  284.2 13.4 %leave.4 = (bf16[2048,2048]{1,0:T(8,128)(2,1)}, bf16[2048,2048]{1,0:T(8,128)(2,1)}, bf16[2048,512]{1,0:T(8,128)(2,1)}, f32[8,2048]{1,0:T(8,128)}) custom-call(s32[2,3]{1,0:T(2,128)} %fusion.25.table, bf16[512,2048]{1,0:T(8,128)(2,1)} %copy-done, ...), custom_call_target="tpu_custom_call", output_to_operand_aliasing={{0}: (6, {}), {1}: (7, {}), {2}: (8, {})} | custom-call | flops 5368709120 | bytes 10485760 | tf_op jit(solution)/shard_map/leave/pallas_call | solution.py:386
  297.6 15.8 %weight_grad_part.2.refs_3_ = f32[4,2560,256]{2,1,0:T(8,128)} custom-call(s32[5]{0:T(128)} %pad_add_fusion.place, bf16[2048,2048]{1,0:T(8,128)(2,1)} %get-tuple-element.117.act_ref.refs_0_, bf16[2048,512]{1,0:T(8,128)(2,1)} %get-tuple-element.116.o_ref.refs_1_, bf16[2048,2048]{1,0:T(8,128)(2,1)} %get-tuple-element.134.refs_2_.refs_3_.refs_4_.refs_6_, ...), custom_call_target="tpu_custom_call" | custom-call | flops 8053063680 | tf_op jit(solution)/shard_map/weight_grad_part/pallas_call | solution.py:555
  315.5 13.4 %leave.5 = (bf16[2048,2048]{1,0:T(8,128)(2,1)}, bf16[2048,2048]{1,0:T(8,128)(2,1)}, bf16[2048,512]{1,0:T(8,128)(2,1)}, f32[8,2048]{1,0:T(8,128)}) custom-call(s32[2,3]{1,0:T(2,128)} %fusion.24.table, bf16[512,2048]{1,0:T(8,128)(2,1)} %collective-permute-done.11.refs_0_, ...), custom_call_target="tpu_custom_call", output_to_operand_aliasing={{0}: (7, {}), {1}: (8, {}), {2}: (9, {})} | custom-call | flops 5368709120 | bytes 10485760 | tf_op jit(solution)/shard_map/leave/pallas_call | solution.py:386
  328.9 11.0 %weight_grad_part.3 = bf16[4,2560,256]{2,1,0:T(8,128)(2,1)} custom-call(s32[3]{0:T(128)} %pad_add_fusion.3.place, bf16[2048,2048]{1,0:T(8,128)(2,1)} %get-tuple-element.117.act_ref.refs_0_, bf16[2048,512]{1,0:T(8,128)(2,1)} %get-tuple-element.116.o_ref.refs_1_, bf16[2048,2048]{1,0:T(8,128)(2,1)} %get-tuple-element.144.refs_2_, ...), custom_call_target="tpu_custom_call" | custom-call | flops 2684354560 | tf_op jit(solution)/shard_map/weight_grad_part/pallas_call | solution.py:555
  340.6 15.0 %weight_grad.5 = bf16[4,256,2048]{2,1,0:T(8,128)(2,1)} custom-call(s32[2]{0:T(128)} %pad_add_fusion.2.place, bf16[2048,2048]{1,0:T(8,128)(2,1)} %get-tuple-element.146.refs_0_, bf16[2048,2048]{1,0:T(8,128)(2,1)} %get-tuple-element.142.refs_1_.dh_ref), custom_call_target="tpu_custom_call" | custom-call | flops 429496736 | bytes 16777216 | tf_op jit(solution)/shard_map/weight_grad/pallas_call | solution.py:504
  356.6 21.2 %weight_grad.6 = (bf16[1,2560,256]{2,1,0:T(8,128)(2,1)}, bf16[1,2560,256]{2,1,0:T(8,128)(2,1)}, bf16[1,2560,256]{2,1,0:T(8,128)(2,1)}, bf16[1,2560,256]{2,1,0:T(8,128)(2,1)}) custom-call(s32[2]{0:T(128)} %pad_add_fusion.1.place, bf16[2048,2048]{1,0:T(8,128)(2,1)} %get-tuple-element.117.act_ref.refs_0_, bf16[2048,512]{1,0:T(8,128)(2,1)} %get-tuple-element.116.o_ref.refs_1_, ...), custom_call_target="tpu_custom_call" | custom-call | flops 2684354560 | bytes 18874368 | tf_op jit(solution)/shard_map/weight_grad/pallas_call | solution.py:504
  378.9 1.5 collective-permute-start.15
  381.2 44.0 %attend_back.1 = (bf16[2048,1536]{1,0:T(8,128)(2,1)}, f32[8,1536]{1,0:T(8,128)}) custom-call(bf16[2048,1536]{1,0:T(8,128)(2,1)} %get-tuple-element.113.q_ref.k_ref.v_ref, bf16[2048,1536]{1,0:T(8,128)(2,1)} %get-tuple-element.113.q_ref.k_ref.v_ref, bf16[2048,1536]{1,0:T(8,128)(2,1)} %get-tuple-element.113.q_ref.k_ref.v_ref, ...), custom_call_target="tpu_custom_call" | custom-call | flops 6710886400 | bytes 3145728 | tf_op jit(solution)/shard_map/attend_back/pallas_call | solution.py:299
  425.2 17.0 %weight_grad.7 = (bf16[1,256,2048]{2,1,0:T(8,128)(2,1)}, bf16[1,256,2048]{2,1,0:T(8,128)(2,1)}, bf16[1,256,2048]{2,1,0:T(8,128)(2,1)}, bf16[1,256,2048]{2,1,0:T(8,128)(2,1)}) custom-call(s32[2]{0:T(128)} %pad_add_fusion.1.place, bf16[2048,2048]{1,0:T(8,128)(2,1)} %get-tuple-element.146.refs_0_, bf16[2048,2048]{1,0:T(8,128)(2,1)} %get-tuple-element.142.refs_1_.dh_ref, ...), custom_call_target="tpu_custom_call" | custom-call | flops 429496736 | bytes 16777216 | tf_op jit(solution)/shard_map/weight_grad/pallas_call | solution.py:504
  443.3 1.5 collective-permute-start.18
  445.7 40.2 %input_back.1 = (bf16[2048,2048]{1,0:T(8,128)(2,1)}, f32[8,2048]{1,0:T(8,128)}) custom-call(bf16[2048,1536]{1,0:T(8,128)(2,1)} %get-tuple-element.157.dm_ref.refs_1_, bf16[2048,2048]{1,0:T(8,128)(2,1)} %get-tuple-element.142.refs_1_.dh_ref, bf16[2048,3584]{1,0:T(8,128)(2,1)} %all-gather.3.cloned.1.call-done.refs_6_.refs_5_.w_ref, ...), custom_call_target="tpu_custom_call" | custom-call | flops 7516192768 | bytes 3670016 | tf_op jit(solution)/shard_map/input_back/pallas_call | solution.py:431
  486.0 4.1 collective-permute-done.18
  490.1 12.2 %weight_grad.8 = bf16[4,256,1536]{2,1,0:T(8,128)(2,1)} custom-call(s32[2]{0:T(128)} %pad_add_fusion.2.place, bf16[2048,2048]{1,0:T(8,128)(2,1)} %get-tuple-element.164.refs_0_, bf16[2048,1536]{1,0:T(8,128)(2,1)} %get-tuple-element.157.dm_ref.refs_1_), custom_call_target="tpu_custom_call" | custom-call | flops 57982058496 | bytes 14680064 | tf_op jit(solution)/shard_map/weight_grad/pallas_call | solution.py:504
  504.1 2.5 multiply_reduce_fusion.1
  507.2 3.1 convert_add_fusion.2
  511.7 13.9 %weight_grad.9 = (bf16[1,256,1536]{2,1,0:T(8,128)(2,1)}, bf16[1,256,1536]{2,1,0:T(8,128)(2,1)}, bf16[1,256,1536]{2,1,0:T(8,128)(2,1)}, bf16[1,256,1536]{2,1,0:T(8,128)(2,1)}) custom-call(s32[2]{0:T(128)} %pad_add_fusion.1.place, bf16[2048,2048]{1,0:T(8,128)(2,1)} %get-tuple-element.164.refs_0_, bf16[2048,1536]{1,0:T(8,128)(2,1)} %get-tuple-element.157.dm_ref.refs_1_, ...), custom_call_target="tpu_custom_call" | custom-call | flops 57982058496 | bytes 14680064 | tf_op jit(solution)/shard_map/weight_grad/pallas_call | solution.py:504
  526.4 1.5 collective-permute-start.23
  531.8 32.0 %collective-permute-done.26 = f32[124,128]{1,0:T(8,128)S(1)} collective-permute-done((f32[124,128]{1,0:T(8,128)S(1)}, f32[124,128]{1,0:T(8,128)S(1)}, u32[]{:S(2)}, u32[]{:S(2)}) %collective-permute-start.26) | collective-permute-done | bytes 63520 | tf_op jit(solution)/shard_map/ppermute | solution.py:628
  566.4 2.7 multiply_reduce_fusion.2
  571.8 6.2 collective-permute-start.32
  579.4 3.3 collective-permute-done.32
  583.3 6.3 collective-permute-start.33
  590.1 1.6 collective-permute-start.29
  592.4 1.7 collective-permute-done.29
  594.7 2.7 collective-permute-start.30
  597.5 1.9 dynamic-slice_reduce_fusion.1
  600.0 2.0 multiply_reduce_fusion.4
  602.0 3.7 collective-permute-done.31
  607.6 1.4 broadcast_multiply_fusion.1
  609.1 1.4 mul.469
  610.5 1.5 add_subtract_fusion.1
  612.0 1.5 add_subtract_fusion.2
  613.5 2.7 multiply_subtract_fusion.3
  616.2 1.6 add_subtract_fusion
  617.9 5.5 multiply_subtract_fusion
  624.5 5.8 multiply_subtract_fusion.1
  630.3 5.2 multiply_subtract_fusion.2
  635.5 5.4 reduce-scatter.5.cloned.1.call-done
  641.0 3.4 convert_reduce_fusion
  644.4 5.4 fusion.7
  (176 shorter events, 41.3 us)
Async XLA Ops:
  7.2 111.4 %all-gather.3.cloned.1.call-start = ((), (), s32[]{:S(2)}) async-start(), calls=%async_computation.2 | async-start | bytes 16515072 | tf_op jit(solution)/shard_map/all_gather | solution.py:685
  9.3 53.7 %copy-start.4 = (f32[2048,256]{1,0:T(8,128)S(1)}, f32[2048,256]{1,0:T(8,128)}, u32[]{:S(2)}) copy-start(f32[2048,256]{1,0:T(8,128)} %param.36) | copy-start | bytes 6291460
  10.7 52.4 %copy-start.19 = (f32[512,256]{1,0:T(8,128)S(1)}, f32[512,256]{1,0:T(8,128)}, u32[]{:S(2)}) copy-start(f32[512,256]{1,0:T(8,128)} %param.34) | copy-start | bytes 1572868
  10.7 218.3 %all-gather.5.cloned.1.call-start = ((), (), s32[]{:S(2)}) async-start(), calls=%async_computation.3 | async-start | bytes 11796480 | tf_op jit(solution)/shard_map/all_gather | solution.py:688
  10.8 50.9 %collective-permute-start = (bf16[512,2048]{1,0:T(8,128)(2,1)}, bf16[512,2048]{1,0:T(8,128)(2,1)S(1)}, u32[]{:S(2)}, u32[]{:S(2)}) collective-permute-start(bf16[512,2048]{1,0:T(8,128)(2,1)} %refs_0_.1), channel_id=1, source_target_pairs={{1,0},{2,1},{3,2},{5,4},{6,5},{7,6},{9,8},{10,9},{11,10},{13,12},{... | collective-permute-start | bytes 6291464 | tf_op jit(solution)/shard_map/ppermute | solution.py:601
  12.2 50.8 %collective-permute-start.1 = (bf16[512,2048]{1,0:T(8,128)(2,1)}, bf16[512,2048]{1,0:T(8,128)(2,1)}, u32[]{:S(2)}, u32[]{:S(2)}) collective-permute-start(bf16[512,2048]{1,0:T(8,128)(2,1)} %refs_0_.1), channel_id=1, source_target_pairs={{0,1},{1,2},{2,3},{4,5},{5,6},{6,7},{8,9},{9,10},{10,11},{12,13},{... | collective-permute-start | bytes 6291464 | tf_op jit(solution)/shard_map/ppermute | solution.py:600
  63.2 7.3 %copy-start.26 = (f32[1536]{0:T(1024)S(1)}, f32[1536]{0:T(1024)}, u32[]{:S(2)}) copy-start(f32[1536]{0:T(1024)} %param.38) | copy-start | bytes 18436
  64.3 425.8 %reduce-scatter.3.cloned.1.call-start = ((), (), s32[]{:S(2)}) async-start(), calls=%async_computation.4 | async-start | bytes 10485760 | tf_op jit(solution)/shard_map/reduce_scatter | solution.py:732
  65.7 49.4 %collective-permute-start.2 = (bf16[512,2048]{1,0:T(8,128)(2,1)}, bf16[512,2048]{1,0:T(8,128)(2,1)}, u32[]{:S(2)}, u32[]{:S(2)}) collective-permute-start(bf16[512,2048]{1,0:T(8,128)(2,1)} %copy-done.34), channel_id=1, source_target_pairs={{1,0},{2,1},{5,4},{6,5},{9,8},{10,9},{13,12},{14,13},{17,16},{18,1... | collective-permute-start | bytes 6291464 | tf_op jit(solution)/shard_map/ppermute | solution.py:601
  67.0 48.1 %collective-permute-start.3 = (bf16[512,2048]{1,0:T(8,128)(2,1)}, bf16[512,2048]{1,0:T(8,128)(2,1)}, u32[]{:S(2)}, u32[]{:S(2)}) collective-permute-start(bf16[512,2048]{1,0:T(8,128)(2,1)} %collective-permute-done.1.refs_2_), channel_id=1, source_target_pairs={{1,2},{2,3},{5,6},{6,7},{9,10},{10,11},{13,14},{14,15},{17,18},{18... | collective-permute-start | bytes 6291464 | tf_op jit(solution)/shard_map/ppermute | solution.py:600
  78.3 84.9 %copy-start.2 = (bf16[512,2048]{1,0:T(8,128)(2,1)}, bf16[512,2048]{1,0:T(8,128)(2,1)S(1)}, u32[]{:S(2)}) copy-start(bf16[512,2048]{1,0:T(8,128)(2,1)S(1)} %get-tuple-element.122.refs_0_) | copy-start | bytes 6291460
  115.1 61.2 %collective-permute-start.4 = (bf16[512,2048]{1,0:T(8,128)(2,1)}, bf16[512,2048]{1,0:T(8,128)(2,1)}, u32[]{:S(2)}, u32[]{:S(2)}) collective-permute-start(bf16[512,2048]{1,0:T(8,128)(2,1)} %collective-permute-done.3.refs_4_.refs_2_), channel_id=1, source_target_pairs={{2,3},{6,7},{10,11},{14,15},{18,19},{22,23},{26,27},{30,31}} | collective-permute-start | bytes 6291464 | tf_op jit(solution)/shard_map/ppermute | solution.py:600
  117.1 59.2 %collective-permute-start.5 = (bf16[512,2048]{1,0:T(8,128)(2,1)}, bf16[512,2048]{1,0:T(8,128)(2,1)}, u32[]{:S(2)}, u32[]{:S(2)}) collective-permute-start(bf16[512,2048]{1,0:T(8,128)(2,1)} %collective-permute-done.2.refs_3_.refs_1_), channel_id=1, source_target_pairs={{1,0},{5,4},{9,8},{13,12},{17,16},{21,20},{25,24},{29,28}} | collective-permute-start | bytes 6291464 | tf_op jit(solution)/shard_map/ppermute | solution.py:601
  161.8 51.0 %collective-permute-start.6 = (bf16[512,2048]{1,0:T(8,128)(2,1)S(1)}, bf16[512,2048]{1,0:T(8,128)(2,1)}, u32[]{:S(2)}, u32[]{:S(2)}) collective-permute-start(bf16[512,2048]{1,0:T(8,128)(2,1)S(1)} %get-tuple-element.122.refs_0_), channel_id=1, source_target_pairs={{1,0},{2,1},{3,2},{5,4},{6,5},{7,6},{9,8},{10,9},{11,10},{13,12},{... | collective-permute-start | bytes 6291464 | tf_op jit(solution)/shard_map/ppermute | solution.py:601
  163.1 50.8 %collective-permute-start.7 = (bf16[512,2048]{1,0:T(8,128)(2,1)S(1)}, bf16[512,2048]{1,0:T(8,128)(2,1)}, u32[]{:S(2)}, u32[]{:S(2)}) collective-permute-start(bf16[512,2048]{1,0:T(8,128)(2,1)S(1)} %get-tuple-element.122.refs_0_), channel_id=1, source_target_pairs={{0,1},{1,2},{2,3},{4,5},{5,6},{6,7},{8,9},{9,10},{10,11},{12,13},{... | collective-permute-start | bytes 6291464 | tf_op jit(solution)/shard_map/ppermute | solution.py:600
  213.9 47.1 %collective-permute-start.8 = (bf16[512,2048]{1,0:T(8,128)(2,1)}, bf16[512,2048]{1,0:T(8,128)(2,1)S(1)}, u32[]{:S(2)}, u32[]{:S(2)}) collective-permute-start(bf16[512,2048]{1,0:T(8,128)(2,1)} %collective-permute-done.6.refs_1_), channel_id=1, source_target_pairs={{1,0},{2,1},{5,4},{6,5},{9,8},{10,9},{13,12},{14,13},{17,16},{18,1... | collective-permute-start | bytes 6291464 | tf_op jit(solution)/shard_map/ppermute | solution.py:601
  215.2 45.8 %collective-permute-start.9 = (bf16[512,2048]{1,0:T(8,128)(2,1)}, bf16[512,2048]{1,0:T(8,128)(2,1)}, u32[]{:S(2)}, u32[]{:S(2)}) collective-permute-start(bf16[512,2048]{1,0:T(8,128)(2,1)} %collective-permute-done.7.refs_2_), channel_id=1, source_target_pairs={{1,2},{2,3},{5,6},{6,7},{9,10},{10,11},{13,14},{14,15},{17,18},{18... | collective-permute-start | bytes 6291464 | tf_op jit(solution)/shard_map/ppermute | solution.py:600
  261.0 23.2 %copy-start = (bf16[512,2048]{1,0:T(8,128)(2,1)}, bf16[512,2048]{1,0:T(8,128)(2,1)S(1)}, u32[]{:S(2)}) copy-start(bf16[512,2048]{1,0:T(8,128)(2,1)S(1)} %collective-permute-done.8.refs_0_.refs_1_) | copy-start | bytes 6291460
  261.0 52.4 %collective-permute-start.10 = (bf16[512,2048]{1,0:T(8,128)(2,1)}, bf16[512,2048]{1,0:T(8,128)(2,1)}, u32[]{:S(2)}, u32[]{:S(2)}) collective-permute-start(bf16[512,2048]{1,0:T(8,128)(2,1)} %collective-permute-done.9.refs_2_), channel_id=1, source_target_pairs={{2,3},{6,7},{10,11},{14,15},{18,19},{22,23},{26,27},{30,31}} | collective-permute-start | bytes 6291464 | tf_op jit(solution)/shard_map/ppermute | solution.py:600
  263.0 50.4 %collective-permute-start.11 = (bf16[512,2048]{1,0:T(8,128)(2,1)S(1)}, bf16[512,2048]{1,0:T(8,128)(2,1)}, u32[]{:S(2)}, u32[]{:S(2)}) collective-permute-start(bf16[512,2048]{1,0:T(8,128)(2,1)S(1)} %collective-permute-done.8.refs_0_.refs_1_), channel_id=1, source_target_pairs={{1,0},{5,4},{9,8},{13,12},{17,16},{21,20},{25,24},{29,28}} | collective-permute-start | bytes 6291464 | tf_op jit(solution)/shard_map/ppermute | solution.py:601
  313.4 327.5 %reduce-scatter.5.cloned.1.call-start = ((), (), s32[]{:S(2)}) async-start(), calls=%async_computation.5 | async-start | bytes 10485760 | tf_op jit(solution)/shard_map/reduce_scatter | solution.py:762
  339.9 16.7 %collective-permute-start.12 = (bf16[4,2560,256]{2,1,0:T(8,128)(2,1)}, bf16[4,2560,256]{2,1,0:T(8,128)(2,1)}, u32[]{:S(2)}, u32[]{:S(2)}) collective-permute-start(bf16[4,2560,256]{2,1,0:T(8,128)(2,1)} %weight_grad_part.3), channel_id=1, source_target_pairs={{0,4},{4,0},{1,5},{5,1},{2,6},{6,2},{3,7},{7,3},{8,12},{12,8},{9,1... | collective-permute-start | bytes 15728648 | tf_op jit(solution)/shard_map/ppermute | solution.py:752
  355.5 69.7 %collective-permute-start.13 = (bf16[4,256,2048]{2,1,0:T(8,128)(2,1)}, bf16[4,256,2048]{2,1,0:T(8,128)(2,1)}, u32[]{:S(2)}, u32[]{:S(2)}) collective-permute-start(bf16[4,256,2048]{2,1,0:T(8,128)(2,1)} %weight_grad.5), channel_id=1, source_target_pairs={{0,4},{4,0},{1,5},{5,1},{2,6},{6,2},{3,7},{7,3},{8,12},{12,8},{9,1... | collective-permute-start | bytes 12582920 | tf_op jit(solution)/shard_map/ppermute | solution.py:736
  377.8 67.1 %collective-permute-start.14 = (bf16[1,2560,256]{2,1,0:T(8,128)(2,1)}, bf16[1,2560,256]{2,1,0:T(8,128)(2,1)}, u32[]{:S(2)}, u32[]{:S(2)}) collective-permute-start(bf16[1,2560,256]{2,1,0:T(8,128)(2,1)} %get-tuple-element.154), channel_id=1, source_target_pairs={{0,8},{8,0},{16,24},{24,16},{1,9},{9,1},{17,25},{25,17},{2,10},{10... | collective-permute-start | bytes 3932168 | tf_op jit(solution)/shard_map/ppermute | solution.py:741
  378.9 66.9 %collective-permute-start.15 = (bf16[1,2560,256]{2,1,0:T(8,128)(2,1)}, bf16[1,2560,256]{2,1,0:T(8,128)(2,1)}, u32[]{:S(2)}, u32[]{:S(2)}) collective-permute-start(bf16[1,2560,256]{2,1,0:T(8,128)(2,1)} %get-tuple-element.155), channel_id=1, source_target_pairs={{0,16},{8,24},{16,0},{24,8},{1,17},{9,25},{17,1},{25,9},{2,18},{10... | collective-permute-start | bytes 3932168 | tf_op jit(solution)/shard_map/ppermute | solution.py:741
  380.4 65.4 %collective-permute-start.16 = (bf16[1,2560,256]{2,1,0:T(8,128)(2,1)}, bf16[1,2560,256]{2,1,0:T(8,128)(2,1)}, u32[]{:S(2)}, u32[]{:S(2)}) collective-permute-start(bf16[1,2560,256]{2,1,0:T(8,128)(2,1)} %get-tuple-element.156), channel_id=1, source_target_pairs={{0,24},{8,16},{16,8},{24,0},{1,25},{9,17},{17,9},{25,1},{2,26},{10... | collective-permute-start | bytes 3932168 | tf_op jit(solution)/shard_map/ppermute | solution.py:741
  442.2 43.7 %collective-permute-start.17 = (bf16[1,256,2048]{2,1,0:T(8,128)(2,1)}, bf16[1,256,2048]{2,1,0:T(8,128)(2,1)S(1)}, u32[]{:S(2)}, u32[]{:S(2)}) collective-permute-start(bf16[1,256,2048]{2,1,0:T(8,128)(2,1)} %get-tuple-element.160), channel_id=1, source_target_pairs={{0,8},{8,0},{16,24},{24,16},{1,9},{9,1},{17,25},{25,17},{2,10},{10... | collective-permute-start | bytes 3145736 | tf_op jit(solution)/shard_map/ppermute | solution.py:741
  443.3 46.8 %collective-permute-start.18 = (bf16[1,256,2048]{2,1,0:T(8,128)(2,1)}, bf16[1,256,2048]{2,1,0:T(8,128)(2,1)S(1)}, u32[]{:S(2)}, u32[]{:S(2)}) collective-permute-start(bf16[1,256,2048]{2,1,0:T(8,128)(2,1)} %get-tuple-element.161), channel_id=1, source_target_pairs={{0,16},{8,24},{16,0},{24,8},{1,17},{9,25},{17,1},{25,9},{2,18},{10... | collective-permute-start | bytes 3145736 | tf_op jit(solution)/shard_map/ppermute | solution.py:741
  444.9 45.2 %collective-permute-start.19 = (bf16[1,256,2048]{2,1,0:T(8,128)(2,1)}, bf16[1,256,2048]{2,1,0:T(8,128)(2,1)}, u32[]{:S(2)}, u32[]{:S(2)}) collective-permute-start(bf16[1,256,2048]{2,1,0:T(8,128)(2,1)} %get-tuple-element.162), channel_id=1, source_target_pairs={{0,24},{8,16},{16,8},{24,0},{1,25},{9,17},{17,9},{25,1},{2,26},{10... | collective-permute-start | bytes 3145736 | tf_op jit(solution)/shard_map/ppermute | solution.py:741
  486.0 18.0 %copy-start.12 = (bf16[1,256,2048]{2,1,0:T(8,128)(2,1)}, bf16[1,256,2048]{2,1,0:T(8,128)(2,1)S(1)}, u32[]{:S(2)}) copy-start(bf16[1,256,2048]{2,1,0:T(8,128)(2,1)S(1)} %collective-permute-done.17) | copy-start | bytes 3145732
  490.1 14.0 %copy-start.14 = (bf16[1,256,2048]{2,1,0:T(8,128)(2,1)}, bf16[1,256,2048]{2,1,0:T(8,128)(2,1)S(1)}, u32[]{:S(2)}) copy-start(bf16[1,256,2048]{2,1,0:T(8,128)(2,1)S(1)} %collective-permute-done.18) | copy-start | bytes 3145732
  490.1 14.0 %copy-start.10 = (bf16[1,256,2048]{2,1,0:T(8,128)(2,1)S(1)}, bf16[1,256,2048]{2,1,0:T(8,128)(2,1)}, u32[]{:S(2)}) copy-start(bf16[1,256,2048]{2,1,0:T(8,128)(2,1)} %get-tuple-element.153) | copy-start | bytes 3145732
  502.3 9.4 %collective-permute-start.21 = (bf16[4,256,1536]{2,1,0:T(8,128)(2,1)}, bf16[4,256,1536]{2,1,0:T(8,128)(2,1)}, u32[]{:S(2)}, u32[]{:S(2)}) collective-permute-start(bf16[4,256,1536]{2,1,0:T(8,128)(2,1)} %weight_grad.8), channel_id=1, source_target_pairs={{0,4},{4,0},{1,5},{5,1},{2,6},{6,2},{3,7},{7,3},{8,12},{12,8},{9,1... | collective-permute-start | bytes 9437192 | tf_op jit(solution)/shard_map/ppermute | solution.py:736
  506.7 3.7 collective-permute-start.20
  510.4 19.9 %collective-permute-start.25 = (f32[124,128]{1,0:T(8,128)S(1)}, f32[124,128]{1,0:T(8,128)S(1)}, u32[]{:S(2)}, u32[]{:S(2)}) collective-permute-start(f32[124,128]{1,0:T(8,128)S(1)} %fusion.26), channel_id=1, source_target_pairs={{0,8},{8,0},{16,24},{24,16},{1,9},{9,1},{17,25},{25,17},{2,10},{10... | collective-permute-start | bytes 190472 | tf_op jit(solution)/shard_map/ppermute | solution.py:628
  525.6 40.7 %copy-start.16 = (bf16[1,256,1536]{2,1,0:T(8,128)(2,1)S(1)}, bf16[1,256,1536]{2,1,0:T(8,128)(2,1)}, u32[]{:S(2)}) copy-start(bf16[1,256,1536]{2,1,0:T(8,128)(2,1)} %get-tuple-element.170) | copy-start | bytes 2359300
  525.6 40.7 %collective-permute-start.22 = (bf16[1,256,1536]{2,1,0:T(8,128)(2,1)}, bf16[1,256,1536]{2,1,0:T(8,128)(2,1)}, u32[]{:S(2)}, u32[]{:S(2)}) collective-permute-start(bf16[1,256,1536]{2,1,0:T(8,128)(2,1)} %get-tuple-element.171), channel_id=1, source_target_pairs={{0,8},{8,0},{16,24},{24,16},{1,9},{9,1},{17,25},{25,17},{2,10},{10... | collective-permute-start | bytes 2359304 | tf_op jit(solution)/shard_map/ppermute | solution.py:741
  526.4 39.9 %collective-permute-start.23 = (bf16[1,256,1536]{2,1,0:T(8,128)(2,1)}, bf16[1,256,1536]{2,1,0:T(8,128)(2,1)}, u32[]{:S(2)}, u32[]{:S(2)}) collective-permute-start(bf16[1,256,1536]{2,1,0:T(8,128)(2,1)} %get-tuple-element.172), channel_id=1, source_target_pairs={{0,16},{8,24},{16,0},{24,8},{1,17},{9,25},{17,1},{25,9},{2,18},{10... | collective-permute-start | bytes 2359304 | tf_op jit(solution)/shard_map/ppermute | solution.py:741
  527.9 38.5 %collective-permute-start.24 = (bf16[1,256,1536]{2,1,0:T(8,128)(2,1)}, bf16[1,256,1536]{2,1,0:T(8,128)(2,1)}, u32[]{:S(2)}, u32[]{:S(2)}) collective-permute-start(bf16[1,256,1536]{2,1,0:T(8,128)(2,1)} %get-tuple-element.173), channel_id=1, source_target_pairs={{0,24},{8,16},{16,8},{24,0},{1,25},{9,17},{17,9},{25,1},{2,26},{10... | collective-permute-start | bytes 2359304 | tf_op jit(solution)/shard_map/ppermute | solution.py:741
  530.4 61.4 %copy-start.23 = (f32[6,2048]{1,0:T(8,128)S(1)}, f32[6,2048]{1,0:T(8,128)}, u32[]{:S(2)}) copy-start(f32[6,2048]{1,0:T(8,128)} %vec_ref.1) | copy-start | bytes 147460
  530.4 33.4 %collective-permute-start.26 = (f32[124,128]{1,0:T(8,128)S(1)}, f32[124,128]{1,0:T(8,128)S(1)}, u32[]{:S(2)}, u32[]{:S(2)}) collective-permute-start(f32[124,128]{1,0:T(8,128)S(1)} %fusion.43), channel_id=1, source_target_pairs={{0,16},{8,24},{16,0},{24,8},{1,17},{9,25},{17,1},{25,9},{2,18},{10... | collective-permute-start | bytes 190472 | tf_op jit(solution)/shard_map/ppermute | solution.py:628
  566.4 44.1 %copy-start.24 = (f32[2048]{0:T(1024)S(1)}, f32[2048]{0:T(1024)}, u32[]{:S(2)}) copy-start(f32[2048]{0:T(1024)} %param.39) | copy-start | bytes 24580
  566.4 45.6 %copy-start.27 = (f32[1536]{0:T(1024)S(1)}, f32[1536]{0:T(1024)}, u32[]{:S(2)}) copy-start(f32[1536]{0:T(1024)} %param.38) | copy-start | bytes 18436
  571.7 6.3 collective-permute-start.27
  571.8 10.8 %collective-permute-start.32 = (f32[96,128]{1,0:T(8,128)S(1)}, f32[96,128]{1,0:T(8,128)S(1)}, u32[]{:S(2)}, u32[]{:S(2)}) collective-permute-start(f32[96,128]{1,0:T(8,128)S(1)} %slice.92), channel_id=1, source_target_pairs={{0,1},{1,0},{2,3},{3,2},{4,5},{5,4},{6,7},{7,6},{8,9},{9,8},{10,11... | collective-permute-start | bytes 147464 | tf_op jit(solution)/shard_map/ppermute | solution.py:628
  578.0 11.5 %collective-permute-start.28 = (f32[8,128]{1,0:T(8,128)S(1)}, f32[8,128]{1,0:T(8,128)S(1)}, u32[]{:S(2)}, u32[]{:S(2)}) collective-permute-start(f32[8,128]{1,0:T(8,128)S(1)} %broadcast_add_fusion), channel_id=1, source_target_pairs={{0,8},{8,0},{16,24},{24,16},{1,9},{9,1},{17,25},{25,17},{2,10},{10... | collective-permute-start | bytes 12296 | tf_op jit(solution)/shard_map/ppermute | solution.py:628
  583.3 16.7 %collective-permute-start.33 = (f32[96,128]{1,0:T(8,128)}, f32[96,128]{1,0:T(8,128)}, u32[]{:S(2)}, u32[]{:S(2)}) collective-permute-start(f32[96,128]{1,0:T(8,128)} %slice_add_fusion.2), channel_id=1, source_target_pairs={{0,2},{1,3},{2,0},{3,1},{4,6},{5,7},{6,4},{7,5},{8,10},{9,11},{10,... | collective-permute-start | bytes 147464 | tf_op jit(solution)/shard_map/ppermute | solution.py:628
  590.1 3.9 collective-permute-start.29
  594.7 5.2 collective-permute-start.30
  600.0 5.8 collective-permute-start.31
  610.5 7.3 %copy-start.20 = (f32[2048,256]{1,0:T(8,128)S(1)}, f32[2048,256]{1,0:T(8,128)}, u32[]{:S(2)}) copy-start(f32[2048,256]{1,0:T(8,128)} %param.43) | copy-start | bytes 6291460
  612.0 5.8 copy-start.5
  617.8 5.6 copy-start.1
  617.8 5.6 copy-start.11
  617.9 5.6 copy-start.13
  617.9 5.6 copy-start.15
  617.9 5.6 copy-start.17
  617.9 6.6 %copy-start.18 = (f32[256,2048]{1,0:T(8,128)S(1)}, f32[256,2048]{1,0:T(8,128)}, u32[]{:S(2)}) copy-start(f32[256,2048]{1,0:T(8,128)} %param.49) | copy-start | bytes 6291460
  624.5 5.8 copy-start.9
  624.5 5.8 copy-start.21
  624.5 5.8 copy-start.22
  630.3 10.6 %copy-start.6 = (bf16[512,2048]{1,0:T(8,128)(2,1)S(1)}, bf16[512,2048]{1,0:T(8,128)(2,1)}, u32[]{:S(2)}) copy-start(bf16[512,2048]{1,0:T(8,128)(2,1)} %refs_0_.1) | copy-start | bytes 6291460
  630.3 10.6 %copy-start.30 = (f32[512]{0:T(512)S(1)}, f32[512]{0:T(512)}, u32[]{:S(2)}) copy-start(f32[512]{0:T(512)} %get-tuple-element.176) | copy-start | bytes 6148
  630.3 10.6 %copy-start.31 = (f32[512]{0:T(512)S(1)}, f32[512]{0:T(512)}, u32[]{:S(2)}) copy-start(f32[512]{0:T(512)} %get-tuple-element.177) | copy-start | bytes 6148
  (9 other events, 24.2 us)
Sparse Core Ops, SparseCore 0:
  10.8 83.6 all-gather.2
  97.0 65.2 all-gather.4
  313.5 151.7 reduce-scatter.2
  486.1 154.7 reduce-scatter.4

commit v2 on v1

--- a/solution.py
+++ b/solution.py
@@ -317,7 +317,7 @@
         out_shape=[shape((group, heads * 3 * HD), BF16), shape((8, heads * 3 * HD), F32)],
         scratch_shapes=[pltpu.VMEM((group, HD), F32), pltpu.VMEM((group, HD), F32)],
         compiler_params=params(56),
-        cost_estimate=cost(flops / 2, 3 * group * heads * HD),
+        cost_estimate=cost(flops / 100, 0),
         name="attend_back",
     )(qkv, qkv, qkv, dctx, begin, lse, *tables)
 
@@ -445,37 +445,88 @@
         ],
         out_shape=[shape((group, D), BF16), shape((8, D), F32)],
         compiler_params=params(60),
-        cost_estimate=cost(group * D * (heads3 + units) / 2, D * (heads3 + units) / 2),
+        cost_estimate=cost(group * D * (heads3 + units) / 50, 0),
         name="input_back",
     )(dmixed, dhid, w_in, x, stat, norm_vec)
 
 
-def wgrad_kernel(n_left, n_right, cut_left, many, place, *refs):
+def finish_kernel(place, g_ref, e_ref, x_ref, stat_ref, out_ref):
+    grad = g_ref[...].astype(F32)
+    rstd = stat_ref[:, 1:2]
+    xhat = (x_ref[...].astype(F32) - stat_ref[:, 0:1]) * rstd
+    mean = jnp.mean(grad, axis=1, keepdims=True)
+    along = jnp.mean(grad * xhat, axis=1, keepdims=True)
+    out_ref[...] = (e_ref[...].astype(F32) + rstd * (grad - mean - xhat * along)).astype(BF16)
+
+
+def finish(place, grad, back, x, stat):
+    rows = grad.shape[0]
+    tile = min(256, rows)
+    steps = rows // tile
+    row = pl.BlockSpec((tile, D), lambda i, p: (i, 0))
+    return pl.pallas_call(
+        finish_kernel,
+        grid_spec=pltpu.PrefetchScalarGridSpec(
+            num_scalar_prefetch=1,
+            grid=(steps,),
+            in_specs=[row, row, row, pl.BlockSpec((tile, 128), lambda i, p: (p[0] * steps + i, 0))],
+            out_specs=row,
+        ),
+        out_shape=shape((rows, D), BF16),
+        compiler_params=params(32),
+        cost_estimate=cost(20 * rows * D, 8 * rows * D),
+        name="finish",
+    )(place, grad, back, x, stat)
+
+
+def halves(quads):
+    bits = list(range(quads.bit_length() - 1))
+    plans = []
+    for order in (bits, bits[::-1]):
+        first = [i for i in range(quads) if i >> order[0] & 1]
+        plans.append((order, first, [i for i in range(quads) if i not in first]))
+    return plans
+
+
+def wgrad_kernel(n_left, n_right, cut_left, quads, place, *refs):
     lefts, rights = refs[:n_left], refs[n_left : n_left + n_right]
     rest = refs[n_left + n_right :]
-    got, outs = (rest[0], rest[1:]) if len(rest) > many else (None, rest)
     pairs = list(zip(lefts, rights)) if cut_left else [(v, rights[0]) for v in lefts]
-    values = [mm(a[...], b[...], TN) for a, b in pairs]
-    axis = 1 if cut_left else 0
-
-    def put(ref):
-        at = 0
-        for value in values:
-            span = slice(at, at + value.shape[axis])
-            at += value.shape[axis]
-            view = (0, slice(None), span) if cut_left else (0, span, slice(None))
-            if got is not None:
-                value = value + got[view].astype(F32)
-            ref[view] = value.astype(BF16)
-
-    if many == 1:
-        put(outs[0])
-    else:
-        for i in range(many):
-
-            @pl.when(pl.program_id(0) == i)
-            def _(i=i):
-                put(outs[i])
+    pieces, at = [], 0
+    for a, b in pairs:
+        value = mm(a[...], b[...], TN)
+        if cut_left:
+            pieces.append(((0, value.shape[0]), slice(at, at + value.shape[1]), value))
+            at += value.shape[1]
+        else:
+            pieces.append(((at, at + value.shape[0]), slice(None), value))
+            at += value.shape[0]
+
+    if len(rest) == 1:
+        for (low, high), cols, value in pieces:
+            rest[0][0, low:high, cols] = value.astype(BF16)
+        return
+    got, outs = rest[0], rest[1:]
+    size = got.shape[1] // 2
+
+    def put(ref, which, half):
+        for (low, high), cols, value in pieces:
+            start, stop = max(low, half * size), min(high, (half + 1) * size)
+            if start < stop:
+                part = value[start - low : stop - low] + got[0, start:stop, cols].astype(F32)
+                ref[which, start - half * size : stop - half * size, cols] = part.astype(BF16)
+
+    for i in range(quads):
+
+        @pl.when(pl.program_id(0) == i)
+        def _(i=i):
+            at = 0
+            for half, (_, first, others) in enumerate(halves(quads)):
+                if i in first:
+                    put(outs[at], first.index(i), half)
+                else:
+                    put(outs[at + 1 + others.index(i)], 0, half)
+                at += 1 + len(others)
 
 
 def wgrad(lefts, rights, cut_left, weight, place, quads, got):
@@ -496,21 +547,58 @@
     else:
         in_specs.append(stacked)
         args.append(got)
-        out_specs = [
-            pl.BlockSpec((1, *tile), lambda i, p: (0, 0, 0), pipeline_mode=pl.Buffered(1))
-        ] * quads
-        out_shape = [shape((1, *tile), BF16)] * quads
+        out_specs, out_shape = [], []
+        for _, first, others in halves(quads):
+            for count in [len(first)] + [1] * len(others):
+                dims = (count, tile[0] // 2, tile[1])
+                out_specs.append(
+                    pl.BlockSpec(dims, lambda i, p: (0, 0, 0), pipeline_mode=pl.Buffered(1))
+                )
+                out_shape.append(shape(dims, BF16))
     flops = rows * tile[0] * tile[1] * 2 * quads * weight
     return pl.pallas_call(
-        functools.partial(wgrad_kernel, len(lefts), len(rights), cut_left, len(out_specs)),
+        functools.partial(wgrad_kernel, len(lefts), len(rights), cut_left, quads),
         grid_spec=pltpu.PrefetchScalarGridSpec(
             num_scalar_prefetch=1, grid=(quads,), in_specs=in_specs, out_specs=out_specs
         ),
         out_shape=out_shape,
         compiler_params=params(60),
-        cost_estimate=cost(flops, 2 * rows * sum(widths[0] + widths[1])),
+        cost_estimate=cost(flops, 0),
         name="weight_grad",
     )(*args)
+
+
+class Spread:
+    def __init__(self, outs, quads):
+        self.mark, self.quads, self.lanes, self.got, at = outs[0], quads, [], [], 0
+        for order, first, others in halves(quads):
+            held = {i: [(outs[at + 1 + k], None, 0)] for k, i in enumerate(others)}
+            self.lanes.append((order, held))
+            self.hand(held, order[0], first, outs[at])
+            at += 1 + len(others)
+
+    def hand(self, held, bit, blocks, stack):
+        got = lax.ppermute(stack, "quad", [(i, i ^ 1 << bit) for i in range(self.quads)])
+        for k, i in enumerate(blocks):
+            held[i ^ 1 << bit].append((None, len(self.got), k))
+        self.got.append(got)
+
+    def add(self, terms):
+        values = [own if at is None else self.got[at][k : k + 1] for own, at, k in terms]
+        return sum(v.astype(F32) for v in values)
+
+    def rest(self, *earlier):
+        for turn_at in range(1, len(self.lanes[0][0])):
+            self.got = after(self.got, *earlier)
+            for order, held in self.lanes:
+                blocks = [i for i in held if i >> order[turn_at] & 1]
+                sums = [self.add(held.pop(i)).astype(BF16) for i in blocks]
+                stack = sums[0] if len(sums) == 1 else jnp.concatenate(sums, axis=0)
+                self.hand(held, order[turn_at], blocks, stack)
+        return self
+
+    def total(self):
+        return jnp.concatenate([self.add(held[0])[0] for _, held in self.lanes], axis=0)
 
 
 def part_kernel(n_left, turns, size, place, *refs):
@@ -621,13 +709,13 @@
         return lookup(tables, self.place), arrays
 
 
-def everywhere(value, axes):
-    for axis, size in axes:
-        hop = 1
-        while hop < size:
-            value = value + lax.ppermute(value, axis, [(i, i ^ hop) for i in range(size)])
-            hop *= 2
-    return value
+def everywhere(value, axis, size):
+    values = [value] + [
+        lax.ppermute(value, axis, [(i, i ^ hop) for i in range(size)]) for hop in range(1, size)
+    ]
+    while len(values) > 1:
+        values = [values[i] + values[i + 1] for i in range(0, len(values), 2)]
+    return values[0]
 
 
 def adam_step(weight, grad, first, second, rate, decay):
@@ -679,8 +767,10 @@
 
     sub = min(256, rows)
     back_own = cotangent * live_own[:, None]
-    x_line = Gather([tokens], count, place)
-    x_line.step(0)
+    many = rows // sub
+    x_line = Gather([tokens[i * sub : (i + 1) * sub] for i in range(many)], count, place)
+    for piece in range(many):
+        x_line.step(piece)
     full_in = jnp.concatenate([w_up.astype(BF16), w_qkv.astype(BF16)], axis=1)
     full_in = lax.all_gather(full_in, dp, axis=0, tiled=True)
     late_down, late_out = after((w_down, w_out), x_line.last()[0])
@@ -688,15 +778,22 @@
     full_back = lax.all_gather(full_back, dp, axis=1, tiled=True)
     b_up_row, b_qkv_row = b_up.reshape(1, -1), b_qkv.reshape(1, -1)
 
-    for step in range(2, count):
-        x_line.step(0)
+    for step in range(2, count - 1):
+        for piece in range(many):
+            x_line.step(piece)
+    x_line.step(0)
     enter_rest = (norm_vec, full_in, b_up_row, b_qkv_row, tables)
-    table, sources = x_line.turns(0, count - 2, sub)
-    state = enter(sub, table, sources, *enter_rest, None)
-    e_line = Gather([after(back_own, state[0])], count, place)
+    table, sources = x_line.turns(0, 1, sub)
+    ready = (x_line.right[0][count - 2], x_line.left[0][count - 2])
+    state = enter(sub, after(table, ready), sources, *enter_rest, None)
+    for piece in range(1, many):
+        x_line.step(piece, state[0])
+    table, sources = x_line.turns(2, count - 2, sub)
+    state = enter(sub, after(table, state[0]), sources, *enter_rest, state)
+    e_line = Gather([after(back_own, state[0], x_line.last()[0])], count, place)
     e_line.step(0)
     table, sources = x_line.turns(count - 1, count - 1, sub)
-    table = after(table, state, x_line.last())
+    table = after(table, state[0], x_line.last())
     state = enter(sub, table, sources, *enter_rest, state)
     x_all, a1, a2, stat, act, gelu_slope, qkv = state
 
@@ -735,73 +832,54 @@
         half = wgrad(*product, after(there, *earlier), quads, None)[0]
         return lax.ppermute(half, "pair", [(0, 1), (1, 0)]), half
 
-    def settle(product, got, *earlier):
-        blocks = wgrad(*product, after(here, *earlier), quads, got)
-        terms = [
-            lax.ppermute(blocks[hop], "quad", [(i, i ^ hop) for i in range(quads)])
-            for hop in range(1, quads)
-        ]
-        return [blocks[0]] + terms
-
-    def total(terms):
-        return sum(v[0].astype(F32) for v in terms)
-
-    up = ((a2,), (dhid,), True, 0.05)
+    def settle(product, got, earlier, before_sending):
+        return Spread(after(wgrad(*product, after(here, *earlier), quads, got), before_sending), quads)
+
     late = jnp.concatenate([there, arrival[count - 1 :]])
     mark = wgrad_part(second, back_rows, rows, after(late, dhid), 1, quads, give_second)
     got_second = lax.ppermute(mark, "pair", [(0, 1), (1, 0)])
-    got_up, mark = give(up, mark)
-    sum_second = settle((second, (back_rows,), False, 0.25), got_second, mark)
-    dmixed, col_qkv = attn_bwd(qkv, dctx, after(begin, sum_second[0]), lse, tables)
+    got_up, mark = give(((a2,), (dhid,), True, 0.05), mark)
+    sum_second = settle((second, (back_rows,), False, 0.05), got_second, (mark,), ())
+    dmixed, col_qkv = attn_bwd(qkv, dctx, after(begin, sum_second.mark), lse, tables)
     grad_bqkv = col_qkv[0]
-    inner = ((a1,), (dmixed,), True, 9)
-    sum_up = settle(up, got_up, dmixed)
-    grad_parts, col = din_all(
-        after(dmixed, sum_up[0], *sum_second[1:]), dhid, full_in, x_all, stat, norm_vec
-    )
-    grad_rows = lax.psum_scatter(grad_parts, "mp", scatter_dimension=0, tiled=True).astype(F32)
-
-    back_vals = back_own.astype(F32)
-    out_bias = jnp.sum(back_vals, axis=0)
-    small = jnp.concatenate([col[0:4], out_bias[None], out_bias[None]], axis=0)
-    packed = jnp.concatenate([small.reshape(-1), grad_bqkv, grad_bup]).reshape(-1, 128)
-    got_inner, mark = give(inner, grad_parts, branch, *sum_up[1:])
-    packed = everywhere(packed, (("pair", 2),))
-    sum_inner = settle(inner, got_inner, mark, packed)
-    packed = everywhere(packed, (("quad", quads),))
-    part_up, part_qkv, sum_second = total(sum_up), total(sum_inner), total(sum_second)
+    sum_second.rest(dmixed)
+    grad_parts, col = din_all(dmixed, dhid, full_in, x_all, stat, norm_vec)
+    grad_rows = lax.psum_scatter(grad_parts, "mp", scatter_dimension=0, tiled=True)
+    got_inner, mark = give(((a1,), (dmixed,), True, 16), grad_parts, branch, sum_second.got)
+    sum_up = settle(((a2,), (dhid,), True, 0.05), got_up, (mark,), ())
+    sum_inner = settle(((a1,), (dmixed,), True, 4), got_inner, (sum_up.mark,), ())
+    sum_up.rest(sum_inner.mark)
+    sum_inner.rest()
+    part_up, part_qkv, sum_second = sum_up.total(), sum_inner.total(), sum_second.total()
     units = act.shape[1]
     part_down, part_out = sum_second[:units], sum_second[units:]
     token_vals = tokens.astype(F32)
     layer_out = (token_vals + branch.astype(F32) + norm_vec[4] + norm_vec[5]).astype(BF16)
 
-    n_small = small.size // 128
-    n_qkv = grad_bqkv.size // 128
-    small_sum = everywhere(packed[:n_small], (("mp", count),))
-    grad_small = small_sum.reshape(6, D)
-    sum_bqkv = packed[n_small : n_small + n_qkv].reshape(-1)
-    sum_bup = packed[n_small + n_qkv :].reshape(-1)
-
-    mean, rstd = (lax.dynamic_slice_in_dim(stat, place * rows, rows, 0)[:, i : i + 1] for i in (0, 1))
-    xhat = (token_vals - mean) * rstd
-    grad_in = back_vals + rstd * (
-        grad_rows
-        - jnp.mean(grad_rows, axis=1, keepdims=True)
-        - xhat * jnp.mean(grad_rows * xhat, axis=1, keepdims=True)
-    )
-    grad_in = grad_in.astype(BF16)
-
+    back_vals = back_own.astype(F32)
+    out_bias = jnp.sum(back_vals, axis=0)
+    small = jnp.concatenate([col[0:4], out_bias[None], out_bias[None]], axis=0)
     local_squares = (
         jnp.sum(part_qkv * part_qkv)
         + jnp.sum(part_out * part_out)
         + jnp.sum(part_up * part_up)
         + jnp.sum(part_down * part_down)
-        + (jnp.sum(sum_bqkv * sum_bqkv) + jnp.sum(sum_bup * sum_bup)) / (2 * quads)
-    )
-    total = everywhere(
-        jnp.broadcast_to(local_squares, (8, 128)), (("pair", 2), ("quad", quads), ("mp", count))
-    )[0, 0]
-    grad_norm = jnp.sqrt(total + jnp.sum(grad_small * grad_small))
+    )
+    squares = jnp.broadcast_to(local_squares, (128,))
+    packed = jnp.concatenate([grad_bqkv, grad_bup, small.reshape(-1), squares]).reshape(-1, 128)
+    packed = everywhere(everywhere(packed, "pair", 2), "quad", quads)
+    n_qkv, n_up = grad_bqkv.size // 128, grad_bup.size // 128
+    biases, rest = packed[: n_qkv + n_up], packed[n_qkv + n_up :]
+    sum_bqkv, sum_bup = biases[:n_qkv].reshape(-1), biases[n_qkv:].reshape(-1)
+    rest = rest + jnp.concatenate(
+        [jnp.zeros((rest.shape[0] - 1, 128), F32), jnp.full((1, 128), jnp.sum(biases * biases))], axis=0
+    )
+    rest = everywhere(rest, "mp", count)
+    grad_small = rest[:-1].reshape(6, D)
+    total_squares = rest[-1, 0]
+    grad_in = finish(place.reshape(1).astype(jnp.int32), grad_rows, back_own, tokens, stat)
+
+    grad_norm = jnp.sqrt(total_squares + jnp.sum(grad_small * grad_small))
     factor = jnp.minimum(1.0, CLIP_NORM / (grad_norm + 1e-06))
     rate_big = 2.5 * D ** (-0.5)
     rate_out = 2.5 * max(16 * D // GROUP_TOK, 1) ** (-0.5)

time: 665 us -> 651 us (0.979)
  waiting for transfers between devices: 133 us -> 107 us
  Pallas kernels: 352 us -> 365 us
  other arithmetic: 68.8 us -> 58.1 us
  local copies, waits for them, and re-layouts: 15.7 us -> 24.6 us
    ppermute x6 -> x9, waiting for transfers between devices: 81 us -> 37.2 us  [step(): lax.ppermute(there, 'mp', [(i + 1, i) for i in range(0, count - step)])]
    ppermute x9 -> x12, waiting for transfers between devices: 4.1 us -> 37 us  [hand(): lax.ppermute(stack, 'quad', [(i, i ^ 1 << bit) for i in range(self.quads)])]
    ppermute x10 -> x7, waiting for transfers between devices: 41.3 us -> 9.32 us  [everywhere(): lax.ppermute(value, axis, [(i, i ^ hop) for i in range(size)])]
    ppermute x6 -> x9, waiting for transfers between devices: 1.1 us -> 23.4 us  [step(): lax.ppermute(here, 'mp', [(i, i + 1) for i in range(step - 1, count - 1)])]
    pallas_call x2 -> x3, Pallas kernels: 64 us -> 73.9 us  [enter(): pl.pallas_call(functools.partial(enter_kernel, many, units), grid_spec=pl...]
    ppermute x10 -> x7, starting transfers between devices: 20.9 us -> 11.7 us  [everywhere(): lax.ppermute(value, axis, [(i, i ^ hop) for i in range(size)])]
    unnamed x70 -> x124, local copies, waits for them, and re-layouts: 2.62 us -> 10.4 us
    ppermute x9 -> x12, starting transfers between devices: 10.5 us -> 14.5 us  [hand(): lax.ppermute(stack, 'quad', [(i, i ^ 1 << bit) for i in range(self.quads)])]
  transfers between devices with their start and end apart: 38 -> 44, of which waited for: 12 -> 20; matrix products, arithmetic and copies ran while one was open for 11% -> 11% of each run, Pallas kernels for 53% -> 56%
where the time goes in v2:
time: 651 us; the launch traced here: 644 us
  Pallas kernels  365 us (56%)
  waiting for transfers between devices  107 us (16%)
  starting transfers between devices  67.1 us (10%)
  other arithmetic  58.1 us (9%)
  local copies, waits for them, and re-layouts  24.6 us (4%)
  between operations  21.6 us (3%)
    pallas_call x5, Pallas kernels, wgrad(): pl.pallas_call(functools.partial(wgrad_kernel, len(lefts), len(rights), c...  79.4 us
    pallas_call x3, Pallas kernels, enter(): pl.pallas_call(functools.partial(enter_kernel, many, units), grid_spec=pl...  73.9 us
    pallas_call x3, Pallas kernels, leave(): pl.pallas_call(functools.partial(leave_kernel, many, units), grid_spec=pl...  46.5 us
    pallas_call x1, Pallas kernels, attn_bwd(): pl.pallas_call(functools.partial(attn_bwd_kernel, cases, width), grid=(he...  44 us
    pallas_call x1, Pallas kernels, din_all(): pl.pallas_call(din_kernel, grid=(D // tile, group // rows), in_specs=[pl....  40.4 us
    ppermute x9, waiting for transfers between devices, step(): lax.ppermute(there, 'mp', [(i + 1, i) for i in range(0, count - step)])  37.2 us
    ppermute x12, waiting for transfers between devices, hand(): lax.ppermute(stack, 'quad', [(i, i ^ 1 << bit) for i in range(self.quads)])  37 us
    pallas_call x1, Pallas kernels, branch_all(): pl.pallas_call(functools.partial(branch_kernel, units), grid=(D // tile,...  28.3 us
  transfers between devices with their start and end apart: 44, of which 20 were waited for; matrix products, arithmetic and copies ran while one was open for 11% of the time, Pallas kernels for 56%

profile of v2, /device:TPU:0, one launch (start us, length us, event | category | flops | bytes accessed | tf_op | source)
XLA Modules:
  0.0 643.5 jit_solution(13795204330080800256)
XLA Ops:
  7.2 1.6 convert_element_type.148
  12.8 5.0 collective-permute-start
  19.1 21.0 %collective-permute-done.refs_3_ = bf16[256,2048]{1,0:T(8,128)(2,1)S(1)} collective-permute-done((bf16[256,2048]{1,0:T(8,128)(2,1)S(1)}, bf16[256,2048]{1,0:T(8,128)(2,1)S(1)}, u32[]{:S(2)}, u32[]{:S(2)}) %collective-permute-start) | collective-permute-done | bytes 1048608 | tf_op jit(solution)/shard_map/ppermute | solution.py:688
  41.1 3.3 collective-permute-done.1.refs_2_.refs_1_
  45.8 4.5 collective-permute-start.5
  60.6 2.8 convert_reduce_fusion
  65.4 3.7 multiply_sine_fusion
  69.2 2.5 maximum_maximum_fusion.2
  71.8 6.8 %collective-permute-done.4.refs_4_ = bf16[256,2048]{1,0:T(8,128)(2,1)} collective-permute-done((bf16[256,2048]{1,0:T(8,128)(2,1)}, bf16[256,2048]{1,0:T(8,128)(2,1)}, u32[]{:S(2)}, u32[]{:S(2)}) %collective-permute-start.4) | collective-permute-done | bytes 1048608 | tf_op jit(solution)/shard_map/ppermute | solution.py:689
  78.5 1.6 collective-permute-start.7
  81.5 19.5 %collective-permute-done.3.refs_0_.refs_1_ = bf16[256,2048]{1,0:T(8,128)(2,1)} collective-permute-done((bf16[256,2048]{1,0:T(8,128)(2,1)}, bf16[256,2048]{1,0:T(8,128)(2,1)}, u32[]{:S(2)}, u32[]{:S(2)}) %collective-permute-start.3) | collective-permute-done | bytes 1048608 | tf_op jit(solution)/shard_map/ppermute | solution.py:689
  101.0 1.7 collective-permute-start.8
  102.7 1.7 collective-permute-start.9
  104.5 32.4 %enter.3 = (bf16[2048,2048]{1,0:T(8,128)(2,1)}, bf16[2048,2048]{1,0:T(8,128)(2,1)}, bf16[2048,2048]{1,0:T(8,128)(2,1)}, f32[2048,128]{1,0:T(8,128)}, bf16[2048,2...) custom-call(s32[4,3]{1,0:T(4,128)} %dynamic-slice_bitcast_fusion.1.table, ...), custom_call_target="tpu_custom_call" | custom-call | flops 15032385536 | bytes 14680064 | tf_op jit(solution)/shard_map/enter/pallas_call | solution.py:144
  136.9 1.7 collective-permute-start.10
  139.9 21.0 %enter.4 = (bf16[2048,2048]{1,0:T(8,128)(2,1)}, bf16[2048,2048]{1,0:T(8,128)(2,1)}, bf16[2048,2048]{1,0:T(8,128)(2,1)}, f32[2048,128]{1,0:T(8,128)}, bf16[2048,2...) custom-call(s32[2,3]{1,0:T(2,128)} %fusion.14.table, ...), custom_call_target="tpu_custom_call", output_to_operand_aliasing={{0}: (14, {}), {1}: (15, {}), {2}: (16, {}), {3}: (17, {}),... | custom-call | flops 7516192768 | bytes 14680064 | tf_op jit(solution)/shard_map/enter/pallas_call | solution.py:144
  160.9 7.8 %collective-permute-start.13 = (bf16[512,2048]{1,0:T(8,128)(2,1)S(1)}, bf16[512,2048]{1,0:T(8,128)(2,1)}, u32[]{:S(2)}, u32[]{:S(2)}) collective-permute-start(bf16[512,2048]{1,0:T(8,128)(2,1)S(1)} %get-tuple-element.163.refs_0_.e_ref), channel_id=1, source_target_pairs={{0,1},{1,2},{2,3},{4,5},{5,6},{6,7},{8,9},{9,10},{10,11},{12,13},{... | collective-permute-start | bytes 6291464 | tf_op jit(solution)/shard_map/ppermute | solution.py:688
  173.3 20.5 %enter.5 = (bf16[2048,2048]{1,0:T(8,128)(2,1)}, bf16[2048,2048]{1,0:T(8,128)(2,1)}, bf16[2048,2048]{1,0:T(8,128)(2,1)}, f32[2048,128]{1,0:T(8,128)}, bf16[2048,2...) custom-call(s32[2,3]{1,0:T(2,128)} %fusion.13.table, ...), custom_call_target="tpu_custom_call", output_to_operand_aliasing={{0}: (16, {}), {1}: (17, {}), {2}: (18, {}), {3}: (19, {}),... | custom-call | flops 7516192768 | bytes 14680064 | tf_op jit(solution)/shard_map/enter/pallas_call | solution.py:144
  193.8 11.4 %attend.2 = (bf16[2048,512]{1,0:T(8,128)(2,1)}, f32[4,1,2048]{2,1,0:T(1,128)}) custom-call(bf16[2048,1536]{1,0:T(8,128)(2,1)} %get-tuple-element.154.q_ref.k_ref.v_ref, bf16[2048,1536]{1,0:T(8,128)(2,1)} %get-tuple-element.154.q_ref.k_ref.v_ref, bf16[2048,1536]{1,0:T(8,128)(2,1)} %get-tuple-element.154.q_ref.k_ref.v_ref, ...), custom_call_target="tpu_custom_call" | custom-call | flops 10737418240 | bytes 4194304 | tf_op jit(solution)/shard_map/attend/pallas_call | solution.py:219
  205.2 2.4 collective-permute-done.13.refs_2_
  207.6 6.7 %collective-permute-done.12.refs_1_ = bf16[512,2048]{1,0:T(8,128)(2,1)} collective-permute-done((bf16[512,2048]{1,0:T(8,128)(2,1)S(1)}, bf16[512,2048]{1,0:T(8,128)(2,1)}, u32[]{:S(2)}, u32[]{:S(2)}) %collective-permute-start.12) | collective-permute-done | bytes 2097184 | tf_op jit(solution)/shard_map/ppermute | solution.py:689
  215.6 2.2 collective-permute-start.15
  217.8 11.4 %attend.3 = (bf16[2048,512]{1,0:T(8,128)(2,1)}, f32[4,1,2048]{2,1,0:T(1,128)}) custom-call(bf16[2048,1536]{1,0:T(8,128)(2,1)} %get-tuple-element.154.q_ref.k_ref.v_ref, bf16[2048,1536]{1,0:T(8,128)(2,1)} %get-tuple-element.154.q_ref.k_ref.v_ref, ...), custom_call_target="tpu_custom_call", output_to_operand_aliasing={{0}: (4, {}), {1}: (5, {})} | custom-call | flops 10737418240 | bytes 4194304 | tf_op jit(solution)/shard_map/attend/pallas_call | solution.py:219
  229.2 28.3 %branch.1 = bf16[2048,2048]{1,0:T(8,128)(2,1)} custom-call(bf16[2048,512]{1,0:T(8,128)(2,1)} %get-tuple-element.157.o_ref.refs_1_, bf16[2048,2048]{1,0:T(8,128)(2,1)} %get-tuple-element.158.act_ref.refs_0_, bf16[2560,2048]{1,0:T(8,128)(2,1)} %all-gather.5.cloned.1.call-done.w_ref.refs_3_.refs_4_), custom_call_target="tpu_custom_call" | custom-call | flops 21474836480 | bytes 10485760 | tf_op jit(solution)/shard_map/branch/pallas_call | solution.py:333
  258.3 2.0 collective-permute-start.16
  260.3 1.5 collective-permute-start.17
  261.8 19.7 %leave.3 = (bf16[2048,2048]{1,0:T(8,128)(2,1)}, bf16[2048,2048]{1,0:T(8,128)(2,1)}, bf16[2048,512]{1,0:T(8,128)(2,1)}, f32[8,2048]{1,0:T(8,128)}) custom-call(s32[4,3]{1,0:T(4,128)} %dynamic-slice_bitcast_fusion.table, bf16[512,2048]{1,0:T(8,128)(2,1)} %copy-done.3, bf16[512,2048]{1,0:T(8,128)(2,1)} %collective-permute-done.12.refs_1_, ...), custom_call_target="tpu_custom_call" | custom-call | flops 10737418240 | bytes 10485760 | tf_op jit(solution)/shard_map/leave/pallas_call | solution.py:386
  281.6 13.4 %leave.4 = (bf16[2048,2048]{1,0:T(8,128)(2,1)}, bf16[2048,2048]{1,0:T(8,128)(2,1)}, bf16[2048,512]{1,0:T(8,128)(2,1)}, f32[8,2048]{1,0:T(8,128)}) custom-call(s32[2,3]{1,0:T(2,128)} %fusion.15.table, bf16[512,2048]{1,0:T(8,128)(2,1)} %copy-done.14, ...), custom_call_target="tpu_custom_call", output_to_operand_aliasing={{0}: (6, {}), {1}: (7, {}), {2}: (8, {})} | custom-call | flops 5368709120 | bytes 10485760 | tf_op jit(solution)/shard_map/leave/pallas_call | solution.py:386
  295.0 15.9 %weight_grad_part.2.refs_3_ = f32[4,2560,256]{2,1,0:T(8,128)} custom-call(s32[5]{0:T(128)} %pad_add_fusion.place, bf16[2048,2048]{1,0:T(8,128)(2,1)} %get-tuple-element.158.act_ref.refs_0_, bf16[2048,512]{1,0:T(8,128)(2,1)} %get-tuple-element.157.o_ref.refs_1_, bf16[2048,2048]{1,0:T(8,128)(2,1)} %get-tuple-element.175.refs_2_.refs_3_.refs_4_.refs_6_, ...), custom_call_target="tpu_custom_call" | custom-call | flops 8053063680 | tf_op jit(solution)/shard_map/weight_grad_part/pallas_call | solution.py:643
  314.5 13.4 %leave.5 = (bf16[2048,2048]{1,0:T(8,128)(2,1)}, bf16[2048,2048]{1,0:T(8,128)(2,1)}, bf16[2048,512]{1,0:T(8,128)(2,1)}, f32[8,2048]{1,0:T(8,128)}) custom-call(s32[2,3]{1,0:T(2,128)} %fusion.16.table, bf16[512,2048]{1,0:T(8,128)(2,1)} %collective-permute-done.17.refs_0_, ...), custom_call_target="tpu_custom_call", output_to_operand_aliasing={{0}: (7, {}), {1}: (8, {}), {2}: (9, {})} | custom-call | flops 5368709120 | bytes 10485760 | tf_op jit(solution)/shard_map/leave/pallas_call | solution.py:386
  327.9 11.0 %weight_grad_part.3 = bf16[4,2560,256]{2,1,0:T(8,128)(2,1)} custom-call(s32[3]{0:T(128)} %pad_add_fusion.3.place, bf16[2048,2048]{1,0:T(8,128)(2,1)} %get-tuple-element.158.act_ref.refs_0_, bf16[2048,512]{1,0:T(8,128)(2,1)} %get-tuple-element.157.o_ref.refs_1_, bf16[2048,2048]{1,0:T(8,128)(2,1)} %get-tuple-element.184.refs_2_, ...), custom_call_target="tpu_custom_call" | custom-call | flops 2684354560 | tf_op jit(solution)/shard_map/weight_grad_part/pallas_call | solution.py:643
  340.1 15.0 %weight_grad.5 = bf16[4,256,2048]{2,1,0:T(8,128)(2,1)} custom-call(s32[2]{0:T(128)} %pad_add_fusion.2.place, bf16[2048,2048]{1,0:T(8,128)(2,1)} %get-tuple-element.186.refs_0_, bf16[2048,2048]{1,0:T(8,128)(2,1)} %get-tuple-element.182.refs_1_.dh_ref), custom_call_target="tpu_custom_call" | custom-call | flops 429496736 | tf_op jit(solution)/shard_map/weight_grad/pallas_call | solution.py:559
  355.1 21.2 %weight_grad.6 = (bf16[2,1280,256]{2,1,0:T(8,128)(2,1)}, bf16[1,1280,256]{2,1,0:T(8,128)(2,1)}, bf16[1,1280,256]{2,1,0:T(8,128)(2,1)}, bf16[2,1280,256]{2,1,0:T(...) custom-call(s32[2]{0:T(128)} %pad_add_fusion.1.place, ...), custom_call_target="tpu_custom_call" | custom-call | flops 536870912 | tf_op jit(solution)/shard_map/weight_grad/pallas_call | solution.py:559
  376.3 1.5 collective-permute-start.19
  377.8 1.5 collective-permute-start.20
  379.3 44.0 %attend_back.1 = (bf16[2048,1536]{1,0:T(8,128)(2,1)}, f32[8,1536]{1,0:T(8,128)}) custom-call(bf16[2048,1536]{1,0:T(8,128)(2,1)} %get-tuple-element.154.q_ref.k_ref.v_ref, bf16[2048,1536]{1,0:T(8,128)(2,1)} %get-tuple-element.154.q_ref.k_ref.v_ref, bf16[2048,1536]{1,0:T(8,128)(2,1)} %get-tuple-element.154.q_ref.k_ref.v_ref, ...), custom_call_target="tpu_custom_call" | custom-call | flops 134217728 | tf_op jit(solution)/shard_map/attend_back/pallas_call | solution.py:299
  426.5 40.4 %input_back.1 = (bf16[2048,2048]{1,0:T(8,128)(2,1)}, f32[8,2048]{1,0:T(8,128)}) custom-call(bf16[2048,1536]{1,0:T(8,128)(2,1)} %get-tuple-element.191.dm_ref.refs_1_, bf16[2048,2048]{1,0:T(8,128)(2,1)} %get-tuple-element.182.refs_1_.dh_ref, bf16[2048,3584]{1,0:T(8,128)(2,1)} %all-gather.3.cloned.1.call-done.refs_7_.refs_9_.w_ref, ...), custom_call_target="tpu_custom_call" | custom-call | flops 300647712 | tf_op jit(solution)/shard_map/input_back/pallas_call | solution.py:431
  467.0 12.2 %weight_grad.7 = bf16[4,256,1536]{2,1,0:T(8,128)(2,1)} custom-call(s32[2]{0:T(128)} %pad_add_fusion.2.place, bf16[2048,2048]{1,0:T(8,128)(2,1)} %get-tuple-element.205.refs_0_, bf16[2048,1536]{1,0:T(8,128)(2,1)} %get-tuple-element.191.dm_ref.refs_1_), custom_call_target="tpu_custom_call" | custom-call | flops 103079215104 | tf_op jit(solution)/shard_map/weight_grad/pallas_call | solution.py:559
  481.7 1.5 convert_add_fusion
  485.5 17.1 %weight_grad.8 = (bf16[2,128,2048]{2,1,0:T(8,128)(2,1)}, bf16[1,128,2048]{2,1,0:T(8,128)(2,1)}, bf16[1,128,2048]{2,1,0:T(8,128)(2,1)}, bf16[2,128,2048]{2,1,0:T(...) custom-call(s32[2]{0:T(128)} %pad_add_fusion.1.place, ...), custom_call_target="tpu_custom_call" | custom-call | flops 429496736 | tf_op jit(solution)/shard_map/weight_grad/pallas_call | solution.py:559
  504.1 1.7 collective-permute-start.30
  505.8 13.9 %weight_grad.9 = (bf16[2,128,1536]{2,1,0:T(8,128)(2,1)}, bf16[1,128,1536]{2,1,0:T(8,128)(2,1)}, bf16[1,128,1536]{2,1,0:T(8,128)(2,1)}, bf16[2,128,1536]{2,1,0:T(...) custom-call(s32[2]{0:T(128)} %pad_add_fusion.1.place, ...), custom_call_target="tpu_custom_call" | custom-call | flops 25769803776 | tf_op jit(solution)/shard_map/weight_grad/pallas_call | solution.py:559
  519.8 8.2 %collective-permute-done.29 = bf16[2,128,2048]{2,1,0:T(8,128)(2,1)} collective-permute-done((bf16[2,128,2048]{2,1,0:T(8,128)(2,1)}, bf16[2,128,2048]{2,1,0:T(8,128)(2,1)}, u32[]{:S(2)}, u32[]{:S(2)}) %collective-permute-start.29) | collective-permute-done | bytes 1048608 | tf_op jit(solution)/shard_map/ppermute | solution.py:581
  532.4 1.6 collective-permute-start.31
  535.1 1.7 collective-permute-start.25
  537.1 8.2 %collective-permute-done.32 = bf16[1,128,2048]{2,1,0:T(8,128)(2,1)S(1)} collective-permute-done((bf16[1,128,2048]{2,1,0:T(8,128)(2,1)S(1)}, bf16[1,128,2048]{2,1,0:T(8,128)(2,1)S(1)}, u32[]{:S(2)}, u32[]{:S(2)}) %collective-permute-start.32) | collective-permute-done | bytes 524320 | tf_op jit(solution)/shard_map/ppermute | solution.py:581
  549.8 10.2 %collective-permute-done.25 = bf16[2,128,1536]{2,1,0:T(8,128)(2,1)S(1)} collective-permute-done((bf16[2,128,1536]{2,1,0:T(8,128)(2,1)S(1)}, bf16[2,128,1536]{2,1,0:T(8,128)(2,1)S(1)}, u32[]{:S(2)}, u32[]{:S(2)}) %collective-permute-start.25) | collective-permute-done | bytes 786464 | tf_op jit(solution)/shard_map/ppermute | solution.py:581
  560.0 1.7 collective-permute-done.26
  561.8 1.5 collective-permute-start.28
  563.4 1.7 collective-permute-start.27
  565.2 5.5 collective-permute-done.28
  578.0 1.7 collective-permute-start.35
  582.3 2.8 collective-permute-done.36
  586.5 7.4 %collective-permute-start.38 = (f32[97,128]{1,0:T(8,128)S(1)}, f32[97,128]{1,0:T(8,128)S(1)}, u32[]{:S(2)}, u32[]{:S(2)}) collective-permute-start(f32[97,128]{1,0:T(8,128)S(1)} %slice_add_fusion), channel_id=1, source_target_pairs={{0,2},{1,3},{2,0},{3,1},{4,6},{5,7},{6,4},{7,5},{8,10},{9,11},{10,... | collective-permute-start | bytes 149000 | tf_op jit(solution)/shard_map/ppermute | solution.py:714
  594.6 3.8 add_convert_fusion
  598.4 3.9 collective-permute-done.38
  608.4 1.5 add_subtract_fusion.1
  609.9 2.7 multiply_subtract_fusion.3
  613.4 5.2 multiply_subtract_fusion.2
  619.6 3.9 multiply_subtract_fusion.1
  625.5 3.7 multiply_subtract_fusion
  629.2 1.6 copy-done.4
  630.8 1.6 copy-done.5
  632.4 3.1 finish.1
  (247 shorter events, 70.0 us)
Async XLA Ops:
  7.2 97.2 %all-gather.3.cloned.1.call-start = ((), (), s32[]{:S(2)}) async-start(), calls=%async_computation.2 | async-start | bytes 16515072 | tf_op jit(solution)/shard_map/all_gather | solution.py:775
  10.8 33.6 %copy-start.25 = (f32[512,256]{1,0:T(8,128)S(1)}, f32[512,256]{1,0:T(8,128)}, u32[]{:S(2)}) copy-start(f32[512,256]{1,0:T(8,128)} %param.35) | copy-start | bytes 1572868
  10.8 218.4 %all-gather.5.cloned.1.call-start = ((), (), s32[]{:S(2)}) async-start(), calls=%async_computation.3 | async-start | bytes 11796480 | tf_op jit(solution)/shard_map/all_gather | solution.py:778
  11.7 32.8 %copy-start.17 = (f32[2048,256]{1,0:T(8,128)S(1)}, f32[2048,256]{1,0:T(8,128)}, u32[]{:S(2)}) copy-start(f32[2048,256]{1,0:T(8,128)} %param.37) | copy-start | bytes 6291460
  12.8 31.6 %copy-start.32 = (bf16[256,2048]{1,0:T(8,128)(2,1)}, bf16[256,2048]{1,0:T(8,128)(2,1)S(1)}, u32[]{:S(2)}) copy-start(bf16[256,2048]{1,0:T(8,128)(2,1)S(1)} %get-tuple-element.126.refs_0_) | copy-start | bytes 3145732
  12.8 27.3 %collective-permute-start = (bf16[256,2048]{1,0:T(8,128)(2,1)S(1)}, bf16[256,2048]{1,0:T(8,128)(2,1)S(1)}, u32[]{:S(2)}, u32[]{:S(2)}) collective-permute-start(bf16[256,2048]{1,0:T(8,128)(2,1)S(1)} %get-tuple-element.126.refs_0_), channel_id=1, source_target_pairs={{0,1},{1,2},{2,3},{4,5},{5,6},{6,7},{8,9},{9,10},{10,11},{12,13},{... | collective-permute-start | bytes 3145736 | tf_op jit(solution)/shard_map/ppermute | solution.py:688
  17.8 26.6 %collective-permute-start.1 = (bf16[256,2048]{1,0:T(8,128)(2,1)S(1)}, bf16[256,2048]{1,0:T(8,128)(2,1)}, u32[]{:S(2)}, u32[]{:S(2)}) collective-permute-start(bf16[256,2048]{1,0:T(8,128)(2,1)S(1)} %get-tuple-element.126.refs_0_), channel_id=1, source_target_pairs={{1,0},{2,1},{3,2},{5,4},{6,5},{7,6},{9,8},{10,9},{11,10},{13,12},{... | collective-permute-start | bytes 3145736 | tf_op jit(solution)/shard_map/ppermute | solution.py:689
  45.7 421.2 %reduce-scatter.3.cloned.1.call-start = ((), (), s32[]{:S(2)}) async-start(), calls=%async_computation.4 | async-start | bytes 10485760 | tf_op jit(solution)/shard_map/reduce_scatter | solution.py:829
  45.8 26.0 %collective-permute-start.5 = (bf16[256,2048]{1,0:T(8,128)(2,1)}, bf16[256,2048]{1,0:T(8,128)(2,1)}, u32[]{:S(2)}, u32[]{:S(2)}) collective-permute-start(bf16[256,2048]{1,0:T(8,128)(2,1)} %get-tuple-element.130.refs_1_), channel_id=1, source_target_pairs={{0,1},{1,2},{2,3},{4,5},{5,6},{6,7},{8,9},{9,10},{10,11},{12,13},{... | collective-permute-start | bytes 3145736 | tf_op jit(solution)/shard_map/ppermute | solution.py:688
  50.2 28.3 %collective-permute-start.4 = (bf16[256,2048]{1,0:T(8,128)(2,1)}, bf16[256,2048]{1,0:T(8,128)(2,1)}, u32[]{:S(2)}, u32[]{:S(2)}) collective-permute-start(bf16[256,2048]{1,0:T(8,128)(2,1)} %get-tuple-element.130.refs_1_), channel_id=1, source_target_pairs={{1,0},{2,1},{3,2},{5,4},{6,5},{7,6},{9,8},{10,9},{11,10},{13,12},{... | collective-permute-start | bytes 3145736 | tf_op jit(solution)/shard_map/ppermute | solution.py:689
  63.4 105.3 %copy-start.3 = (bf16[512,2048]{1,0:T(8,128)(2,1)}, bf16[512,2048]{1,0:T(8,128)(2,1)S(1)}, u32[]{:S(2)}) copy-start(bf16[512,2048]{1,0:T(8,128)(2,1)S(1)} %get-tuple-element.163.refs_0_.e_ref) | copy-start | bytes 6291460
  63.4 18.0 %collective-permute-start.2 = (bf16[256,2048]{1,0:T(8,128)(2,1)S(1)}, bf16[256,2048]{1,0:T(8,128)(2,1)S(1)}, u32[]{:S(2)}, u32[]{:S(2)}) collective-permute-start(bf16[256,2048]{1,0:T(8,128)(2,1)S(1)} %copy-done.57), channel_id=1, source_target_pairs={{1,2},{2,3},{5,6},{6,7},{9,10},{10,11},{13,14},{14,15},{17,18},{18... | collective-permute-start | bytes 3145736 | tf_op jit(solution)/shard_map/ppermute | solution.py:688
  64.1 36.9 %collective-permute-start.3 = (bf16[256,2048]{1,0:T(8,128)(2,1)}, bf16[256,2048]{1,0:T(8,128)(2,1)}, u32[]{:S(2)}, u32[]{:S(2)}) collective-permute-start(bf16[256,2048]{1,0:T(8,128)(2,1)} %collective-permute-done.1.refs_2_.refs_1_), channel_id=1, source_target_pairs={{1,0},{2,1},{5,4},{6,5},{9,8},{10,9},{13,12},{14,13},{17,16},{18,1... | collective-permute-start | bytes 3145736 | tf_op jit(solution)/shard_map/ppermute | solution.py:689
  78.5 58.4 %collective-permute-start.7 = (bf16[256,2048]{1,0:T(8,128)(2,1)}, bf16[256,2048]{1,0:T(8,128)(2,1)}, u32[]{:S(2)}, u32[]{:S(2)}) collective-permute-start(bf16[256,2048]{1,0:T(8,128)(2,1)} %collective-permute-done.5.refs_5_), channel_id=1, source_target_pairs={{1,2},{2,3},{5,6},{6,7},{9,10},{10,11},{13,14},{14,15},{17,18},{18... | collective-permute-start | bytes 3145736 | tf_op jit(solution)/shard_map/ppermute | solution.py:688
  80.2 56.7 %collective-permute-start.6 = (bf16[256,2048]{1,0:T(8,128)(2,1)}, bf16[256,2048]{1,0:T(8,128)(2,1)}, u32[]{:S(2)}, u32[]{:S(2)}) collective-permute-start(bf16[256,2048]{1,0:T(8,128)(2,1)} %collective-permute-done.4.refs_4_), channel_id=1, source_target_pairs={{1,0},{2,1},{5,4},{6,5},{9,8},{10,9},{13,12},{14,13},{17,16},{18,1... | collective-permute-start | bytes 3145736 | tf_op jit(solution)/shard_map/ppermute | solution.py:689
  81.5 55.4 %copy-start.24 = (bf16[256,2048]{1,0:T(8,128)(2,1)}, bf16[256,2048]{1,0:T(8,128)(2,1)S(1)}, u32[]{:S(2)}) copy-start(bf16[256,2048]{1,0:T(8,128)(2,1)S(1)} %collective-permute-done.2.refs_2_) | copy-start | bytes 3145732
  101.0 59.8 %collective-permute-start.8 = (bf16[256,2048]{1,0:T(8,128)(2,1)S(1)}, bf16[256,2048]{1,0:T(8,128)(2,1)}, u32[]{:S(2)}, u32[]{:S(2)}) collective-permute-start(bf16[256,2048]{1,0:T(8,128)(2,1)S(1)} %collective-permute-done.2.refs_2_), channel_id=1, source_target_pairs={{2,3},{6,7},{10,11},{14,15},{18,19},{22,23},{26,27},{30,31}} | collective-permute-start | bytes 3145736 | tf_op jit(solution)/shard_map/ppermute | solution.py:688
  102.7 58.2 %collective-permute-start.9 = (bf16[256,2048]{1,0:T(8,128)(2,1)}, bf16[256,2048]{1,0:T(8,128)(2,1)}, u32[]{:S(2)}, u32[]{:S(2)}) collective-permute-start(bf16[256,2048]{1,0:T(8,128)(2,1)} %collective-permute-done.3.refs_0_.refs_1_), channel_id=1, source_target_pairs={{1,0},{5,4},{9,8},{13,12},{17,16},{21,20},{25,24},{29,28}} | collective-permute-start | bytes 3145736 | tf_op jit(solution)/shard_map/ppermute | solution.py:689
  136.9 36.4 %collective-permute-start.10 = (bf16[256,2048]{1,0:T(8,128)(2,1)}, bf16[256,2048]{1,0:T(8,128)(2,1)}, u32[]{:S(2)}, u32[]{:S(2)}) collective-permute-start(bf16[256,2048]{1,0:T(8,128)(2,1)} %collective-permute-done.7.refs_5_.refs_6_), channel_id=1, source_target_pairs={{2,3},{6,7},{10,11},{14,15},{18,19},{22,23},{26,27},{30,31}} | collective-permute-start | bytes 3145736 | tf_op jit(solution)/shard_map/ppermute | solution.py:688
  138.6 34.7 %collective-permute-start.11 = (bf16[256,2048]{1,0:T(8,128)(2,1)}, bf16[256,2048]{1,0:T(8,128)(2,1)}, u32[]{:S(2)}, u32[]{:S(2)}) collective-permute-start(bf16[256,2048]{1,0:T(8,128)(2,1)} %collective-permute-done.6.refs_3_.refs_5_), channel_id=1, source_target_pairs={{1,0},{5,4},{9,8},{13,12},{17,16},{21,20},{25,24},{29,28}} | collective-permute-start | bytes 3145736 | tf_op jit(solution)/shard_map/ppermute | solution.py:689
  160.9 46.7 %collective-permute-start.13 = (bf16[512,2048]{1,0:T(8,128)(2,1)S(1)}, bf16[512,2048]{1,0:T(8,128)(2,1)}, u32[]{:S(2)}, u32[]{:S(2)}) collective-permute-start(bf16[512,2048]{1,0:T(8,128)(2,1)S(1)} %get-tuple-element.163.refs_0_.e_ref), channel_id=1, source_target_pairs={{0,1},{1,2},{2,3},{4,5},{5,6},{6,7},{8,9},{9,10},{10,11},{12,13},{... | collective-permute-start | bytes 6291464 | tf_op jit(solution)/shard_map/ppermute | solution.py:688
  168.7 45.6 %collective-permute-start.12 = (bf16[512,2048]{1,0:T(8,128)(2,1)S(1)}, bf16[512,2048]{1,0:T(8,128)(2,1)}, u32[]{:S(2)}, u32[]{:S(2)}) collective-permute-start(bf16[512,2048]{1,0:T(8,128)(2,1)S(1)} %get-tuple-element.163.refs_0_.e_ref), channel_id=1, source_target_pairs={{1,0},{2,1},{3,2},{5,4},{6,5},{7,6},{9,8},{10,9},{11,10},{13,12},{... | collective-permute-start | bytes 6291464 | tf_op jit(solution)/shard_map/ppermute | solution.py:689
  214.3 44.0 %collective-permute-start.14 = (bf16[512,2048]{1,0:T(8,128)(2,1)}, bf16[512,2048]{1,0:T(8,128)(2,1)S(1)}, u32[]{:S(2)}, u32[]{:S(2)}) collective-permute-start(bf16[512,2048]{1,0:T(8,128)(2,1)} %collective-permute-done.12.refs_1_), channel_id=1, source_target_pairs={{1,0},{2,1},{5,4},{6,5},{9,8},{10,9},{13,12},{14,13},{17,16},{18,1... | collective-permute-start | bytes 6291464 | tf_op jit(solution)/shard_map/ppermute | solution.py:689
  215.6 42.8 %collective-permute-start.15 = (bf16[512,2048]{1,0:T(8,128)(2,1)}, bf16[512,2048]{1,0:T(8,128)(2,1)}, u32[]{:S(2)}, u32[]{:S(2)}) collective-permute-start(bf16[512,2048]{1,0:T(8,128)(2,1)} %collective-permute-done.13.refs_2_), channel_id=1, source_target_pairs={{1,2},{2,3},{5,6},{6,7},{9,10},{10,11},{13,14},{14,15},{17,18},{18... | collective-permute-start | bytes 6291464 | tf_op jit(solution)/shard_map/ppermute | solution.py:688
  258.3 23.2 %copy-start.14 = (bf16[512,2048]{1,0:T(8,128)(2,1)}, bf16[512,2048]{1,0:T(8,128)(2,1)S(1)}, u32[]{:S(2)}) copy-start(bf16[512,2048]{1,0:T(8,128)(2,1)S(1)} %collective-permute-done.14.refs_0_.refs_1_) | copy-start | bytes 6291460
  258.3 52.5 %collective-permute-start.16 = (bf16[512,2048]{1,0:T(8,128)(2,1)}, bf16[512,2048]{1,0:T(8,128)(2,1)}, u32[]{:S(2)}, u32[]{:S(2)}) collective-permute-start(bf16[512,2048]{1,0:T(8,128)(2,1)} %collective-permute-done.15.refs_2_), channel_id=1, source_target_pairs={{2,3},{6,7},{10,11},{14,15},{18,19},{22,23},{26,27},{30,31}} | collective-permute-start | bytes 6291464 | tf_op jit(solution)/shard_map/ppermute | solution.py:688
  260.3 50.6 %collective-permute-start.17 = (bf16[512,2048]{1,0:T(8,128)(2,1)S(1)}, bf16[512,2048]{1,0:T(8,128)(2,1)}, u32[]{:S(2)}, u32[]{:S(2)}) collective-permute-start(bf16[512,2048]{1,0:T(8,128)(2,1)S(1)} %collective-permute-done.14.refs_0_.refs_1_), channel_id=1, source_target_pairs={{1,0},{5,4},{9,8},{13,12},{17,16},{21,20},{25,24},{29,28}} | collective-permute-start | bytes 6291464 | tf_op jit(solution)/shard_map/ppermute | solution.py:689
  310.9 318.3 %reduce-scatter.5.cloned.1.call-start = ((), (), s32[]{:S(2)}) async-start(), calls=%async_computation.5 | async-start | bytes 10485760 | tf_op jit(solution)/shard_map/reduce_scatter | solution.py:847
  338.9 16.3 %collective-permute-start.18 = (bf16[4,2560,256]{2,1,0:T(8,128)(2,1)}, bf16[4,2560,256]{2,1,0:T(8,128)(2,1)}, u32[]{:S(2)}, u32[]{:S(2)}) collective-permute-start(bf16[4,2560,256]{2,1,0:T(8,128)(2,1)} %weight_grad_part.3), channel_id=1, source_target_pairs={{0,4},{4,0},{1,5},{5,1},{2,6},{6,2},{3,7},{7,3},{8,12},{12,8},{9,1... | collective-permute-start | bytes 15728648 | tf_op jit(solution)/shard_map/ppermute | solution.py:840
  376.3 47.0 %collective-permute-start.19 = (bf16[2,1280,256]{2,1,0:T(8,128)(2,1)}, bf16[2,1280,256]{2,1,0:T(8,128)(2,1)S(1)}, u32[]{:S(2)}, u32[]{:S(2)}) collective-permute-start(bf16[2,1280,256]{2,1,0:T(8,128)(2,1)} %get-tuple-element.188), channel_id=1, source_target_pairs={{0,8},{8,0},{16,24},{24,16},{1,9},{9,1},{17,25},{25,17},{2,10},{10... | collective-permute-start | bytes 3932168 | tf_op jit(solution)/shard_map/ppermute | solution.py:581
  377.8 45.5 %collective-permute-start.20 = (bf16[2,1280,256]{2,1,0:T(8,128)(2,1)}, bf16[2,1280,256]{2,1,0:T(8,128)(2,1)S(1)}, u32[]{:S(2)}, u32[]{:S(2)}) collective-permute-start(bf16[2,1280,256]{2,1,0:T(8,128)(2,1)} %get-tuple-element.199), channel_id=1, source_target_pairs={{0,16},{8,24},{16,0},{24,8},{1,17},{9,25},{17,1},{25,9},{2,18},{10... | collective-permute-start | bytes 3932168 | tf_op jit(solution)/shard_map/ppermute | solution.py:581
  379.3 45.1 %copy-start.38 = (bf16[1,1280,256]{2,1,0:T(8,128)(2,1)S(1)}, bf16[1,1280,256]{2,1,0:T(8,128)(2,1)}, u32[]{:S(2)}) copy-start(bf16[1,1280,256]{2,1,0:T(8,128)(2,1)} %get-tuple-element.202) | copy-start | bytes 1966084
  424.6 42.3 %collective-permute-start.21 = (bf16[1,1280,256]{2,1,0:T(8,128)(2,1)S(1)}, bf16[1,1280,256]{2,1,0:T(8,128)(2,1)S(1)}, u32[]{:S(2)}, u32[]{:S(2)}) collective-permute-start(bf16[1,1280,256]{2,1,0:T(8,128)(2,1)S(1)} %add_convert_fusion.2), channel_id=1, source_target_pairs={{0,16},{8,24},{16,0},{24,8},{1,17},{9,25},{17,1},{25,9},{2,18},{10... | collective-permute-start | bytes 1966088 | tf_op jit(solution)/shard_map/ppermute | solution.py:581
  425.9 41.0 %collective-permute-start.22 = (bf16[1,1280,256]{2,1,0:T(8,128)(2,1)}, bf16[1,1280,256]{2,1,0:T(8,128)(2,1)S(1)}, u32[]{:S(2)}, u32[]{:S(2)}) collective-permute-start(bf16[1,1280,256]{2,1,0:T(8,128)(2,1)} %add_convert_fusion.1), channel_id=1, source_target_pairs={{0,8},{8,0},{16,24},{24,16},{1,9},{9,1},{17,25},{25,17},{2,10},{10... | collective-permute-start | bytes 1966088 | tf_op jit(solution)/shard_map/ppermute | solution.py:581
  426.5 59.0 %collective-permute-start.23 = (bf16[4,256,2048]{2,1,0:T(8,128)(2,1)}, bf16[4,256,2048]{2,1,0:T(8,128)(2,1)}, u32[]{:S(2)}, u32[]{:S(2)}) collective-permute-start(bf16[4,256,2048]{2,1,0:T(8,128)(2,1)} %weight_grad.5), channel_id=1, source_target_pairs={{0,4},{4,0},{1,5},{5,1},{2,6},{6,2},{3,7},{7,3},{8,12},{12,8},{9,1... | collective-permute-start | bytes 12582920 | tf_op jit(solution)/shard_map/ppermute | solution.py:833
  479.1 26.7 %collective-permute-start.24 = (bf16[4,256,1536]{2,1,0:T(8,128)(2,1)}, bf16[4,256,1536]{2,1,0:T(8,128)(2,1)}, u32[]{:S(2)}, u32[]{:S(2)}) collective-permute-start(bf16[4,256,1536]{2,1,0:T(8,128)(2,1)} %weight_grad.7), channel_id=1, source_target_pairs={{0,4},{4,0},{1,5},{5,1},{2,6},{6,2},{3,7},{7,3},{8,12},{12,8},{9,1... | collective-permute-start | bytes 9437192 | tf_op jit(solution)/shard_map/ppermute | solution.py:833
  483.2 126.8 %copy-start.6 = (f32[1,1280,256]{2,1,0:T(8,128)}, f32[1,1280,256]{2,1,0:T(8,128)S(1)}, u32[]{:S(2)}) copy-start(f32[1,1280,256]{2,1,0:T(8,128)S(1)} %convert_add_fusion) | copy-start | bytes 3932164
  485.5 48.5 %copy-start.8 = (f32[1280,256]{1,0:T(8,128)}, f32[1280,256]{1,0:T(8,128)S(1)}, u32[]{:S(2)}) copy-start(f32[1280,256]{1,0:T(8,128)S(1)} %add_bitcast_fusion) | copy-start | bytes 3932164
  502.6 25.4 %collective-permute-start.29 = (bf16[2,128,2048]{2,1,0:T(8,128)(2,1)}, bf16[2,128,2048]{2,1,0:T(8,128)(2,1)}, u32[]{:S(2)}, u32[]{:S(2)}) collective-permute-start(bf16[2,128,2048]{2,1,0:T(8,128)(2,1)} %get-tuple-element.207), channel_id=1, source_target_pairs={{0,8},{8,0},{16,24},{24,16},{1,9},{9,1},{17,25},{25,17},{2,10},{10... | collective-permute-start | bytes 3145736 | tf_op jit(solution)/shard_map/ppermute | solution.py:581
  504.1 25.1 %copy-start.43 = (bf16[1,128,2048]{2,1,0:T(8,128)(2,1)S(1)}, bf16[1,128,2048]{2,1,0:T(8,128)(2,1)}, u32[]{:S(2)}) copy-start(bf16[1,128,2048]{2,1,0:T(8,128)(2,1)} %get-tuple-element.224) | copy-start | bytes 1572868
  504.1 26.9 %copy-start.42 = (bf16[1,128,2048]{2,1,0:T(8,128)(2,1)S(1)}, bf16[1,128,2048]{2,1,0:T(8,128)(2,1)}, u32[]{:S(2)}) copy-start(bf16[1,128,2048]{2,1,0:T(8,128)(2,1)} %get-tuple-element.221) | copy-start | bytes 1572868
  504.1 25.1 %collective-permute-start.30 = (bf16[2,128,2048]{2,1,0:T(8,128)(2,1)}, bf16[2,128,2048]{2,1,0:T(8,128)(2,1)}, u32[]{:S(2)}, u32[]{:S(2)}) collective-permute-start(bf16[2,128,2048]{2,1,0:T(8,128)(2,1)} %get-tuple-element.219), channel_id=1, source_target_pairs={{0,16},{8,24},{16,0},{24,8},{1,17},{9,25},{17,1},{25,9},{2,18},{10... | collective-permute-start | bytes 3145736 | tf_op jit(solution)/shard_map/ppermute | solution.py:581
  530.4 14.9 %collective-permute-start.32 = (bf16[1,128,2048]{2,1,0:T(8,128)(2,1)S(1)}, bf16[1,128,2048]{2,1,0:T(8,128)(2,1)S(1)}, u32[]{:S(2)}, u32[]{:S(2)}) collective-permute-start(bf16[1,128,2048]{2,1,0:T(8,128)(2,1)S(1)} %add_convert_fusion.3), channel_id=1, source_target_pairs={{0,8},{8,0},{16,24},{24,16},{1,9},{9,1},{17,25},{25,17},{2,10},{10... | collective-permute-start | bytes 1572872 | tf_op jit(solution)/shard_map/ppermute | solution.py:581
  531.0 14.3 %copy-start.41 = (bf16[1,128,2048]{2,1,0:T(8,128)(2,1)S(1)}, bf16[1,128,2048]{2,1,0:T(8,128)(2,1)}, u32[]{:S(2)}) copy-start(bf16[1,128,2048]{2,1,0:T(8,128)(2,1)} %get-tuple-element.222) | copy-start | bytes 1572868
  532.4 14.9 %collective-permute-start.31 = (bf16[1,128,2048]{2,1,0:T(8,128)(2,1)S(1)}, bf16[1,128,2048]{2,1,0:T(8,128)(2,1)S(1)}, u32[]{:S(2)}, u32[]{:S(2)}) collective-permute-start(bf16[1,128,2048]{2,1,0:T(8,128)(2,1)S(1)} %add_convert_fusion.4), channel_id=1, source_target_pairs={{0,16},{8,24},{16,0},{24,8},{1,17},{9,25},{17,1},{25,9},{2,18},{10... | collective-permute-start | bytes 1572872 | tf_op jit(solution)/shard_map/ppermute | solution.py:581
  535.1 24.9 %collective-permute-start.25 = (bf16[2,128,1536]{2,1,0:T(8,128)(2,1)S(1)}, bf16[2,128,1536]{2,1,0:T(8,128)(2,1)S(1)}, u32[]{:S(2)}, u32[]{:S(2)}) collective-permute-start(bf16[2,128,1536]{2,1,0:T(8,128)(2,1)S(1)} %copy-done.59), channel_id=1, source_target_pairs={{0,8},{8,0},{16,24},{24,16},{1,9},{9,1},{17,25},{25,17},{2,10},{10... | collective-permute-start | bytes 2359304 | tf_op jit(solution)/shard_map/ppermute | solution.py:581
  536.8 24.9 %collective-permute-start.26 = (bf16[2,128,1536]{2,1,0:T(8,128)(2,1)S(1)}, bf16[2,128,1536]{2,1,0:T(8,128)(2,1)S(1)}, u32[]{:S(2)}, u32[]{:S(2)}) collective-permute-start(bf16[2,128,1536]{2,1,0:T(8,128)(2,1)S(1)} %copy-done.58), channel_id=1, source_target_pairs={{0,16},{8,24},{16,0},{24,8},{1,17},{9,25},{17,1},{25,9},{2,18},{10... | collective-permute-start | bytes 2359304 | tf_op jit(solution)/shard_map/ppermute | solution.py:581
  547.3 14.4 %copy-start.45 = (bf16[1,128,1536]{2,1,0:T(8,128)(2,1)S(1)}, bf16[1,128,1536]{2,1,0:T(8,128)(2,1)}, u32[]{:S(2)}) copy-start(bf16[1,128,1536]{2,1,0:T(8,128)(2,1)} %get-tuple-element.216) | copy-start | bytes 1179652
  548.6 14.8 %copy-start.12 = (f32[128,2048]{1,0:T(8,128)}, f32[128,2048]{1,0:T(8,128)S(1)}, u32[]{:S(2)}) copy-start(f32[128,2048]{1,0:T(8,128)S(1)} %add_bitcast_fusion.2) | copy-start | bytes 3145732
  548.6 14.7 %copy-start.44 = (bf16[1,128,1536]{2,1,0:T(8,128)(2,1)S(1)}, bf16[1,128,1536]{2,1,0:T(8,128)(2,1)}, u32[]{:S(2)}) copy-start(bf16[1,128,1536]{2,1,0:T(8,128)(2,1)} %get-tuple-element.213) | copy-start | bytes 1179652
  548.6 22.1 %copy-start.47 = (bf16[1,128,1536]{2,1,0:T(8,128)(2,1)S(1)}, bf16[1,128,1536]{2,1,0:T(8,128)(2,1)}, u32[]{:S(2)}) copy-start(bf16[1,128,1536]{2,1,0:T(8,128)(2,1)} %get-tuple-element.214) | copy-start | bytes 1179652
  561.8 8.9 %collective-permute-start.28 = (bf16[1,128,1536]{2,1,0:T(8,128)(2,1)S(1)}, bf16[1,128,1536]{2,1,0:T(8,128)(2,1)S(1)}, u32[]{:S(2)}, u32[]{:S(2)}) collective-permute-start(bf16[1,128,1536]{2,1,0:T(8,128)(2,1)S(1)} %add_convert_fusion.5), channel_id=1, source_target_pairs={{0,8},{8,0},{16,24},{24,16},{1,9},{9,1},{17,25},{25,17},{2,10},{10... | collective-permute-start | bytes 1179656 | tf_op jit(solution)/shard_map/ppermute | solution.py:581
  563.4 8.5 %collective-permute-start.27 = (bf16[1,128,1536]{2,1,0:T(8,128)(2,1)S(1)}, bf16[1,128,1536]{2,1,0:T(8,128)(2,1)S(1)}, u32[]{:S(2)}, u32[]{:S(2)}) collective-permute-start(bf16[1,128,1536]{2,1,0:T(8,128)(2,1)S(1)} %add_convert_fusion.6), channel_id=1, source_target_pairs={{0,16},{8,24},{16,0},{24,8},{1,17},{9,25},{17,1},{25,9},{2,18},{10... | collective-permute-start | bytes 1179656 | tf_op jit(solution)/shard_map/ppermute | solution.py:581
  572.0 13.8 %copy-start.61 = (f32[96]{0:T(128)S(1)}, f32[96]{0:T(128)}, u32[]{:S(2)}) copy-start(f32[96]{0:T(128)} %copy-done.60) | copy-start | bytes 1156
  572.0 22.6 %copy-start.1 = (bf16[512,2048]{1,0:T(8,128)(2,1)S(1)}, bf16[512,2048]{1,0:T(8,128)(2,1)}, u32[]{:S(2)}) copy-start(bf16[512,2048]{1,0:T(8,128)(2,1)} %x_ref.1) | copy-start | bytes 6291460
  576.7 1.3 collective-permute-start.33
  578.0 4.3 collective-permute-start.35
  579.7 5.5 collective-permute-start.36
  580.5 4.7 collective-permute-start.34
  585.2 17.7 %copy-start.39 = (f32[125,128]{1,0:T(8,128)}, f32[125,128]{1,0:T(8,128)S(1)}, u32[]{:S(2)}) copy-start(f32[125,128]{1,0:T(8,128)S(1)} %add_add_fusion) | copy-start | bytes 192004
  586.5 15.8 %collective-permute-start.38 = (f32[97,128]{1,0:T(8,128)S(1)}, f32[97,128]{1,0:T(8,128)S(1)}, u32[]{:S(2)}, u32[]{:S(2)}) collective-permute-start(f32[97,128]{1,0:T(8,128)S(1)} %slice_add_fusion), channel_id=1, source_target_pairs={{0,2},{1,3},{2,0},{3,1},{4,6},{5,7},{6,4},{7,5},{8,10},{9,11},{10,... | collective-permute-start | bytes 149000 | tf_op jit(solution)/shard_map/ppermute | solution.py:714
  594.0 8.4 %collective-permute-start.39 = (f32[97,128]{1,0:T(8,128)S(1)}, f32[97,128]{1,0:T(8,128)S(1)}, u32[]{:S(2)}, u32[]{:S(2)}) collective-permute-start(f32[97,128]{1,0:T(8,128)S(1)} %slice_add_fusion), channel_id=1, source_target_pairs={{0,3},{1,2},{2,1},{3,0},{4,7},{5,6},{6,5},{7,4},{8,11},{9,10},{10,... | collective-permute-start | bytes 149000 | tf_op jit(solution)/shard_map/ppermute | solution.py:714
  594.0 9.0 %collective-permute-start.37 = (f32[97,128]{1,0:T(8,128)S(1)}, f32[97,128]{1,0:T(8,128)S(1)}, u32[]{:S(2)}, u32[]{:S(2)}) collective-permute-start(f32[97,128]{1,0:T(8,128)S(1)} %slice_add_fusion), channel_id=1, source_target_pairs={{0,1},{1,0},{2,3},{3,2},{4,5},{5,4},{6,7},{7,6},{8,9},{9,8},{10,11... | collective-permute-start | bytes 149000 | tf_op jit(solution)/shard_map/ppermute | solution.py:714
  594.6 13.8 %copy-start.48 = (f32[2048]{0:T(1024)S(1)}, f32[2048]{0:T(1024)}, u32[]{:S(2)}) copy-start(f32[2048]{0:T(1024)} %param.40) | copy-start | bytes 24580
  (42 other events, 239.2 us)
Sparse Core Ops, SparseCore 0:
  10.9 83.6 all-gather.2
  97.1 65.3 all-gather.4
  311.0 148.6 reduce-scatter.2
  467.0 152.9 reduce-scatter.4

commit v3 on v2

--- a/solution.py
+++ b/solution.py
@@ -473,7 +473,7 @@
             out_specs=row,
         ),
         out_shape=shape((rows, D), BF16),
-        compiler_params=params(32),
+        compiler_params=params(60),
         cost_estimate=cost(20 * rows * D, 8 * rows * D),
         name="finish",
     )(place, grad, back, x, stat)
@@ -727,6 +727,38 @@
     return (weight_new, first_new, second_new)
 
 
+def adam_kernel(rates, factor_ref, *refs):
+    ins, outs = refs[: 4 * len(rates)], refs[4 * len(rates) :]
+    factor = factor_ref[0]
+    for i, rate in enumerate(rates):
+        weight, grad, first, second = (r[...] for r in ins[4 * i : 4 * i + 4])
+        for ref, new in zip(outs[3 * i : 3 * i + 3], adam_step(weight, factor * grad, first, second, rate, DECAY)):
+            ref[...] = new
+
+
+def adam_all(factor, groups):
+    steps = 8
+    in_specs, out_specs, out_shape, args = [], [], [], []
+    for weight, grad, low, first, second, _ in groups:
+        rows, cols = weight.shape[0] // steps, weight.shape[1]
+        spec = pl.BlockSpec((rows, cols), lambda i, p: (i, 0))
+        shifted = pl.BlockSpec((rows, cols), lambda i, p, at=low // rows: (at + i, 0))
+        in_specs += [spec, shifted, spec, spec]
+        args += [weight, grad, first, second]
+        out_specs += [spec] * 3
+        out_shape += [shape(weight.shape, F32)] * 3
+    return pl.pallas_call(
+        functools.partial(adam_kernel, [g[-1] for g in groups]),
+        grid_spec=pltpu.PrefetchScalarGridSpec(
+            num_scalar_prefetch=1, grid=(steps,), in_specs=in_specs, out_specs=out_specs
+        ),
+        out_shape=out_shape,
+        compiler_params=params(60),
+        cost_estimate=cost(0, 28 * sum(g[0].size for g in groups)),
+        name="adam",
+    )(factor, *args)
+
+
 def rotation_tables(position):
     half = ROT // 2
     inverse = ROPE_BASE ** (-jnp.arange(half, dtype=F32) * 2.0 / ROT)
@@ -852,7 +884,6 @@
     sum_inner.rest()
     part_up, part_qkv, sum_second = sum_up.total(), sum_inner.total(), sum_second.total()
     units = act.shape[1]
-    part_down, part_out = sum_second[:units], sum_second[units:]
     token_vals = tokens.astype(F32)
     layer_out = (token_vals + branch.astype(F32) + norm_vec[4] + norm_vec[5]).astype(BF16)
 
@@ -861,9 +892,8 @@
     small = jnp.concatenate([col[0:4], out_bias[None], out_bias[None]], axis=0)
     local_squares = (
         jnp.sum(part_qkv * part_qkv)
-        + jnp.sum(part_out * part_out)
         + jnp.sum(part_up * part_up)
-        + jnp.sum(part_down * part_down)
+        + jnp.sum(sum_second * sum_second)
     )
     squares = jnp.broadcast_to(local_squares, (128,))
     packed = jnp.concatenate([grad_bqkv, grad_bup, small.reshape(-1), squares]).reshape(-1, 128)
@@ -883,11 +913,17 @@
     factor = jnp.minimum(1.0, CLIP_NORM / (grad_norm + 1e-06))
     rate_big = 2.5 * D ** (-0.5)
     rate_out = 2.5 * max(16 * D // GROUP_TOK, 1) ** (-0.5)
-    upd_qkv, mom_qkv, sec_qkv = adam_step(w_qkv, factor * part_qkv, m_qkv, v_qkv, rate_big, DECAY)
-    upd_out, mom_out, sec_out = adam_step(w_out, factor * part_out, m_out, v_out, rate_out, DECAY)
-    upd_up, mom_up, sec_up = adam_step(w_up, factor * part_up, m_up, v_up, rate_big, DECAY)
-    upd_down, mom_down, sec_down = adam_step(
-        w_down, factor * part_down, m_down, v_down, rate_big, DECAY
+    (
+        upd_qkv, mom_qkv, sec_qkv, upd_out, mom_out, sec_out,
+        upd_up, mom_up, sec_up, upd_down, mom_down, sec_down,
+    ) = adam_all(
+        factor.reshape(1),
+        (
+            (w_qkv, part_qkv, 0, m_qkv, v_qkv, rate_big),
+            (w_out, sum_second, units, m_out, v_out, rate_out),
+            (w_up, part_up, 0, m_up, v_up, rate_big),
+            (w_down, sum_second, 0, m_down, v_down, rate_big),
+        ),
     )
     upd_norm, mom_norm, sec_norm = adam_step(
         norm_vec, factor * grad_small, m_norm, v_norm, RATE_SMALL, 0.0

time: 651 us -> 645 us (level)
  Pallas kernels: 365 us -> 385 us
  other arithmetic: 58.1 us -> 43 us
  local copies, waits for them, and re-layouts: 24.6 us -> 15.7 us
    pallas_call x0 -> x1, Pallas kernels: none -> 17.8 us  [adam_all(): pl.pallas_call(functools.partial(adam_kernel, [g[-1] for g in groups]), g...]
    sub x7 -> x3, other arithmetic: 19.2 us -> 1.95 us  [adam_step(): weight - rate * (first_hat / (jnp.sqrt(second_hat) + ADAM_EPS) + decay *...]
    unnamed x124 -> x76, local copies, waits for them, and re-layouts: 10.4 us -> 2.35 us
    concatenate x0 -> x3, other arithmetic: none -> 7.2 us  [total(): jnp.concatenate([self.add(held[0])[0] for _, held in self.lanes], axis=0)]
  transfers between devices with their start and end apart: 44 -> 44, of which waited for: 20 -> 21; matrix products, arithmetic and copies ran while one was open for 11% -> 8% of each run, Pallas kernels for 56% -> 60%
where the time goes in v3:
time: 645 us; the launch traced here: 637 us
  Pallas kernels  385 us (60%)
  waiting for transfers between devices  106 us (16%)
  starting transfers between devices  66.6 us (10%)
  other arithmetic  43 us (7%)
  between operations  20.9 us (3%)
  local copies, waits for them, and re-layouts  15.7 us (2%)
    pallas_call x5, Pallas kernels, wgrad(): pl.pallas_call(functools.partial(wgrad_kernel, len(lefts), len(rights), c...  79.5 us
    pallas_call x3, Pallas kernels, enter(): pl.pallas_call(functools.partial(enter_kernel, many, units), grid_spec=pl...  73.9 us
    pallas_call x3, Pallas kernels, leave(): pl.pallas_call(functools.partial(leave_kernel, many, units), grid_spec=pl...  46.6 us
    pallas_call x1, Pallas kernels, attn_bwd(): pl.pallas_call(functools.partial(attn_bwd_kernel, cases, width), grid=(he...  44 us
    pallas_call x1, Pallas kernels, din_all(): pl.pallas_call(din_kernel, grid=(D // tile, group // rows), in_specs=[pl....  40.3 us
    ppermute x9, waiting for transfers between devices, step(): lax.ppermute(there, 'mp', [(i + 1, i) for i in range(0, count - step)])  37.4 us
    ppermute x12, waiting for transfers between devices, hand(): lax.ppermute(stack, 'quad', [(i, i ^ 1 << bit) for i in range(self.quads)])  35.3 us
    pallas_call x1, Pallas kernels, branch_all(): pl.pallas_call(functools.partial(branch_kernel, units), grid=(D // tile,...  28.2 us
  transfers between devices with their start and end apart: 44, of which 21 were waited for; matrix products, arithmetic and copies ran while one was open for 8% of the time, Pallas kernels for 60%

profile of v3, /device:TPU:0, one launch (start us, length us, event | category | flops | bytes accessed | tf_op | source)
XLA Modules:
  0.0 637.3 jit_solution(4431893463682152333)
XLA Ops:
  7.2 1.6 convert_element_type.148
  12.8 5.0 collective-permute-start
  19.1 21.0 %collective-permute-done.refs_3_ = bf16[256,2048]{1,0:T(8,128)(2,1)S(1)} collective-permute-done((bf16[256,2048]{1,0:T(8,128)(2,1)S(1)}, bf16[256,2048]{1,0:T(8,128)(2,1)S(1)}, u32[]{:S(2)}, u32[]{:S(2)}) %collective-permute-start) | collective-permute-done | bytes 1048608 | tf_op jit(solution)/shard_map/ppermute | solution.py:688
  41.1 3.3 collective-permute-done.1.refs_2_.refs_1_
  45.8 4.4 collective-permute-start.5
  60.5 2.8 convert_reduce_fusion
  65.4 3.7 multiply_sine_fusion
  69.2 2.5 maximum_maximum_fusion.2
  71.7 6.8 %collective-permute-done.4.refs_4_ = bf16[256,2048]{1,0:T(8,128)(2,1)} collective-permute-done((bf16[256,2048]{1,0:T(8,128)(2,1)}, bf16[256,2048]{1,0:T(8,128)(2,1)}, u32[]{:S(2)}, u32[]{:S(2)}) %collective-permute-start.4) | collective-permute-done | bytes 1048608 | tf_op jit(solution)/shard_map/ppermute | solution.py:689
  78.5 1.6 collective-permute-start.7
  81.4 19.5 %collective-permute-done.3.refs_0_.refs_1_ = bf16[256,2048]{1,0:T(8,128)(2,1)} collective-permute-done((bf16[256,2048]{1,0:T(8,128)(2,1)}, bf16[256,2048]{1,0:T(8,128)(2,1)}, u32[]{:S(2)}, u32[]{:S(2)}) %collective-permute-start.3) | collective-permute-done | bytes 1048608 | tf_op jit(solution)/shard_map/ppermute | solution.py:689
  101.0 1.7 collective-permute-start.8
  102.6 1.5 collective-permute-start.9
  104.1 32.5 %enter.3 = (bf16[2048,2048]{1,0:T(8,128)(2,1)}, bf16[2048,2048]{1,0:T(8,128)(2,1)}, bf16[2048,2048]{1,0:T(8,128)(2,1)}, f32[2048,128]{1,0:T(8,128)}, bf16[2048,2...) custom-call(s32[4,3]{1,0:T(4,128)} %dynamic-slice_bitcast_fusion.1.table, ...), custom_call_target="tpu_custom_call" | custom-call | flops 15032385536 | bytes 14680064 | tf_op jit(solution)/shard_map/enter/pallas_call | solution.py:144
  136.7 1.7 collective-permute-start.10
  139.7 20.9 %enter.4 = (bf16[2048,2048]{1,0:T(8,128)(2,1)}, bf16[2048,2048]{1,0:T(8,128)(2,1)}, bf16[2048,2048]{1,0:T(8,128)(2,1)}, f32[2048,128]{1,0:T(8,128)}, bf16[2048,2...) custom-call(s32[2,3]{1,0:T(2,128)} %fusion.9.table, ...), custom_call_target="tpu_custom_call", output_to_operand_aliasing={{0}: (14, {}), {1}: (15, {}), {2}: (16, {}), {3}: (17, {}),... | custom-call | flops 7516192768 | bytes 14680064 | tf_op jit(solution)/shard_map/enter/pallas_call | solution.py:144
  160.6 7.8 %collective-permute-start.13 = (bf16[512,2048]{1,0:T(8,128)(2,1)S(1)}, bf16[512,2048]{1,0:T(8,128)(2,1)}, u32[]{:S(2)}, u32[]{:S(2)}) collective-permute-start(bf16[512,2048]{1,0:T(8,128)(2,1)S(1)} %get-tuple-element.175.refs_0_.e_ref), channel_id=1, source_target_pairs={{0,1},{1,2},{2,3},{4,5},{5,6},{6,7},{8,9},{9,10},{10,11},{12,13},{... | collective-permute-start | bytes 6291464 | tf_op jit(solution)/shard_map/ppermute | solution.py:688
  168.5 1.5 collective-permute-start.12
  173.1 20.5 %enter.5 = (bf16[2048,2048]{1,0:T(8,128)(2,1)}, bf16[2048,2048]{1,0:T(8,128)(2,1)}, bf16[2048,2048]{1,0:T(8,128)(2,1)}, f32[2048,128]{1,0:T(8,128)}, bf16[2048,2...) custom-call(s32[2,3]{1,0:T(2,128)} %fusion.8.table, ...), custom_call_target="tpu_custom_call", output_to_operand_aliasing={{0}: (16, {}), {1}: (17, {}), {2}: (18, {}), {3}: (19, {}),... | custom-call | flops 7516192768 | bytes 14680064 | tf_op jit(solution)/shard_map/enter/pallas_call | solution.py:144
  193.6 11.4 %attend.2 = (bf16[2048,512]{1,0:T(8,128)(2,1)}, f32[4,1,2048]{2,1,0:T(1,128)}) custom-call(bf16[2048,1536]{1,0:T(8,128)(2,1)} %get-tuple-element.166.q_ref.k_ref.v_ref, bf16[2048,1536]{1,0:T(8,128)(2,1)} %get-tuple-element.166.q_ref.k_ref.v_ref, bf16[2048,1536]{1,0:T(8,128)(2,1)} %get-tuple-element.166.q_ref.k_ref.v_ref, ...), custom_call_target="tpu_custom_call" | custom-call | flops 10737418240 | bytes 4194304 | tf_op jit(solution)/shard_map/attend/pallas_call | solution.py:219
  205.0 2.1 collective-permute-done.13.refs_2_
  207.1 6.9 %collective-permute-done.12.refs_1_ = bf16[512,2048]{1,0:T(8,128)(2,1)} collective-permute-done((bf16[512,2048]{1,0:T(8,128)(2,1)S(1)}, bf16[512,2048]{1,0:T(8,128)(2,1)}, u32[]{:S(2)}, u32[]{:S(2)}) %collective-permute-start.12) | collective-permute-done | bytes 2097184 | tf_op jit(solution)/shard_map/ppermute | solution.py:689
  215.4 2.2 collective-permute-start.15
  217.6 11.4 %attend.3 = (bf16[2048,512]{1,0:T(8,128)(2,1)}, f32[4,1,2048]{2,1,0:T(1,128)}) custom-call(bf16[2048,1536]{1,0:T(8,128)(2,1)} %get-tuple-element.166.q_ref.k_ref.v_ref, bf16[2048,1536]{1,0:T(8,128)(2,1)} %get-tuple-element.166.q_ref.k_ref.v_ref, ...), custom_call_target="tpu_custom_call", output_to_operand_aliasing={{0}: (4, {}), {1}: (5, {})} | custom-call | flops 10737418240 | bytes 4194304 | tf_op jit(solution)/shard_map/attend/pallas_call | solution.py:219
  229.0 28.2 %branch.1 = bf16[2048,2048]{1,0:T(8,128)(2,1)} custom-call(bf16[2048,512]{1,0:T(8,128)(2,1)} %get-tuple-element.169.o_ref.refs_1_, bf16[2048,2048]{1,0:T(8,128)(2,1)} %get-tuple-element.170.act_ref.refs_0_, bf16[2560,2048]{1,0:T(8,128)(2,1)} %all-gather.5.cloned.1.call-done.w_ref.refs_3_.refs_4_), custom_call_target="tpu_custom_call" | custom-call | flops 21474836480 | bytes 10485760 | tf_op jit(solution)/shard_map/branch/pallas_call | solution.py:333
  258.1 2.0 collective-permute-start.16
  260.1 1.7 collective-permute-start.17
  261.8 19.8 %leave.3 = (bf16[2048,2048]{1,0:T(8,128)(2,1)}, bf16[2048,2048]{1,0:T(8,128)(2,1)}, bf16[2048,512]{1,0:T(8,128)(2,1)}, f32[8,2048]{1,0:T(8,128)}) custom-call(s32[4,3]{1,0:T(4,128)} %dynamic-slice_bitcast_fusion.table, bf16[512,2048]{1,0:T(8,128)(2,1)} %copy-done.2, bf16[512,2048]{1,0:T(8,128)(2,1)} %collective-permute-done.12.refs_1_, ...), custom_call_target="tpu_custom_call" | custom-call | flops 10737418240 | bytes 10485760 | tf_op jit(solution)/shard_map/leave/pallas_call | solution.py:386
  281.6 13.4 %leave.4 = (bf16[2048,2048]{1,0:T(8,128)(2,1)}, bf16[2048,2048]{1,0:T(8,128)(2,1)}, bf16[2048,512]{1,0:T(8,128)(2,1)}, f32[8,2048]{1,0:T(8,128)}) custom-call(s32[2,3]{1,0:T(2,128)} %fusion.10.table, bf16[512,2048]{1,0:T(8,128)(2,1)} %copy-done.3, ...), custom_call_target="tpu_custom_call", output_to_operand_aliasing={{0}: (6, {}), {1}: (7, {}), {2}: (8, {})} | custom-call | flops 5368709120 | bytes 10485760 | tf_op jit(solution)/shard_map/leave/pallas_call | solution.py:386
  295.1 15.8 %weight_grad_part.2.refs_3_ = f32[4,2560,256]{2,1,0:T(8,128)} custom-call(s32[5]{0:T(128)} %pad_add_fusion.place, bf16[2048,2048]{1,0:T(8,128)(2,1)} %get-tuple-element.170.act_ref.refs_0_, bf16[2048,512]{1,0:T(8,128)(2,1)} %get-tuple-element.169.o_ref.refs_1_, bf16[2048,2048]{1,0:T(8,128)(2,1)} %get-tuple-element.187.refs_2_.refs_3_.refs_4_.refs_6_, ...), custom_call_target="tpu_custom_call" | custom-call | flops 8053063680 | tf_op jit(solution)/shard_map/weight_grad_part/pallas_call | solution.py:643
  314.2 13.4 %leave.5 = (bf16[2048,2048]{1,0:T(8,128)(2,1)}, bf16[2048,2048]{1,0:T(8,128)(2,1)}, bf16[2048,512]{1,0:T(8,128)(2,1)}, f32[8,2048]{1,0:T(8,128)}) custom-call(s32[2,3]{1,0:T(2,128)} %fusion.11.table, bf16[512,2048]{1,0:T(8,128)(2,1)} %collective-permute-done.17.refs_0_, ...), custom_call_target="tpu_custom_call", output_to_operand_aliasing={{0}: (7, {}), {1}: (8, {}), {2}: (9, {})} | custom-call | flops 5368709120 | bytes 10485760 | tf_op jit(solution)/shard_map/leave/pallas_call | solution.py:386
  327.6 11.0 %weight_grad_part.3 = bf16[4,2560,256]{2,1,0:T(8,128)(2,1)} custom-call(s32[3]{0:T(128)} %pad_add_fusion.3.place, bf16[2048,2048]{1,0:T(8,128)(2,1)} %get-tuple-element.170.act_ref.refs_0_, bf16[2048,512]{1,0:T(8,128)(2,1)} %get-tuple-element.169.o_ref.refs_1_, bf16[2048,2048]{1,0:T(8,128)(2,1)} %get-tuple-element.196.refs_2_, ...), custom_call_target="tpu_custom_call" | custom-call | flops 2684354560 | tf_op jit(solution)/shard_map/weight_grad_part/pallas_call | solution.py:643
  339.9 15.0 %weight_grad.5 = bf16[4,256,2048]{2,1,0:T(8,128)(2,1)} custom-call(s32[2]{0:T(128)} %pad_add_fusion.2.place, bf16[2048,2048]{1,0:T(8,128)(2,1)} %get-tuple-element.198.refs_0_, bf16[2048,2048]{1,0:T(8,128)(2,1)} %get-tuple-element.194.refs_1_.dh_ref), custom_call_target="tpu_custom_call" | custom-call | flops 429496736 | tf_op jit(solution)/shard_map/weight_grad/pallas_call | solution.py:559
  354.9 21.2 %weight_grad.6 = (bf16[2,1280,256]{2,1,0:T(8,128)(2,1)}, bf16[1,1280,256]{2,1,0:T(8,128)(2,1)}, bf16[1,1280,256]{2,1,0:T(8,128)(2,1)}, bf16[2,1280,256]{2,1,0:T(...) custom-call(s32[2]{0:T(128)} %pad_add_fusion.1.place, ...), custom_call_target="tpu_custom_call" | custom-call | flops 536870912 | tf_op jit(solution)/shard_map/weight_grad/pallas_call | solution.py:559
  376.1 1.6 collective-permute-start.19
  377.7 1.4 collective-permute-start.20
  379.1 44.0 %attend_back.1 = (bf16[2048,1536]{1,0:T(8,128)(2,1)}, f32[8,1536]{1,0:T(8,128)}) custom-call(bf16[2048,1536]{1,0:T(8,128)(2,1)} %get-tuple-element.166.q_ref.k_ref.v_ref, bf16[2048,1536]{1,0:T(8,128)(2,1)} %get-tuple-element.166.q_ref.k_ref.v_ref, bf16[2048,1536]{1,0:T(8,128)(2,1)} %get-tuple-element.166.q_ref.k_ref.v_ref, ...), custom_call_target="tpu_custom_call" | custom-call | flops 134217728 | tf_op jit(solution)/shard_map/attend_back/pallas_call | solution.py:299
  426.0 40.3 %input_back.1 = (bf16[2048,2048]{1,0:T(8,128)(2,1)}, f32[8,2048]{1,0:T(8,128)}) custom-call(bf16[2048,1536]{1,0:T(8,128)(2,1)} %get-tuple-element.203.dm_ref.refs_1_, bf16[2048,2048]{1,0:T(8,128)(2,1)} %get-tuple-element.194.refs_1_.dh_ref, bf16[2048,3584]{1,0:T(8,128)(2,1)} %all-gather.3.cloned.1.call-done.refs_7_.refs_9_.w_ref, ...), custom_call_target="tpu_custom_call" | custom-call | flops 300647712 | tf_op jit(solution)/shard_map/input_back/pallas_call | solution.py:431
  466.4 12.2 %weight_grad.7 = bf16[4,256,1536]{2,1,0:T(8,128)(2,1)} custom-call(s32[2]{0:T(128)} %pad_add_fusion.2.place, bf16[2048,2048]{1,0:T(8,128)(2,1)} %get-tuple-element.217.refs_0_, bf16[2048,1536]{1,0:T(8,128)(2,1)} %get-tuple-element.203.dm_ref.refs_1_), custom_call_target="tpu_custom_call" | custom-call | flops 103079215104 | tf_op jit(solution)/shard_map/weight_grad/pallas_call | solution.py:559
  481.0 1.5 add_bitcast_fusion
  483.9 17.1 %weight_grad.8 = (bf16[2,128,2048]{2,1,0:T(8,128)(2,1)}, bf16[1,128,2048]{2,1,0:T(8,128)(2,1)}, bf16[1,128,2048]{2,1,0:T(8,128)(2,1)}, bf16[2,128,2048]{2,1,0:T(...) custom-call(s32[2]{0:T(128)} %pad_add_fusion.1.place, ...), custom_call_target="tpu_custom_call" | custom-call | flops 429496736 | tf_op jit(solution)/shard_map/weight_grad/pallas_call | solution.py:559
  501.1 1.6 collective-permute-start.29
  502.6 1.7 collective-permute-start.30
  504.3 14.0 %weight_grad.9 = (bf16[2,128,1536]{2,1,0:T(8,128)(2,1)}, bf16[1,128,1536]{2,1,0:T(8,128)(2,1)}, bf16[1,128,1536]{2,1,0:T(8,128)(2,1)}, bf16[2,128,1536]{2,1,0:T(...) custom-call(s32[2]{0:T(128)} %pad_add_fusion.1.place, ...), custom_call_target="tpu_custom_call" | custom-call | flops 25769803776 | tf_op jit(solution)/shard_map/weight_grad/pallas_call | solution.py:559
  518.3 8.0 %collective-permute-done.29 = bf16[2,128,2048]{2,1,0:T(8,128)(2,1)S(1)} collective-permute-done((bf16[2,128,2048]{2,1,0:T(8,128)(2,1)}, bf16[2,128,2048]{2,1,0:T(8,128)(2,1)S(1)}, u32[]{:S(2)}, u32[]{:S(2)}) %collective-permute-start.29) | collective-permute-done | bytes 1048608 | tf_op jit(solution)/shard_map/ppermute | solution.py:581
  530.8 1.6 collective-permute-start.31
  532.4 2.7 pad_maximum_fusion
  535.1 1.7 collective-permute-start.25
  537.1 6.9 %collective-permute-done.32 = bf16[1,128,2048]{2,1,0:T(8,128)(2,1)S(1)} collective-permute-done((bf16[1,128,2048]{2,1,0:T(8,128)(2,1)S(1)}, bf16[1,128,2048]{2,1,0:T(8,128)(2,1)S(1)}, u32[]{:S(2)}, u32[]{:S(2)}) %collective-permute-start.32) | collective-permute-done | bytes 524320 | tf_op jit(solution)/shard_map/ppermute | solution.py:581
  546.0 2.4 pad_maximum_fusion.1
  548.4 10.3 %collective-permute-done.25 = bf16[2,128,1536]{2,1,0:T(8,128)(2,1)S(1)} collective-permute-done((bf16[2,128,1536]{2,1,0:T(8,128)(2,1)S(1)}, bf16[2,128,1536]{2,1,0:T(8,128)(2,1)S(1)}, u32[]{:S(2)}, u32[]{:S(2)}) %collective-permute-start.25) | collective-permute-done | bytes 786464 | tf_op jit(solution)/shard_map/ppermute | solution.py:581
  558.6 1.6 collective-permute-done.26
  560.3 1.5 collective-permute-start.28
  561.9 1.7 collective-permute-start.27
  563.7 5.6 collective-permute-done.28
  570.7 2.1 pad_maximum_fusion.3
  576.1 1.7 collective-permute-start.35
  580.4 2.9 collective-permute-done.36
  584.7 7.3 %collective-permute-start.38 = (f32[97,128]{1,0:T(8,128)S(1)}, f32[97,128]{1,0:T(8,128)S(1)}, u32[]{:S(2)}, u32[]{:S(2)}) collective-permute-start(f32[97,128]{1,0:T(8,128)S(1)} %slice_add_fusion), channel_id=1, source_target_pairs={{0,2},{1,3},{2,0},{3,1},{4,6},{5,7},{6,4},{7,5},{8,10},{9,11},{10,... | collective-permute-start | bytes 149000 | tf_op jit(solution)/shard_map/ppermute | solution.py:714
  592.7 3.8 add_convert_fusion
  596.5 2.0 collective-permute-done.38
  599.7 1.9 collective-permute-done.37
  604.3 17.8 %adam.1 = (f32[256,1536]{1,0:T(8,128)}, f32[256,1536]{1,0:T(8,128)}, f32[256,1536]{1,0:T(8,128)}, f32[512,256]{1,0:T(8,128)}, f32[512,256]{1,0:T(8,128)}, /*inde...) custom-call(f32[1]{0:T(128)} %bitcast.27.factor_ref, ...), custom_call_target="tpu_custom_call" | custom-call | bytes 44040192 | tf_op jit(solution)/shard_map/adam/pallas_call | solution.py:750
  624.1 4.9 finish.1
  (195 shorter events, 56.4 us)
Async XLA Ops:
  7.2 96.9 %all-gather.3.cloned.1.call-start = ((), (), s32[]{:S(2)}) async-start(), calls=%async_computation.2 | async-start | bytes 16515072 | tf_op jit(solution)/shard_map/all_gather | solution.py:807
  10.8 33.6 %copy-start.7 = (f32[512,256]{1,0:T(8,128)S(1)}, f32[512,256]{1,0:T(8,128)}, u32[]{:S(2)}) copy-start(f32[512,256]{1,0:T(8,128)} %refs_4_.1) | copy-start | bytes 1572868
  10.8 218.2 %all-gather.5.cloned.1.call-start = ((), (), s32[]{:S(2)}) async-start(), calls=%async_computation.3 | async-start | bytes 11796480 | tf_op jit(solution)/shard_map/all_gather | solution.py:810
  11.7 32.8 %copy-start.5 = (f32[2048,256]{1,0:T(8,128)S(1)}, f32[2048,256]{1,0:T(8,128)}, u32[]{:S(2)}) copy-start(f32[2048,256]{1,0:T(8,128)} %refs_12_.1) | copy-start | bytes 6291460
  12.8 31.6 %copy-start.9 = (bf16[256,2048]{1,0:T(8,128)(2,1)}, bf16[256,2048]{1,0:T(8,128)(2,1)S(1)}, u32[]{:S(2)}) copy-start(bf16[256,2048]{1,0:T(8,128)(2,1)S(1)} %get-tuple-element.138.refs_0_) | copy-start | bytes 3145732
  12.8 27.3 %collective-permute-start = (bf16[256,2048]{1,0:T(8,128)(2,1)S(1)}, bf16[256,2048]{1,0:T(8,128)(2,1)S(1)}, u32[]{:S(2)}, u32[]{:S(2)}) collective-permute-start(bf16[256,2048]{1,0:T(8,128)(2,1)S(1)} %get-tuple-element.138.refs_0_), channel_id=1, source_target_pairs={{0,1},{1,2},{2,3},{4,5},{5,6},{6,7},{8,9},{9,10},{10,11},{12,13},{... | collective-permute-start | bytes 3145736 | tf_op jit(solution)/shard_map/ppermute | solution.py:688
  17.8 26.6 %collective-permute-start.1 = (bf16[256,2048]{1,0:T(8,128)(2,1)S(1)}, bf16[256,2048]{1,0:T(8,128)(2,1)}, u32[]{:S(2)}, u32[]{:S(2)}) collective-permute-start(bf16[256,2048]{1,0:T(8,128)(2,1)S(1)} %get-tuple-element.138.refs_0_), channel_id=1, source_target_pairs={{1,0},{2,1},{3,2},{5,4},{6,5},{7,6},{9,8},{10,9},{11,10},{13,12},{... | collective-permute-start | bytes 3145736 | tf_op jit(solution)/shard_map/ppermute | solution.py:689
  45.7 420.6 %reduce-scatter.3.cloned.1.call-start = ((), (), s32[]{:S(2)}) async-start(), calls=%async_computation.4 | async-start | bytes 10485760 | tf_op jit(solution)/shard_map/reduce_scatter | solution.py:861
  45.8 26.0 %collective-permute-start.5 = (bf16[256,2048]{1,0:T(8,128)(2,1)}, bf16[256,2048]{1,0:T(8,128)(2,1)}, u32[]{:S(2)}, u32[]{:S(2)}) collective-permute-start(bf16[256,2048]{1,0:T(8,128)(2,1)} %get-tuple-element.142.refs_1_), channel_id=1, source_target_pairs={{0,1},{1,2},{2,3},{4,5},{5,6},{6,7},{8,9},{9,10},{10,11},{12,13},{... | collective-permute-start | bytes 3145736 | tf_op jit(solution)/shard_map/ppermute | solution.py:688
  50.2 28.3 %collective-permute-start.4 = (bf16[256,2048]{1,0:T(8,128)(2,1)}, bf16[256,2048]{1,0:T(8,128)(2,1)}, u32[]{:S(2)}, u32[]{:S(2)}) collective-permute-start(bf16[256,2048]{1,0:T(8,128)(2,1)} %get-tuple-element.142.refs_1_), channel_id=1, source_target_pairs={{1,0},{2,1},{3,2},{5,4},{6,5},{7,6},{9,8},{10,9},{11,10},{13,12},{... | collective-permute-start | bytes 3145736 | tf_op jit(solution)/shard_map/ppermute | solution.py:689
  63.4 105.1 %copy-start.2 = (bf16[512,2048]{1,0:T(8,128)(2,1)}, bf16[512,2048]{1,0:T(8,128)(2,1)S(1)}, u32[]{:S(2)}) copy-start(bf16[512,2048]{1,0:T(8,128)(2,1)S(1)} %get-tuple-element.175.refs_0_.e_ref) | copy-start | bytes 6291460
  63.4 18.0 %collective-permute-start.2 = (bf16[256,2048]{1,0:T(8,128)(2,1)S(1)}, bf16[256,2048]{1,0:T(8,128)(2,1)S(1)}, u32[]{:S(2)}, u32[]{:S(2)}) collective-permute-start(bf16[256,2048]{1,0:T(8,128)(2,1)S(1)} %copy-done.33), channel_id=1, source_target_pairs={{1,2},{2,3},{5,6},{6,7},{9,10},{10,11},{13,14},{14,15},{17,18},{18... | collective-permute-start | bytes 3145736 | tf_op jit(solution)/shard_map/ppermute | solution.py:688
  64.1 36.9 %collective-permute-start.3 = (bf16[256,2048]{1,0:T(8,128)(2,1)}, bf16[256,2048]{1,0:T(8,128)(2,1)}, u32[]{:S(2)}, u32[]{:S(2)}) collective-permute-start(bf16[256,2048]{1,0:T(8,128)(2,1)} %collective-permute-done.1.refs_2_.refs_1_), channel_id=1, source_target_pairs={{1,0},{2,1},{5,4},{6,5},{9,8},{10,9},{13,12},{14,13},{17,16},{18,1... | collective-permute-start | bytes 3145736 | tf_op jit(solution)/shard_map/ppermute | solution.py:689
  78.5 58.2 %collective-permute-start.7 = (bf16[256,2048]{1,0:T(8,128)(2,1)}, bf16[256,2048]{1,0:T(8,128)(2,1)}, u32[]{:S(2)}, u32[]{:S(2)}) collective-permute-start(bf16[256,2048]{1,0:T(8,128)(2,1)} %collective-permute-done.5.refs_5_), channel_id=1, source_target_pairs={{1,2},{2,3},{5,6},{6,7},{9,10},{10,11},{13,14},{14,15},{17,18},{18... | collective-permute-start | bytes 3145736 | tf_op jit(solution)/shard_map/ppermute | solution.py:688
  80.1 56.6 %collective-permute-start.6 = (bf16[256,2048]{1,0:T(8,128)(2,1)}, bf16[256,2048]{1,0:T(8,128)(2,1)}, u32[]{:S(2)}, u32[]{:S(2)}) collective-permute-start(bf16[256,2048]{1,0:T(8,128)(2,1)} %collective-permute-done.4.refs_4_), channel_id=1, source_target_pairs={{1,0},{2,1},{5,4},{6,5},{9,8},{10,9},{13,12},{14,13},{17,16},{18,1... | collective-permute-start | bytes 3145736 | tf_op jit(solution)/shard_map/ppermute | solution.py:689
  81.4 55.2 %copy-start.6 = (bf16[256,2048]{1,0:T(8,128)(2,1)}, bf16[256,2048]{1,0:T(8,128)(2,1)S(1)}, u32[]{:S(2)}) copy-start(bf16[256,2048]{1,0:T(8,128)(2,1)S(1)} %collective-permute-done.2.refs_2_) | copy-start | bytes 3145732
  101.0 59.7 %collective-permute-start.8 = (bf16[256,2048]{1,0:T(8,128)(2,1)S(1)}, bf16[256,2048]{1,0:T(8,128)(2,1)}, u32[]{:S(2)}, u32[]{:S(2)}) collective-permute-start(bf16[256,2048]{1,0:T(8,128)(2,1)S(1)} %collective-permute-done.2.refs_2_), channel_id=1, source_target_pairs={{2,3},{6,7},{10,11},{14,15},{18,19},{22,23},{26,27},{30,31}} | collective-permute-start | bytes 3145736 | tf_op jit(solution)/shard_map/ppermute | solution.py:688
  102.6 58.0 %collective-permute-start.9 = (bf16[256,2048]{1,0:T(8,128)(2,1)}, bf16[256,2048]{1,0:T(8,128)(2,1)}, u32[]{:S(2)}, u32[]{:S(2)}) collective-permute-start(bf16[256,2048]{1,0:T(8,128)(2,1)} %collective-permute-done.3.refs_0_.refs_1_), channel_id=1, source_target_pairs={{1,0},{5,4},{9,8},{13,12},{17,16},{21,20},{25,24},{29,28}} | collective-permute-start | bytes 3145736 | tf_op jit(solution)/shard_map/ppermute | solution.py:689
  136.7 36.4 %collective-permute-start.10 = (bf16[256,2048]{1,0:T(8,128)(2,1)}, bf16[256,2048]{1,0:T(8,128)(2,1)}, u32[]{:S(2)}, u32[]{:S(2)}) collective-permute-start(bf16[256,2048]{1,0:T(8,128)(2,1)} %collective-permute-done.7.refs_5_.refs_6_), channel_id=1, source_target_pairs={{2,3},{6,7},{10,11},{14,15},{18,19},{22,23},{26,27},{30,31}} | collective-permute-start | bytes 3145736 | tf_op jit(solution)/shard_map/ppermute | solution.py:688
  138.4 34.7 %collective-permute-start.11 = (bf16[256,2048]{1,0:T(8,128)(2,1)}, bf16[256,2048]{1,0:T(8,128)(2,1)}, u32[]{:S(2)}, u32[]{:S(2)}) collective-permute-start(bf16[256,2048]{1,0:T(8,128)(2,1)} %collective-permute-done.6.refs_3_.refs_5_), channel_id=1, source_target_pairs={{1,0},{5,4},{9,8},{13,12},{17,16},{21,20},{25,24},{29,28}} | collective-permute-start | bytes 3145736 | tf_op jit(solution)/shard_map/ppermute | solution.py:689
  160.6 46.5 %collective-permute-start.13 = (bf16[512,2048]{1,0:T(8,128)(2,1)S(1)}, bf16[512,2048]{1,0:T(8,128)(2,1)}, u32[]{:S(2)}, u32[]{:S(2)}) collective-permute-start(bf16[512,2048]{1,0:T(8,128)(2,1)S(1)} %get-tuple-element.175.refs_0_.e_ref), channel_id=1, source_target_pairs={{0,1},{1,2},{2,3},{4,5},{5,6},{6,7},{8,9},{9,10},{10,11},{12,13},{... | collective-permute-start | bytes 6291464 | tf_op jit(solution)/shard_map/ppermute | solution.py:688
  168.5 45.6 %collective-permute-start.12 = (bf16[512,2048]{1,0:T(8,128)(2,1)S(1)}, bf16[512,2048]{1,0:T(8,128)(2,1)}, u32[]{:S(2)}, u32[]{:S(2)}) collective-permute-start(bf16[512,2048]{1,0:T(8,128)(2,1)S(1)} %get-tuple-element.175.refs_0_.e_ref), channel_id=1, source_target_pairs={{1,0},{2,1},{3,2},{5,4},{6,5},{7,6},{9,8},{10,9},{11,10},{13,12},{... | collective-permute-start | bytes 6291464 | tf_op jit(solution)/shard_map/ppermute | solution.py:689
  214.1 44.0 %collective-permute-start.14 = (bf16[512,2048]{1,0:T(8,128)(2,1)}, bf16[512,2048]{1,0:T(8,128)(2,1)S(1)}, u32[]{:S(2)}, u32[]{:S(2)}) collective-permute-start(bf16[512,2048]{1,0:T(8,128)(2,1)} %collective-permute-done.12.refs_1_), channel_id=1, source_target_pairs={{1,0},{2,1},{5,4},{6,5},{9,8},{10,9},{13,12},{14,13},{17,16},{18,1... | collective-permute-start | bytes 6291464 | tf_op jit(solution)/shard_map/ppermute | solution.py:689
  215.4 42.7 %collective-permute-start.15 = (bf16[512,2048]{1,0:T(8,128)(2,1)}, bf16[512,2048]{1,0:T(8,128)(2,1)}, u32[]{:S(2)}, u32[]{:S(2)}) collective-permute-start(bf16[512,2048]{1,0:T(8,128)(2,1)} %collective-permute-done.13.refs_2_), channel_id=1, source_target_pairs={{1,2},{2,3},{5,6},{6,7},{9,10},{10,11},{13,14},{14,15},{17,18},{18... | collective-permute-start | bytes 6291464 | tf_op jit(solution)/shard_map/ppermute | solution.py:688
  258.1 23.5 %copy-start.3 = (bf16[512,2048]{1,0:T(8,128)(2,1)}, bf16[512,2048]{1,0:T(8,128)(2,1)S(1)}, u32[]{:S(2)}) copy-start(bf16[512,2048]{1,0:T(8,128)(2,1)S(1)} %collective-permute-done.14.refs_0_.refs_1_) | copy-start | bytes 6291460
  258.1 52.8 %collective-permute-start.16 = (bf16[512,2048]{1,0:T(8,128)(2,1)}, bf16[512,2048]{1,0:T(8,128)(2,1)}, u32[]{:S(2)}, u32[]{:S(2)}) collective-permute-start(bf16[512,2048]{1,0:T(8,128)(2,1)} %collective-permute-done.15.refs_2_), channel_id=1, source_target_pairs={{2,3},{6,7},{10,11},{14,15},{18,19},{22,23},{26,27},{30,31}} | collective-permute-start | bytes 6291464 | tf_op jit(solution)/shard_map/ppermute | solution.py:688
  260.1 50.8 %collective-permute-start.17 = (bf16[512,2048]{1,0:T(8,128)(2,1)S(1)}, bf16[512,2048]{1,0:T(8,128)(2,1)}, u32[]{:S(2)}, u32[]{:S(2)}) collective-permute-start(bf16[512,2048]{1,0:T(8,128)(2,1)S(1)} %collective-permute-done.14.refs_0_.refs_1_), channel_id=1, source_target_pairs={{1,0},{5,4},{9,8},{13,12},{17,16},{21,20},{25,24},{29,28}} | collective-permute-start | bytes 6291464 | tf_op jit(solution)/shard_map/ppermute | solution.py:689
  310.9 313.2 %reduce-scatter.5.cloned.1.call-start = ((), (), s32[]{:S(2)}) async-start(), calls=%async_computation.5 | async-start | bytes 10485760 | tf_op jit(solution)/shard_map/reduce_scatter | solution.py:879
  338.6 16.3 %collective-permute-start.18 = (bf16[4,2560,256]{2,1,0:T(8,128)(2,1)}, bf16[4,2560,256]{2,1,0:T(8,128)(2,1)}, u32[]{:S(2)}, u32[]{:S(2)}) collective-permute-start(bf16[4,2560,256]{2,1,0:T(8,128)(2,1)} %weight_grad_part.3), channel_id=1, source_target_pairs={{0,4},{4,0},{1,5},{5,1},{2,6},{6,2},{3,7},{7,3},{8,12},{12,8},{9,1... | collective-permute-start | bytes 15728648 | tf_op jit(solution)/shard_map/ppermute | solution.py:872
  376.1 47.0 %collective-permute-start.19 = (bf16[2,1280,256]{2,1,0:T(8,128)(2,1)}, bf16[2,1280,256]{2,1,0:T(8,128)(2,1)S(1)}, u32[]{:S(2)}, u32[]{:S(2)}) collective-permute-start(bf16[2,1280,256]{2,1,0:T(8,128)(2,1)} %get-tuple-element.200), channel_id=1, source_target_pairs={{0,8},{8,0},{16,24},{24,16},{1,9},{9,1},{17,25},{25,17},{2,10},{10... | collective-permute-start | bytes 3932168 | tf_op jit(solution)/shard_map/ppermute | solution.py:581
  377.7 45.5 %collective-permute-start.20 = (bf16[2,1280,256]{2,1,0:T(8,128)(2,1)}, bf16[2,1280,256]{2,1,0:T(8,128)(2,1)S(1)}, u32[]{:S(2)}, u32[]{:S(2)}) collective-permute-start(bf16[2,1280,256]{2,1,0:T(8,128)(2,1)} %get-tuple-element.211), channel_id=1, source_target_pairs={{0,16},{8,24},{16,0},{24,8},{1,17},{9,25},{17,1},{25,9},{2,18},{10... | collective-permute-start | bytes 3932168 | tf_op jit(solution)/shard_map/ppermute | solution.py:581
  379.1 44.0 %copy-start.13 = (bf16[1,1280,256]{2,1,0:T(8,128)(2,1)S(1)}, bf16[1,1280,256]{2,1,0:T(8,128)(2,1)}, u32[]{:S(2)}) copy-start(bf16[1,1280,256]{2,1,0:T(8,128)(2,1)} %get-tuple-element.214) | copy-start | bytes 1966084
  424.2 42.1 %collective-permute-start.21 = (bf16[1,1280,256]{2,1,0:T(8,128)(2,1)}, bf16[1,1280,256]{2,1,0:T(8,128)(2,1)S(1)}, u32[]{:S(2)}, u32[]{:S(2)}) collective-permute-start(bf16[1,1280,256]{2,1,0:T(8,128)(2,1)} %add_convert_fusion.2), channel_id=1, source_target_pairs={{0,16},{8,24},{16,0},{24,8},{1,17},{9,25},{17,1},{25,9},{2,18},{10... | collective-permute-start | bytes 1966088 | tf_op jit(solution)/shard_map/ppermute | solution.py:581
  425.5 40.8 %collective-permute-start.22 = (bf16[1,1280,256]{2,1,0:T(8,128)(2,1)}, bf16[1,1280,256]{2,1,0:T(8,128)(2,1)}, u32[]{:S(2)}, u32[]{:S(2)}) collective-permute-start(bf16[1,1280,256]{2,1,0:T(8,128)(2,1)} %add_convert_fusion.1), channel_id=1, source_target_pairs={{0,8},{8,0},{16,24},{24,16},{1,9},{9,1},{17,25},{25,17},{2,10},{10... | collective-permute-start | bytes 1966088 | tf_op jit(solution)/shard_map/ppermute | solution.py:581
  426.0 58.0 %collective-permute-start.23 = (bf16[4,256,2048]{2,1,0:T(8,128)(2,1)}, bf16[4,256,2048]{2,1,0:T(8,128)(2,1)}, u32[]{:S(2)}, u32[]{:S(2)}) collective-permute-start(bf16[4,256,2048]{2,1,0:T(8,128)(2,1)} %weight_grad.5), channel_id=1, source_target_pairs={{0,4},{4,0},{1,5},{5,1},{2,6},{6,2},{3,7},{7,3},{8,12},{12,8},{9,1... | collective-permute-start | bytes 12582920 | tf_op jit(solution)/shard_map/ppermute | solution.py:865
  466.4 13.7 %copy-start.23 = (f32[2048]{0:T(1024)S(1)}, f32[2048]{0:T(1024)}, u32[]{:S(2)}) copy-start(f32[2048]{0:T(1024)} %get-tuple-element.259) | copy-start | bytes 24580
  478.5 25.8 %collective-permute-start.24 = (bf16[4,256,1536]{2,1,0:T(8,128)(2,1)}, bf16[4,256,1536]{2,1,0:T(8,128)(2,1)}, u32[]{:S(2)}, u32[]{:S(2)}) collective-permute-start(bf16[4,256,1536]{2,1,0:T(8,128)(2,1)} %weight_grad.7), channel_id=1, source_target_pairs={{0,4},{4,0},{1,5},{5,1},{2,6},{6,2},{3,7},{7,3},{8,12},{12,8},{9,1... | collective-permute-start | bytes 9437192 | tf_op jit(solution)/shard_map/ppermute | solution.py:865
  501.1 25.3 %collective-permute-start.29 = (bf16[2,128,2048]{2,1,0:T(8,128)(2,1)}, bf16[2,128,2048]{2,1,0:T(8,128)(2,1)S(1)}, u32[]{:S(2)}, u32[]{:S(2)}) collective-permute-start(bf16[2,128,2048]{2,1,0:T(8,128)(2,1)} %get-tuple-element.219), channel_id=1, source_target_pairs={{0,8},{8,0},{16,24},{24,16},{1,9},{9,1},{17,25},{25,17},{2,10},{10... | collective-permute-start | bytes 3145736 | tf_op jit(solution)/shard_map/ppermute | solution.py:581
  502.6 25.1 %collective-permute-start.30 = (bf16[2,128,2048]{2,1,0:T(8,128)(2,1)}, bf16[2,128,2048]{2,1,0:T(8,128)(2,1)}, u32[]{:S(2)}, u32[]{:S(2)}) collective-permute-start(bf16[2,128,2048]{2,1,0:T(8,128)(2,1)} %get-tuple-element.230), channel_id=1, source_target_pairs={{0,16},{8,24},{16,0},{24,8},{1,17},{9,25},{17,1},{25,9},{2,18},{10... | collective-permute-start | bytes 3145736 | tf_op jit(solution)/shard_map/ppermute | solution.py:581
  529.1 14.9 %collective-permute-start.32 = (bf16[1,128,2048]{2,1,0:T(8,128)(2,1)S(1)}, bf16[1,128,2048]{2,1,0:T(8,128)(2,1)S(1)}, u32[]{:S(2)}, u32[]{:S(2)}) collective-permute-start(bf16[1,128,2048]{2,1,0:T(8,128)(2,1)S(1)} %add_convert_fusion.3), channel_id=1, source_target_pairs={{0,8},{8,0},{16,24},{24,16},{1,9},{9,1},{17,25},{25,17},{2,10},{10... | collective-permute-start | bytes 1572872 | tf_op jit(solution)/shard_map/ppermute | solution.py:581
  530.8 14.9 %collective-permute-start.31 = (bf16[1,128,2048]{2,1,0:T(8,128)(2,1)S(1)}, bf16[1,128,2048]{2,1,0:T(8,128)(2,1)S(1)}, u32[]{:S(2)}, u32[]{:S(2)}) collective-permute-start(bf16[1,128,2048]{2,1,0:T(8,128)(2,1)S(1)} %add_convert_fusion.4), channel_id=1, source_target_pairs={{0,16},{8,24},{16,0},{24,8},{1,17},{9,25},{17,1},{25,9},{2,18},{10... | collective-permute-start | bytes 1572872 | tf_op jit(solution)/shard_map/ppermute | solution.py:581
  535.1 23.6 %collective-permute-start.25 = (bf16[2,128,1536]{2,1,0:T(8,128)(2,1)S(1)}, bf16[2,128,1536]{2,1,0:T(8,128)(2,1)S(1)}, u32[]{:S(2)}, u32[]{:S(2)}) collective-permute-start(bf16[2,128,1536]{2,1,0:T(8,128)(2,1)S(1)} %copy-done.35), channel_id=1, source_target_pairs={{0,8},{8,0},{16,24},{24,16},{1,9},{9,1},{17,25},{25,17},{2,10},{10... | collective-permute-start | bytes 2359304 | tf_op jit(solution)/shard_map/ppermute | solution.py:581
  536.8 23.5 %collective-permute-start.26 = (bf16[2,128,1536]{2,1,0:T(8,128)(2,1)S(1)}, bf16[2,128,1536]{2,1,0:T(8,128)(2,1)S(1)}, u32[]{:S(2)}, u32[]{:S(2)}) collective-permute-start(bf16[2,128,1536]{2,1,0:T(8,128)(2,1)S(1)} %copy-done.34), channel_id=1, source_target_pairs={{0,16},{8,24},{16,0},{24,8},{1,17},{9,25},{17,1},{25,9},{2,18},{10... | collective-permute-start | bytes 2359304 | tf_op jit(solution)/shard_map/ppermute | solution.py:581
  545.9 14.3 %copy-start.17 = (bf16[1,128,1536]{2,1,0:T(8,128)(2,1)S(1)}, bf16[1,128,1536]{2,1,0:T(8,128)(2,1)}, u32[]{:S(2)}) copy-start(bf16[1,128,1536]{2,1,0:T(8,128)(2,1)} %get-tuple-element.228) | copy-start | bytes 1179652
  546.0 15.9 %copy-start.16 = (bf16[1,128,1536]{2,1,0:T(8,128)(2,1)S(1)}, bf16[1,128,1536]{2,1,0:T(8,128)(2,1)}, u32[]{:S(2)}) copy-start(bf16[1,128,1536]{2,1,0:T(8,128)(2,1)} %get-tuple-element.225) | copy-start | bytes 1179652
  548.4 20.9 %copy-start.19 = (bf16[1,128,1536]{2,1,0:T(8,128)(2,1)S(1)}, bf16[1,128,1536]{2,1,0:T(8,128)(2,1)}, u32[]{:S(2)}) copy-start(bf16[1,128,1536]{2,1,0:T(8,128)(2,1)} %get-tuple-element.226) | copy-start | bytes 1179652
  560.3 8.9 %collective-permute-start.28 = (bf16[1,128,1536]{2,1,0:T(8,128)(2,1)S(1)}, bf16[1,128,1536]{2,1,0:T(8,128)(2,1)S(1)}, u32[]{:S(2)}, u32[]{:S(2)}) collective-permute-start(bf16[1,128,1536]{2,1,0:T(8,128)(2,1)S(1)} %add_convert_fusion.5), channel_id=1, source_target_pairs={{0,8},{8,0},{16,24},{24,16},{1,9},{9,1},{17,25},{25,17},{2,10},{10... | collective-permute-start | bytes 1179656 | tf_op jit(solution)/shard_map/ppermute | solution.py:581
  561.9 8.5 %collective-permute-start.27 = (bf16[1,128,1536]{2,1,0:T(8,128)(2,1)S(1)}, bf16[1,128,1536]{2,1,0:T(8,128)(2,1)S(1)}, u32[]{:S(2)}, u32[]{:S(2)}) collective-permute-start(bf16[1,128,1536]{2,1,0:T(8,128)(2,1)S(1)} %add_convert_fusion.6), channel_id=1, source_target_pairs={{0,16},{8,24},{16,0},{24,8},{1,17},{9,25},{17,1},{25,9},{2,18},{10... | collective-permute-start | bytes 1179656 | tf_op jit(solution)/shard_map/ppermute | solution.py:581
  570.6 22.0 %copy-start.1 = (bf16[512,2048]{1,0:T(8,128)(2,1)S(1)}, bf16[512,2048]{1,0:T(8,128)(2,1)}, u32[]{:S(2)}) copy-start(bf16[512,2048]{1,0:T(8,128)(2,1)} %x_ref.1) | copy-start | bytes 6291460
  574.8 1.3 collective-permute-start.33
  576.1 4.3 collective-permute-start.35
  577.8 5.5 collective-permute-start.36
  578.5 4.9 collective-permute-start.34
  584.7 13.8 %collective-permute-start.38 = (f32[97,128]{1,0:T(8,128)S(1)}, f32[97,128]{1,0:T(8,128)S(1)}, u32[]{:S(2)}, u32[]{:S(2)}) collective-permute-start(f32[97,128]{1,0:T(8,128)S(1)} %slice_add_fusion), channel_id=1, source_target_pairs={{0,2},{1,3},{2,0},{3,1},{4,6},{5,7},{6,4},{7,5},{8,10},{9,11},{10,... | collective-permute-start | bytes 149000 | tf_op jit(solution)/shard_map/ppermute | solution.py:714
  592.0 7.7 %collective-permute-start.39 = (f32[97,128]{1,0:T(8,128)S(1)}, f32[97,128]{1,0:T(8,128)S(1)}, u32[]{:S(2)}, u32[]{:S(2)}) collective-permute-start(f32[97,128]{1,0:T(8,128)S(1)} %slice_add_fusion), channel_id=1, source_target_pairs={{0,3},{1,2},{2,1},{3,0},{4,7},{5,6},{6,5},{7,4},{8,11},{9,10},{10,... | collective-permute-start | bytes 149000 | tf_op jit(solution)/shard_map/ppermute | solution.py:714
  592.0 9.5 %collective-permute-start.37 = (f32[97,128]{1,0:T(8,128)S(1)}, f32[97,128]{1,0:T(8,128)S(1)}, u32[]{:S(2)}, u32[]{:S(2)}) collective-permute-start(f32[97,128]{1,0:T(8,128)S(1)} %slice_add_fusion), channel_id=1, source_target_pairs={{0,1},{1,0},{2,3},{3,2},{4,5},{5,4},{6,7},{7,6},{8,9},{9,8},{10,11... | collective-permute-start | bytes 149000 | tf_op jit(solution)/shard_map/ppermute | solution.py:714
  604.2 18.0 %copy-start.25 = (f32[1536]{0:T(1024)S(1)}, f32[1536]{0:T(1024)}, u32[]{:S(2)}) copy-start(f32[1536]{0:T(1024)} %param.39) | copy-start | bytes 18436
  604.2 17.9 %copy-start.27 = (f32[1536]{0:T(1024)S(1)}, f32[1536]{0:T(1024)}, u32[]{:S(2)}) copy-start(f32[1536]{0:T(1024)} %param.46) | copy-start | bytes 18436
  604.2 17.9 %copy-start.28 = (f32[1536]{0:T(1024)S(1)}, f32[1536]{0:T(1024)}, u32[]{:S(2)}) copy-start(f32[1536]{0:T(1024)} %param.53) | copy-start | bytes 18436
  604.2 18.6 %copy-start.20 = (f32[2048]{0:T(1024)S(1)}, f32[2048]{0:T(1024)}, u32[]{:S(2)}) copy-start(f32[2048]{0:T(1024)} %param.40) | copy-start | bytes 24580
  604.2 18.6 %copy-start.29 = (f32[2048]{0:T(1024)S(1)}, f32[2048]{0:T(1024)}, u32[]{:S(2)}) copy-start(f32[2048]{0:T(1024)} %param.47) | copy-start | bytes 24580
  604.3 18.6 %copy-start.30 = (f32[2048]{0:T(1024)S(1)}, f32[2048]{0:T(1024)}, u32[]{:S(2)}) copy-start(f32[2048]{0:T(1024)} %param.54) | copy-start | bytes 24580
  604.3 19.2 %copy-start.21 = (f32[6,2048]{1,0:T(8,128)S(1)}, f32[6,2048]{1,0:T(8,128)}, u32[]{:S(2)}) copy-start(f32[6,2048]{1,0:T(8,128)} %param.45) | copy-start | bytes 147460
  604.3 19.2 %copy-start.22 = (f32[6,2048]{1,0:T(8,128)S(1)}, f32[6,2048]{1,0:T(8,128)}, u32[]{:S(2)}) copy-start(f32[6,2048]{1,0:T(8,128)} %param.52) | copy-start | bytes 147460
  (18 other events, 127.7 us)
Sparse Core Ops, SparseCore 0:
  10.9 83.7 all-gather.2
  97.1 65.1 all-gather.4
  311.0 148.6 reduce-scatter.2
  466.4 152.8 reduce-scatter.4
